TPU v7x, 128 devices: a whole 4x4x4 slice. The times are simulated.
128 devices in a mesh: dp: 16 (over z, y), row: 2 (over x_lo), col: 4 (over x_hi, core).
Axes of the slice: x: 4 (x_hi: 2, x_lo: 2; x = x_hi * 2 + x_lo), y: 4, z: 4, core: 2. Of those that a mesh axis runs over, the one named last changes fastest.
Arguments:
- layer_input: bfloat16 [16384, 1536], P(('dp', 'row'), 'col'), may hold values from -6 to 6
- gain_attn: bfloat16 [1536], P('col'), may hold values from 0.099609375 to 1.8984375
- w_query: bfloat16 [1536, 1536], P('col', 'row'), may hold values from -0.15625 to 0.15625
- w_key: bfloat16 [1536, 256], P('col', 'row'), may hold values from -0.15625 to 0.15625
- w_value: bfloat16 [1536, 256], P('col', 'row'), may hold values from -0.15625 to 0.15625
- b_query: bfloat16 [1536], P('row'), may hold values from -3 to 3
- b_key: bfloat16 [256], P('row'), may hold values from -3 to 3
- b_value: bfloat16 [256], P('row'), may hold values from -0.3125 to 0.3125
- w_out: bfloat16 [1536, 1536], P('row', 'col'), may hold values from -1.25 to 1.25
- gain_ffn: bfloat16 [1536], P('col'), may hold values from 0.099609375 to 1.8984375
- w_gate: bfloat16 [1536, 8960], P('col', 'row'), may hold values from -0.15625 to 0.15625
- w_up: bfloat16 [1536, 8960], P('col', 'row'), may hold values from -0.15625 to 0.15625
- w_down: bfloat16 [8960, 1536], P('row', 'col'), may hold values from -0.0625 to 0.0625
- out_grad: bfloat16 [16384, 1536], P(('dp', 'row'), 'col'), may hold values from -6 to 6
Outputs:
- layer_output: float32 [16384, 1536], P(('dp', 'row'), 'col')
- grad_input: float32 [16384, 1536], P(('dp', 'row'), 'col')
- grad_gain_attn: float32 [1536], P('col')
- grad_w_query: float32 [1536, 1536], P('col', 'row')
- grad_w_key: float32 [1536, 256], P('col', 'row')
- grad_w_value: float32 [1536, 256], P('col', 'row')
- grad_b_query: float32 [1536], P('row')
- grad_b_key: float32 [256], P('row')
- grad_b_value: float32 [256], P('row')
- grad_w_out: float32 [1536, 1536], P('row', 'col')
- grad_gain_ffn: float32 [1536], P('col')
- grad_w_gate: float32 [1536, 8960], P('col', 'row')
- grad_w_up: float32 [1536, 8960], P('col', 'row')
- grad_w_down: float32 [8960, 1536], P('row', 'col')
All inputs are finite; a program needn't handle non-finite values.
Results may differ from a plain program's by a relative error of at most 0.023.
Values may be sent and summed in bfloat16 or wider, within the bound.
A program may use at most 256 MiB of HBM per device.

v0:
```python
import jax
import jax.numpy as jnp
from jax import lax
from jax.sharding import PartitionSpec as P

EPS = 1e-06
THETA = 1000000.0
NEG = -1e30


def contract(left, right, right_dim):
    return lax.dot_general(
        left, right, (((1,), (right_dim,)), ((), ())), preferred_element_type=jnp.float32
    )


def outer_sum(left, right):
    return lax.dot_general(
        left, right, (((0,), (0,)), ((), ())), preferred_element_type=jnp.float32
    )


def col_total(values):
    return lax.psum(values, "col")


def normalize(values, gain):
    width = values.shape[1] * lax.axis_size("col")
    scale = lax.rsqrt(col_total(jnp.sum(values * values, axis=1)) / width + EPS)
    unit = values * scale[:, None]
    return (scale, unit, (unit * gain).astype(jnp.bfloat16))


def norm_back(d_normed, gain, scale, unit):
    width = unit.shape[1] * lax.axis_size("col")
    bent = d_normed * gain
    mean_term = col_total(jnp.sum(bent * unit, axis=1)) / width
    return (scale[:, None] * (bent - unit * mean_term[:, None]), jnp.sum(d_normed * unit, axis=0))


def row_to_col(acts, weight, weight_dim):
    whole = lax.all_gather(acts, "row", axis=0, tiled=True)
    return (
        whole,
        lax.psum_scatter(
            contract(whole, weight, weight_dim), "col", scatter_dimension=0, tiled=True
        ),
    )


def col_to_row(acts, weight, weight_dim):
    whole = lax.all_gather(acts, "col", axis=0, tiled=True)
    return (
        whole,
        lax.psum_scatter(
            contract(whole, weight, weight_dim), "row", scatter_dimension=0, tiled=True
        ),
    )


def rope_tables(start, count, width):
    places = (start + jnp.arange(count, dtype=jnp.int32)).astype(jnp.float32)
    inverse = 1.0 / THETA ** (jnp.arange(0, width, 2).astype(jnp.float32) / width)
    angles = places[:, None] * inverse[None, :]
    cosine = jnp.concatenate([jnp.cos(angles), jnp.cos(angles)], axis=-1)
    sine = jnp.concatenate([jnp.sin(angles), jnp.sin(angles)], axis=-1)
    return (cosine, sine)


def rotate(values, cosine, sine):
    half = values.shape[-1] // 2
    turned = jnp.concatenate([-values[..., half:], values[..., :half]], axis=-1)
    return values * cosine + turned * sine


def unrotate(grads, cosine, sine):
    half = grads.shape[-1] // 2
    weighted = grads * sine
    return grads * cosine + jnp.concatenate([weighted[..., half:], -weighted[..., :half]], axis=-1)


def masked(scores, qstart, rows, cols):
    keep = (
        jnp.arange(cols, dtype=jnp.int32)[None, :]
        <= (qstart + jnp.arange(rows, dtype=jnp.int32))[:, None]
    )
    return jnp.where(keep[None], scores, NEG)


def body(
    layer_input,
    gain_attn,
    w_query,
    w_key,
    w_value,
    b_query,
    b_key,
    b_value,
    w_out,
    gain_ffn,
    w_gate,
    w_up,
    w_down,
    out_grad,
):
    inputs = layer_input.astype(jnp.float32)
    gain1 = gain_attn.astype(jnp.float32)
    gain2 = gain_ffn.astype(jnp.float32)
    scale1, unit1, normed1 = normalize(inputs, gain1)
    w_qkv = jnp.concatenate([w_query, w_key, w_value], axis=1)
    normed1_all, qkv = row_to_col(normed1, w_qkv, 0)
    qkv = qkv + jnp.concatenate([b_query, b_key, b_value]).astype(jnp.float32)
    width = w_key.shape[1]
    heads = w_query.shape[1] // width
    query_cols = heads * width
    span = qkv.shape[0]
    start = lax.axis_index("col") * span
    cosine, sine = rope_tables(start, span, width)
    query = rotate(
        qkv[:, :query_cols].reshape(span, heads, width), cosine[:, None, :], sine[:, None, :]
    ).astype(jnp.bfloat16)
    key = rotate(qkv[:, query_cols : query_cols + width], cosine, sine).astype(jnp.bfloat16)
    value = qkv[:, query_cols + width :].astype(jnp.bfloat16)
    keys, values = (
        lax.all_gather(key, "col", axis=0, tiled=True),
        lax.all_gather(value, "col", axis=0, tiled=True),
    )
    scaling = width ** (-0.5)
    block = min(span, 512)
    count_blocks = span // block
    starts = start + block * jnp.arange(count_blocks, dtype=jnp.int32)
    query_blocks = query.reshape(count_blocks, block, heads, width)

    def attend_block(item):
        qblk, qstart = item
        raw = jnp.einsum("thd,sd->hts", qblk, keys, preferred_element_type=jnp.float32)
        scores = masked(raw * scaling, qstart, block, keys.shape[0])
        top = jnp.max(scores, axis=-1)
        lse = top + jnp.log(jnp.sum(jnp.exp(scores - top[..., None]), axis=-1))
        probs = jnp.exp(scores - lse[..., None]).astype(jnp.bfloat16)
        return (jnp.einsum("hts,sd->thd", probs, values, preferred_element_type=jnp.float32), lse)

    attn, lse_all = lax.map(attend_block, (query_blocks, starts))
    attn = attn.reshape(span, query_cols).astype(jnp.bfloat16)
    attn_all, attn_proj = col_to_row(attn, w_out, 0)
    mid = inputs + attn_proj
    scale2, unit2, normed2 = normalize(mid, gain2)
    w_both = jnp.concatenate([w_gate, w_up], axis=1)
    normed2_all, both = row_to_col(normed2, w_both, 0)
    units = w_gate.shape[1]
    gate = both[:, :units]
    up = both[:, units:]
    sig = jax.nn.sigmoid(gate)
    act = gate * sig
    hidden = (act * up).astype(jnp.bfloat16)
    hidden_all, ffn_proj = col_to_row(hidden, w_down, 0)
    layer_output = mid + ffn_proj
    grad_all, d_hidden = row_to_col(out_grad, w_down, 1)
    grad_w_down = outer_sum(hidden_all, grad_all)
    d_gate = d_hidden * up * sig * (1.0 + gate * (1.0 - sig))
    d_up = d_hidden * act
    d_both = jnp.concatenate([d_gate, d_up], axis=1).astype(jnp.bfloat16)
    d_both_all, d_normed2 = col_to_row(d_both, w_both, 1)
    grad_both = outer_sum(normed2_all, d_both_all)
    d_mid_norm, grad_gain_ffn = norm_back(d_normed2, gain2, scale2, unit2)
    d_mid = out_grad.astype(jnp.float32) + d_mid_norm
    d_mid_low = d_mid.astype(jnp.bfloat16)
    d_mid_all, d_attn = row_to_col(d_mid_low, w_out, 1)
    grad_w_out = outer_sum(attn_all, d_mid_all)
    d_blocks = d_attn.astype(jnp.bfloat16).reshape(count_blocks, block, heads, width)

    def back_block(carry, item):
        qblk, dblk, lse, qstart = item
        raw = jnp.einsum("thd,sd->hts", qblk, keys, preferred_element_type=jnp.float32)
        scores = masked(raw * scaling, qstart, block, keys.shape[0])
        probs = jnp.exp(scores - lse[..., None])
        d_probs = jnp.einsum("thd,sd->hts", dblk, values, preferred_element_type=jnp.float32)
        inner = jnp.sum(probs * d_probs, axis=-1)
        d_scores = (probs * (d_probs - inner[..., None]) * scaling).astype(jnp.bfloat16)
        d_qblk = jnp.einsum("hts,sd->thd", d_scores, keys, preferred_element_type=jnp.float32)
        key_acc = carry[0] + jnp.einsum(
            "hts,thd->sd", d_scores, qblk, preferred_element_type=jnp.float32
        )
        value_acc = carry[1] + jnp.einsum(
            "hts,thd->sd", probs.astype(jnp.bfloat16), dblk, preferred_element_type=jnp.float32
        )
        return ((key_acc, value_acc), d_qblk)

    empty = jnp.zeros(keys.shape, jnp.float32)
    partials, d_query = lax.scan(
        back_block, (empty, empty), (query_blocks, d_blocks, lse_all, starts)
    )
    d_key, d_value = (
        lax.psum_scatter(partials[0], "col", scatter_dimension=0, tiled=True),
        lax.psum_scatter(partials[1], "col", scatter_dimension=0, tiled=True),
    )
    d_query = unrotate(
        d_query.reshape(span, heads, width), cosine[:, None, :], sine[:, None, :]
    ).reshape(span, query_cols)
    d_key = unrotate(d_key, cosine, sine)
    d_qkv = jnp.concatenate([d_query, d_key, d_value], axis=1).astype(jnp.bfloat16)
    d_qkv_all, d_normed1 = col_to_row(d_qkv, w_qkv, 1)
    grad_qkv = outer_sum(normed1_all, d_qkv_all)
    grad_bias = jnp.dot(
        jnp.ones((1, d_qkv_all.shape[0]), jnp.bfloat16),
        d_qkv_all,
        preferred_element_type=jnp.float32,
    )[0]
    d_in_norm, grad_gain_attn = norm_back(d_normed1, gain1, scale1, unit1)
    grad_input = d_mid + d_in_norm
    grad_gain_attn, grad_gain_ffn = lax.psum((grad_gain_attn, grad_gain_ffn), ("dp", "row"))
    grad_qkv, grad_bias, grad_w_out, grad_both, grad_w_down = lax.psum(
        (grad_qkv, grad_bias, grad_w_out, grad_both, grad_w_down), "dp"
    )
    grad_w_query = grad_qkv[:, :query_cols]
    grad_w_key = grad_qkv[:, query_cols : query_cols + width]
    grad_w_value = grad_qkv[:, query_cols + width :]
    grad_b_query = grad_bias[:query_cols]
    grad_b_key = grad_bias[query_cols : query_cols + width]
    grad_b_value = grad_bias[query_cols + width :]
    grad_w_gate = grad_both[:, :units]
    grad_w_up = grad_both[:, units:]
    return (
        layer_output,
        grad_input,
        grad_gain_attn,
        grad_w_query,
        grad_w_key,
        grad_w_value,
        grad_b_query,
        grad_b_key,
        grad_b_value,
        grad_w_out,
        grad_gain_ffn,
        grad_w_gate,
        grad_w_up,
        grad_w_down,
    )


def solution(mesh):
    in_specs = (
        P(("dp", "row"), "col"),
        P("col"),
        P("col", "row"),
        P("col", "row"),
        P("col", "row"),
        P("row"),
        P("row"),
        P("row"),
        P("row", "col"),
        P("col"),
        P("col", "row"),
        P("col", "row"),
        P("row", "col"),
        P(("dp", "row"), "col"),
    )
    out_specs = (
        P(("dp", "row"), "col"),
        P(("dp", "row"), "col"),
        P("col"),
        P("col", "row"),
        P("col", "row"),
        P("col", "row"),
        P("row"),
        P("row"),
        P("row"),
        P("row", "col"),
        P("col"),
        P("col", "row"),
        P("col", "row"),
        P("row", "col"),
    )
    return jax.shard_map(body, mesh=mesh, in_specs=in_specs, out_specs=out_specs, check_vma=False)
```

profile of v0, /device:TPU:0, one launch (start us, length us, event | category | flops | bytes accessed | tf_op | source)
XLA Modules:
  0.0 1409.7 jit_solution(1290987713356429301)
XLA Ops:
  8.5 10.0 psum.77
  20.4 8.7 all_gather.30
  38.9 51.8 %reduce-scatter.11.cloned.1.call-done = f32[256,1024]{1,0:T(8,128)} async-done(((f32[1024,1024]{1,0:T(8,128)}), f32[256,1024]{1,0:T(8,128)}) %reduce-scatter.11.cloned.1.call-update) | async-done | bytes 1048592 | tf_op jit(solution)/shard_map/reduce_scatter | solution.py:45
  101.9 7.5 all_gather.32
  115.0 7.4 all_gather.31
  125.0 23.4 %all-gather.5.cloned.1.call-done = bf16[1024,768]{0,1:T(8,128)(2,1)} async-done(((bf16[256,768]{0,1:T(8,128)(2,1)}), bf16[1024,768]{0,1:T(8,128)(2,1)}) %all-gather.5.cloned.1.call-update) | async-done | bytes 1572880 | tf_op jit(solution)/shard_map/all_gather | solution.py:52
  152.2 14.8 %all_gather.36 = bf16[1024,384]{1,0:T(8,128)(2,1)S(1)} all-gather(bf16[512,384]{1,0:T(8,128)(2,1)} %param.27), channel_id=1, replica_groups=mesh['dp'=16,'row'=2,'col'=4] {'row'}, dimensions={0}, use_global_device_ids=true | all-gather | bytes 1179648 | tf_op jit(solution)/shard_map/all_gather | solution.py:42
  167.9 8.9 fusion.58
  194.4 11.5 all_gather.34
  206.8 20.2 %fusion.56 = f32[1024,8960]{1,0:T(8,128)} fusion(bf16[1024,384]{1,0:T(8,128)(2,1)S(1)} %all_gather.34, bf16[384,8960]{1,0:T(8,128)(2,1)} %constant_dynamic-update-slice_fusion.3), kind=kOutput, calls=%fused_computation.103 | convolution fusion | flops 7046430720 | bytes 44367872 | tf_op jit(solution)/shard_map/dot_general | solution.py:12
  227.1 100.4 %reduce-scatter.19.cloned.1.call-done = f32[256,4480]{1,0:T(8,128)} async-done(((f32[1024,4480]{1,0:T(8,128)}), f32[256,4480]{1,0:T(8,128)}) %reduce-scatter.19.cloned.1.call-update) | async-done | bytes 4587536 | tf_op jit(solution)/shard_map/reduce_scatter | solution.py:45
  327.5 263.9 %reduce-scatter.15.cloned.1.call-done = f32[256,8960]{1,0:T(8,128)} async-done(((f32[1024,8960]{1,0:T(8,128)}), f32[256,8960]{1,0:T(8,128)}) %reduce-scatter.15.cloned.1.call-update) | async-done | bytes 9175056 | tf_op jit(solution)/shard_map/reduce_scatter | solution.py:45
  591.4 7.3 multiply_convert_fusion.1
  601.2 120.7 %all-gather.9.cloned.1.call-done = bf16[1024,8960]{1,0:T(8,128)(2,1)} async-done(((bf16[256,8960]{1,0:T(8,128)(2,1)}), bf16[1024,8960]{1,0:T(8,128)(2,1)}) %all-gather.9.cloned.1.call-update) | async-done | bytes 18350096 | tf_op jit(solution)/shard_map/all_gather | solution.py:52
  721.9 16.3 %fusion.59 = f32[1024,384]{1,0:T(8,128)} fusion(bf16[1024,8960]{1,0:T(8,128)(2,1)} %all-gather.9.cloned.1.call-done, bf16[384,8960]{1,0:T(8,128)(2,1)} %constant_dynamic-update-slice_fusion.3), kind=kOutput, calls=%fused_computation.106 | convolution fusion | flops 7046430720 | bytes 26804224 | tf_op jit(solution)/shard_map/dot_general | solution.py:12
  738.2 28.1 %reduce-scatter.21.cloned.1.call-done = f32[512,384]{1,0:T(8,128)} async-done(((f32[1024,384]{1,0:T(8,128)}), f32[512,384]{1,0:T(8,128)}) %reduce-scatter.21.cloned.1.call-update) | async-done | bytes 786448 | tf_op jit(solution)/shard_map/reduce_scatter | solution.py:55
  768.0 9.6 psum.79
  779.4 9.1 all_gather.38
  793.7 45.5 %reduce-scatter.23.cloned.1.call-done = f32[256,768]{1,0:T(8,128)} async-done(((f32[1024,768]{1,0:T(8,128)}), f32[256,768]{1,0:T(8,128)}) %reduce-scatter.23.cloned.1.call-update) | async-done | bytes 786448 | tf_op jit(solution)/shard_map/reduce_scatter | solution.py:45
  847.8 13.5 convolution_bitcast_fusion.2
  861.3 14.0 broadcast_multiply_fusion
  893.4 27.3 %reduce-scatter.27.cloned.1.call-done = f32[256,128]{1,0:T(8,128)} async-done(((f32[1024,128]{1,0:T(8,128)}), f32[256,128]{1,0:T(8,128)}) %reduce-scatter.27.cloned.1.call-update) | async-done | bytes 131088 | tf_op jit(solution)/shard_map/reduce_scatter | solution.py:195
  926.3 25.8 %all-gather.11.cloned.1.call-done = bf16[1024,1024]{0,1:T(8,128)(2,1)} async-done(((bf16[256,1024]{0,1:T(8,128)(2,1)}), bf16[1024,1024]{0,1:T(8,128)(2,1)}) %all-gather.11.cloned.1.call-update) | async-done | bytes 2097168 | tf_op jit(solution)/shard_map/all_gather | solution.py:52
  956.4 63.5 %all-gather.7.cloned.1.call-done = bf16[1024,4480]{1,0:T(8,128)(2,1)} async-done(((bf16[256,4480]{1,0:T(8,128)(2,1)}), bf16[1024,4480]{1,0:T(8,128)(2,1)}) %all-gather.7.cloned.1.call-update) | async-done | bytes 9175056 | tf_op jit(solution)/shard_map/all_gather | solution.py:52
  1019.9 8.7 fusion.57
  1028.8 12.2 fusion.65
  1041.0 17.1 %fusion.64 = f32[384,8960]{1,0:T(8,128)} fusion(bf16[1024,384]{1,0:T(8,128)(2,1)S(1)} %copy-done.3, bf16[1024,8960]{1,0:T(8,128)(2,1)} %all-gather.9.cloned.1.call-done), kind=kOutput, calls=%fused_computation.111 | convolution fusion | flops 7046430720 | bytes 32899072 | tf_op jit(solution)/shard_map/dot_general | solution.py:18
  1065.0 40.8 %psum.83 = f32[1024]{0:T(1024)S(1)} all-reduce(f32[1024]{0:T(1024)S(1)} %bitcast.118), channel_id=1, replica_groups=mesh['dp'=16,'row'=2,'col'=4] {'dp'}, use_global_device_ids=true, to_apply=%region_24.25 | all-reduce | flops 1024 | bytes 8192 | tf_op jit(solution)/shard_map/psum | solution.py:212
  1107.8 79.1 %all-reduce = (f32[384]{0:T(512)}, f32[384]{0:T(512)}) all-reduce(f32[384]{0:T(512)S(1)} %get-tuple-element.57, f32[384]{0:T(512)S(1)} %get-tuple-element.55), channel_id=1, replica_groups=mesh['dp'=16,'row'=2,'col'=4] {'dp','row'}, use_global_device_ids=true, to_apply=%region_22.23 | all-reduce | flops 768 | bytes 6144 | tf_op jit(solution)/shard_map/psum | solution.py:211
  1187.0 7.5 psum.80
  1198.3 180.9 %all-reduce.4.cloned.1.call-done = (f32[384,1024]{1,0:T(8,128)}, f32[768,384]{1,0:T(8,128)}, f32[384,8960]{1,0:T(8,128)}, f32[4480,384]{1,0:T(8,128)}) async-done(((f32[384,1024]{1,0:T(8,128)}, f32[768,384]{1,0:T(8,128)}, f32[384,8960]{1,0:T(8,128)}, f32[4480,384]{1,0:T(8,128)}), (f32[384,1024]{1,0:T(8,128)}, f32[768,384]{1,0:T(8,128)}, f32[384,8960]{1,0:T(8,128)}, ...) | async-done | bytes 23396368 | tf_op jit(solution)/shard_map/psum | solution.py:212
  1383.4 11.0 fusion.49
  (144 shorter events, 128.7 us)
Async XLA Ops:
  7.2 160.7 %copy-start = (bf16[4480,384]{1,0:T(8,128)(2,1)S(1)}, bf16[4480,384]{1,0:T(8,128)(2,1)}, u32[]{:S(2)}) copy-start(bf16[4480,384]{1,0:T(8,128)(2,1)} %param.26) | copy-start | bytes 10321924
  7.2 83.5 %reduce-scatter.11.cloned.1.call-start = ((), (), s32[]{:S(2)}) async-start(), calls=%async_computation.10 | async-start | bytes 5242880 | tf_op jit(solution)/shard_map/reduce_scatter | solution.py:45
  29.1 3.3 copy-start.4
  31.5 5.2 copy-start.17
  31.5 5.2 copy-start.19
  31.5 5.2 copy-start.20
  36.6 111.8 %all-gather.5.cloned.1.call-start = ((), (), s32[]{:S(2)}) async-start(), calls=%async_computation.11 | async-start | bytes 1966080 | tf_op jit(solution)/shard_map/all_gather | solution.py:52
  100.7 13.0 copy-start.11
  109.5 4.2 copy-start.14
  113.7 11.2 copy-start.1
  122.4 2.5 copy-start.15
  124.9 58.7 %reduce-scatter.13.cloned.1.call-start = ((), (), s32[]{:S(2)}) async-start(), calls=%async_computation.12 | async-start | bytes 2359296 | tf_op jit(solution)/shard_map/reduce_scatter | solution.py:55
  152.1 175.3 %reduce-scatter.19.cloned.1.call-start = ((), (), s32[]{:S(2)}) async-start(), calls=%async_computation.16 | async-start | bytes 22937600 | tf_op jit(solution)/shard_map/reduce_scatter | solution.py:45
  176.9 414.5 %reduce-scatter.15.cloned.1.call-start = ((), (), s32[]{:S(2)}) async-start(), calls=%async_computation.13 | async-start | bytes 45875200 | tf_op jit(solution)/shard_map/reduce_scatter | solution.py:45
  177.5 4.2 copy-start.7
  205.9 0.9 copy-start.2
  227.0 494.9 %all-gather.9.cloned.1.call-start = ((), (), s32[]{:S(2)}) async-start(), calls=%async_computation.17 | async-start | bytes 22937600 | tf_op jit(solution)/shard_map/all_gather | solution.py:52
  601.1 165.2 %reduce-scatter.21.cloned.1.call-start = ((), (), s32[]{:S(2)}) async-start(), calls=%async_computation.18 | async-start | bytes 2359296 | tf_op jit(solution)/shard_map/reduce_scatter | solution.py:55
  738.2 101.0 %reduce-scatter.23.cloned.1.call-start = ((), (), s32[]{:S(2)}) async-start(), calls=%async_computation.19 | async-start | bytes 3932160 | tf_op jit(solution)/shard_map/reduce_scatter | solution.py:45
  793.2 96.2 %reduce-scatter.25.cloned.1.call-start = ((), (), s32[]{:S(2)}) async-start(), calls=%async_computation.20 | async-start | bytes 655360 | tf_op jit(solution)/shard_map/reduce_scatter | solution.py:194
  861.2 59.4 %reduce-scatter.27.cloned.1.call-start = ((), (), s32[]{:S(2)}) async-start(), calls=%async_computation.21 | async-start | bytes 655360 | tf_op jit(solution)/shard_map/reduce_scatter | solution.py:195
  880.5 71.6 %all-gather.11.cloned.1.call-start = ((), (), s32[]{:S(2)}) async-start(), calls=%async_computation.22 | async-start | bytes 2621440 | tf_op jit(solution)/shard_map/all_gather | solution.py:52
  925.6 94.2 %all-gather.7.cloned.1.call-start = ((), (), s32[]{:S(2)}) async-start(), calls=%async_computation.14 | async-start | bytes 11468800 | tf_op jit(solution)/shard_map/all_gather | solution.py:52
  926.2 180.0 %reduce-scatter.29.cloned.1.call-start = ((), (), s32[]{:S(2)}) async-start(), calls=%async_computation.23 | async-start | bytes 2359296 | tf_op jit(solution)/shard_map/reduce_scatter | solution.py:55
  956.3 238.2 %reduce-scatter.17.cloned.1.call-start = ((), (), s32[]{:S(2)}) async-start(), calls=%async_computation.15 | async-start | bytes 2359296 | tf_op jit(solution)/shard_map/reduce_scatter | solution.py:55
  1028.6 350.6 %all-reduce.4.cloned.1.call-start = ((), (), s32[]{:S(2)}) async-start(), calls=%async_computation.24 | async-start | bytes 46792704 | tf_op jit(solution)/shard_map/psum | solution.py:212
  1028.8 12.2 copy-start.3
  1041.0 17.1 %copy-start.9 = (bf16[1024,384]{1,0:T(8,128)(2,1)S(1)}, bf16[1024,384]{1,0:T(8,128)(2,1)}, u32[]{:S(2)}) copy-start(bf16[1024,384]{1,0:T(8,128)(2,1)} %copy-done.8) | copy-start | bytes 2359300
  1041.0 17.1 %copy-start.21 = (bf16[1024,768]{0,1:T(8,128)(2,1)S(1)}, bf16[1024,768]{0,1:T(8,128)(2,1)}, u32[]{:S(2)}) copy-start(bf16[1024,768]{0,1:T(8,128)(2,1)} %all-gather.5.cloned.1.call-done) | copy-start | bytes 4718596
  1058.1 2.0 copy-start.5
  1058.1 2.0 copy-start.12
  1105.7 288.6 %copy-start.16 = (f32[1024]{0:T(1024)}, f32[1024]{0:T(1024)S(1)}, u32[]{:S(2)}) copy-start(f32[1024]{0:T(1024)S(1)} %psum.83) | copy-start | bytes 12292
  (5 other events, 4.1 us)
Sparse Core Ops, SparseCore 0:
  36.7 53.9 reduce-scatter.10
  125.1 23.3 all-gather.4
  152.3 30.1 reduce-scatter.12
  185.0 142.3 reduce-scatter.18
  330.3 261.0 reduce-scatter.14
  601.3 120.6 all-gather.8
  738.3 28.0 reduce-scatter.20
  793.3 45.8 reduce-scatter.22
  861.4 27.9 reduce-scatter.24
  892.6 27.9 reduce-scatter.26
  925.8 26.2 all-gather.10
  953.6 66.2 all-gather.6
  1022.8 28.0 reduce-scatter.28
  1053.8 29.5 reduce-scatter.16
  1088.2 290.9 all-reduce.3
where the time goes:
time: 1420 us; the launch traced here: 1410 us
  waiting for transfers between devices  938 us (66%)
  blocking collectives  213 us (15%)
  matrix products  147 us (10%)
  local copies, waits for them, and re-layouts  49.4 us (3%)
  other arithmetic  46.4 us (3%)
  between operations  14.5 us (1%)
    reduce_scatter x4, waiting for transfers between devices, row_to_col(): lax.psum_scatter(contract(whole, weight, weight_dim), 'col', scatter_dime...  462 us
    all_gather x4, waiting for transfers between devices, col_to_row(): whole = lax.all_gather(acts, 'col', axis=0, tiled=True)  233 us
    psum x1, waiting for transfers between devices, body(): lax.psum((grad_qkv, grad_bias, grad_w_out, grad_both, grad_w_down), 'dp')  181 us
    psum x1, blocking collectives, body(): lax.psum((grad_gain_attn, grad_gain_ffn), ('dp', 'row'))  79.1 us
    dot_general x8, matrix products, contract(): lax.dot_general(left, right, (((1,), (right_dim,)), ((), ())), preferred_...  68.9 us
    all_gather x4, blocking collectives, row_to_col(): whole = lax.all_gather(acts, 'row', axis=0, tiled=True)  44.2 us
    psum x1, blocking collectives, body(): lax.psum((grad_qkv, grad_bias, grad_w_out, grad_both, grad_w_down), 'dp')  40.8 us
    psum x4, blocking collectives, col_total(): return lax.psum(values, 'col')  34.4 us
  transfers between devices with their start and end apart: 15, of which 12 were waited for; matrix products, arithmetic and copies ran while one was open for 9% of the time, Pallas kernels for 0%

commit v1 on v0

v1 whole, which is shorter than its diff:
```python
import jax
import jax.numpy as jnp
from jax import lax
from jax.sharding import PartitionSpec as P

EPS = 1e-06
THETA = 1000000.0
NEG = -1e30
BF = jnp.bfloat16
F32 = jnp.float32
HEAD = 128
LANES = 128


def dot(left, right, left_dim, right_dim):
    return lax.dot_general(
        left, right, (((left_dim,), (right_dim,)), ((), ())), preferred_element_type=F32
    )


def flip(values, bit):
    count = lax.axis_size("col")
    return lax.ppermute(values, "col", [(i, i ^ bit) for i in range(count)])


def by_source(blocks, me):
    stacked = jnp.stack(blocks)
    return jnp.take(stacked, me ^ jnp.arange(4), axis=0)


def rope_tables(count):
    places = jnp.arange(count, dtype=jnp.int32).astype(F32)
    inverse = 1.0 / THETA ** (jnp.arange(0, HEAD, 2).astype(F32) / HEAD)
    angles = places[:, None] * inverse[None, :]
    cosine = jnp.concatenate([jnp.cos(angles), jnp.cos(angles)], axis=-1)
    sine = jnp.concatenate([jnp.sin(angles), jnp.sin(angles)], axis=-1)
    return (cosine, sine)


def rotate(values, cosine, sine):
    half = values.shape[-1] // 2
    turned = jnp.concatenate([-values[..., half:], values[..., :half]], axis=-1)
    return values * cosine + turned * sine


def unrotate(grads, cosine, sine):
    half = grads.shape[-1] // 2
    weighted = grads * sine
    return grads * cosine + jnp.concatenate([weighted[..., half:], -weighted[..., :half]], axis=-1)


def gather_dp(block):
    n_dp = lax.axis_size("dp")
    rows = block.shape[0] // n_dp
    mine = lax.dynamic_slice_in_dim(block, lax.axis_index("dp") * rows, rows, 0)
    return lax.all_gather(flip(mine, 2), "dp", axis=0, tiled=True)


def body(
    layer_input,
    gain_attn,
    w_query,
    w_key,
    w_value,
    b_query,
    b_key,
    b_value,
    w_out,
    gain_ffn,
    w_gate,
    w_up,
    w_down,
    out_grad,
):
    n_dp = lax.axis_size("dp")
    dp, row, col = lax.axis_index("dp"), lax.axis_index("row"), lax.axis_index("col")
    half, feat = layer_input.shape
    seq, model = 2 * half, 4 * feat
    block = seq // 8
    units = w_gate.shape[1]
    part = -(-units // (4 * LANES)) * LANES
    padded = 4 * part
    query_cols = w_query.shape[1]
    heads = query_cols // HEAD

    w_qkv = jnp.concatenate([w_query, w_key, w_value], axis=1)
    gate_pad = jnp.pad(w_gate, ((0, 0), (0, padded - units)))
    up_pad = jnp.pad(w_up, ((0, 0), (0, padded - units)))
    down_pad = jnp.pad(w_down, ((0, padded - units), (0, 0)))
    mine_half, other_half = (col // 2) * 2 * part, (1 - col // 2) * 2 * part

    def cols_of(array, start, width):
        return lax.dynamic_slice_in_dim(array, start, width, 1)

    def rows_of(array, start, width):
        return lax.dynamic_slice_in_dim(array, start, width, 0)

    qkv_far = gather_dp(w_qkv)
    out_far = gather_dp(w_out)
    gate_far = gather_dp(cols_of(gate_pad, other_half, 2 * part))
    up_far = gather_dp(cols_of(up_pad, other_half, 2 * part))
    down_far = gather_dp(rows_of(down_pad, other_half, 2 * part))
    gate_own = cols_of(gate_pad, mine_half, 2 * part)
    up_own = cols_of(up_pad, mine_half, 2 * part)
    down_own = rows_of(down_pad, mine_half, 2 * part)
    mine, theirs = (col % 2) * part, (1 - col % 2) * part
    qkv_w = by_source([w_qkv, flip(w_qkv, 1), qkv_far, flip(qkv_far, 1)], col).reshape(model, -1)
    out_w = by_source([w_out, flip(w_out, 1), out_far, flip(out_far, 1)], col)
    out_w = out_w.transpose(1, 0, 2).reshape(-1, model)

    def quarter(own, far, pick):
        return by_source(
            [
                pick(own, mine, part),
                flip(pick(own, theirs, part), 1),
                pick(far, mine, part),
                flip(pick(far, theirs, part), 1),
            ],
            col,
        )

    gate_w = quarter(gate_own, gate_far, cols_of).reshape(model, part)
    up_w = quarter(up_own, up_far, cols_of).reshape(model, part)
    down_w = quarter(down_own, down_far, rows_of).transpose(1, 0, 2).reshape(part, model)

    def whole(array):
        stacked = lax.all_gather(array, ("row", "col"))
        return stacked.reshape(2, 4, half, feat).transpose(0, 2, 1, 3).reshape(seq, model)

    def mirror(array):
        return jnp.concatenate(
            [array[:half], array[half:].reshape(4, block, -1)[::-1].reshape(half, -1)]
        )

    inputs_all = whole(layer_input)
    grads_all = mirror(whole(out_grad))
    gain1 = lax.all_gather(gain_attn, "col", tiled=True).astype(F32)
    gain2 = lax.all_gather(gain_ffn, "col", tiled=True).astype(F32)
    low, high = col * block, (7 - col) * block
    shard = jnp.where(row == 0, low, high)

    def pair(array):
        return jnp.concatenate([rows_of(array, low, block), rows_of(array, high, block)])

    def normalize(values, gain):
        scale = lax.rsqrt(jnp.mean(values * values, axis=1, keepdims=True) + EPS)
        unit = values * scale
        return scale, unit, (unit * gain).astype(BF)

    def norm_back(d_normed, gain, scale, unit):
        bent = d_normed * gain
        mean_term = jnp.mean(bent * unit, axis=1, keepdims=True)
        return scale * (bent - unit * mean_term), jnp.sum(d_normed * unit, axis=0)

    _, _, normed1 = normalize(inputs_all.astype(F32), gain1)
    input_shard = rows_of(inputs_all, shard, block).astype(F32)
    scale1, unit1, _ = normalize(input_shard, gain1)

    cosine, sine = rope_tables(seq)
    cos_pair, sin_pair = pair(cosine), pair(sine)
    kv = dot(normed1, qkv_w[:, query_cols:], 1, 0)
    kv = kv + jnp.concatenate([b_key, b_value]).astype(F32)
    key = rotate(kv[:, :HEAD], cosine, sine).astype(BF)
    value = kv[:, HEAD:].astype(BF)
    queries = dot(pair(normed1), qkv_w[:, :query_cols], 1, 0) + b_query.astype(F32)
    queries = rotate(
        queries.reshape(2 * block, heads, HEAD), cos_pair[:, None, :], sin_pair[:, None, :]
    ).astype(BF)
    places = jnp.concatenate([low + jnp.arange(block), high + jnp.arange(block)])
    keep = jnp.arange(seq)[None, :] <= places[:, None]
    scaling = HEAD ** (-0.5)

    def scores_of():
        raw = jnp.einsum("thd,sd->hts", queries, key, preferred_element_type=F32)
        return jnp.where(keep[None], raw * scaling, NEG)

    scores = scores_of()
    top = jnp.max(scores, axis=-1)
    lse = top + jnp.log(jnp.sum(jnp.exp(scores - top[..., None]), axis=-1))
    probs = jnp.exp(scores - lse[..., None]).astype(BF)
    attn = jnp.einsum("hts,sd->thd", probs, value, preferred_element_type=F32)
    attn = attn.reshape(2 * block, query_cols).astype(BF)
    proj = lax.psum_scatter(
        dot(attn, out_w, 1, 0), "row", scatter_dimension=0, tiled=True
    )
    mid = input_shard + proj
    scale2, unit2, normed2 = normalize(mid, gain2)
    normed2_all = lax.all_gather(normed2, ("row", "col"), tiled=True)

    gate = dot(normed2_all, gate_w, 1, 0)
    up = dot(normed2_all, up_w, 1, 0)
    d_hidden = dot(grads_all, down_w, 1, 1)
    sig = jax.nn.sigmoid(gate)
    act = gate * sig
    hidden = (act * up).astype(BF)
    d_gate = (d_hidden * up * sig * (1.0 + gate * (1.0 - sig))).astype(BF)
    d_up = (d_hidden * act).astype(BF)
    d_normed2_part = dot(d_gate, gate_w, 1, 1) + dot(d_up, up_w, 1, 1)

    def shards_sum(partial):
        return lax.psum_scatter(
            partial.astype(BF), ("row", "col"), scatter_dimension=0, tiled=True
        ).astype(F32)

    d_normed2 = shards_sum(d_normed2_part)
    start = (row * 4 + col) * block
    ffn = dot(hidden, down_w, 1, 0)
    ffn = lax.dynamic_update_slice_in_dim(ffn, rows_of(ffn, start, block) + mid, start, 0)
    ffn = mirror(ffn).reshape(2, half, 4, feat).transpose(0, 2, 1, 3).reshape(8 * half, feat)
    layer_output = shards_sum(ffn)

    def sum_dp(grad):
        rows = grad.shape[1] // n_dp
        sliced = grad.astype(BF).reshape(4, n_dp, rows, -1).transpose(1, 0, 2, 3)
        mine = lax.psum_scatter(sliced, "dp", scatter_dimension=0, tiled=True)[0]
        return lax.all_to_all(mine, "col", 0, 0, tiled=True)

    def spread(grad):
        return lax.all_gather(grad, "dp", axis=0, tiled=True).astype(F32)

    def down_order(grad):
        return grad.reshape(part, 4, feat).transpose(1, 0, 2)

    grad_down = sum_dp(down_order(dot(hidden, grads_all, 0, 0)))
    grad_gate = sum_dp(dot(normed2_all, d_gate, 0, 0).reshape(4, feat, part))
    grad_up = sum_dp(dot(normed2_all, d_up, 0, 0).reshape(4, feat, part))

    d_mid_norm, grad_gain_ffn = norm_back(d_normed2, gain2, scale2, unit2)
    d_mid = rows_of(grads_all, start, block).astype(F32) + d_mid_norm
    d_mid_low = d_mid.astype(BF)
    d_mid_all = lax.all_gather(d_mid_low, ("row", "col"))
    d_mid_cols = cols_of(d_mid_all.reshape(seq, model), col * feat, feat)
    d_mid_cols = d_mid_cols.reshape(2, 4, block, feat).transpose(1, 0, 2, 3).reshape(seq, feat)
    d_mid_pair = lax.dynamic_slice_in_dim(d_mid_all, col, 1, 0)
    d_mid_pair = jnp.concatenate([d_mid_pair, lax.dynamic_slice_in_dim(d_mid_all, col + 4, 1, 0)])
    d_mid_pair = d_mid_pair.reshape(2 * block, model)
    attn_all = lax.all_gather(attn, "col", tiled=True)
    grad_out = dot(attn_all, d_mid_cols, 0, 0)
    d_attn = dot(d_mid_pair, out_w, 1, 1).astype(BF).reshape(2 * block, heads, HEAD)

    exact = jnp.exp(scores_of() - lse[..., None])
    d_probs = jnp.einsum("thd,sd->hts", d_attn, value, preferred_element_type=F32)
    inner = jnp.sum(exact * d_probs, axis=-1)
    d_scores = (exact * (d_probs - inner[..., None]) * scaling).astype(BF)
    d_query = jnp.einsum("hts,sd->thd", d_scores, key, preferred_element_type=F32)
    d_key = jnp.einsum("hts,thd->sd", d_scores, queries, preferred_element_type=F32)
    d_value = jnp.einsum("hts,thd->sd", exact.astype(BF), d_attn, preferred_element_type=F32)
    d_kv = jnp.concatenate([d_key, d_value], axis=1)
    d_kv = jnp.stack([d_kv[:half].reshape(4, block, -1), d_kv[half:].reshape(4, block, -1)[::-1]], 1)
    d_kv = lax.psum_scatter(
        d_kv.reshape(seq, 2 * HEAD), "col", scatter_dimension=0, tiled=True
    )
    d_query = unrotate(d_query, cos_pair[:, None, :], sin_pair[:, None, :])
    d_key = unrotate(d_kv[:, :HEAD], cos_pair, sin_pair)
    d_qkv = jnp.concatenate(
        [d_query.reshape(2 * block, query_cols), d_key, d_kv[:, HEAD:]], axis=1
    ).astype(BF)
    d_normed1 = lax.psum_scatter(dot(d_qkv, qkv_w, 1, 1), "row", scatter_dimension=0, tiled=True)
    d_qkv_all = lax.all_gather(d_qkv, "col", tiled=True)
    normed1_cols = cols_of(normed1, col * feat, feat)
    normed1_cols = jnp.stack(
        [normed1_cols[:half].reshape(4, block, -1), normed1_cols[half:].reshape(4, block, -1)[::-1]],
        1,
    ).reshape(seq, feat)
    grad_qkv = dot(normed1_cols, d_qkv_all, 0, 0)
    grad_bias = jnp.sum(d_qkv_all.astype(F32), axis=0)
    d_in_norm, grad_gain_attn = norm_back(d_normed1, gain1, scale1, unit1)
    grad_input = (d_mid + d_in_norm).astype(BF)
    grad_input = lax.all_to_all(
        grad_input.reshape(block, 4, feat).transpose(1, 0, 2), "col", 0, 0, tiled=True
    )
    grad_input = jnp.where(row == 0, grad_input, grad_input[::-1]).reshape(half, feat).astype(F32)

    def sum_all(grad):
        mine = lax.psum_scatter(grad.astype(BF), "dp", scatter_dimension=0, tiled=True)
        return spread(mine)

    grad_qkv = sum_all(grad_qkv)
    grad_out = sum_all(grad_out)
    gains = lax.psum(jnp.stack([grad_gain_attn, grad_gain_ffn]), ("dp", "row", "col"))
    gains = cols_of(gains, col * feat, feat)
    grad_bias = lax.psum(grad_bias, "dp")

    def join(grad):
        return spread(grad.transpose(1, 0, 2).reshape(grad.shape[1], padded)[:, :units])

    def join_down(grad):
        joined = grad.reshape(4, grad.shape[1], feat)
        gathered = lax.all_gather(joined, "dp", axis=1, tiled=True)
        return gathered.reshape(padded, feat)[:units].astype(F32)

    return (
        layer_output,
        grad_input,
        gains[0],
        grad_qkv[:, :query_cols],
        grad_qkv[:, query_cols : query_cols + HEAD],
        grad_qkv[:, query_cols + HEAD :],
        grad_bias[:query_cols],
        grad_bias[query_cols : query_cols + HEAD],
        grad_bias[query_cols + HEAD :],
        grad_out,
        gains[1],
        join(grad_gate),
        join(grad_up),
        join_down(grad_down),
    )


def solution(mesh):
    in_specs = (
        P(("dp", "row"), "col"),
        P("col"),
        P("col", "row"),
        P("col", "row"),
        P("col", "row"),
        P("row"),
        P("row"),
        P("row"),
        P("row", "col"),
        P("col"),
        P("col", "row"),
        P("col", "row"),
        P("row", "col"),
        P(("dp", "row"), "col"),
    )
    out_specs = (
        P(("dp", "row"), "col"),
        P(("dp", "row"), "col"),
        P("col"),
        P("col", "row"),
        P("col", "row"),
        P("col", "row"),
        P("row"),
        P("row"),
        P("row"),
        P("row", "col"),
        P("col"),
        P("col", "row"),
        P("col", "row"),
        P("row", "col"),
    )
    return jax.shard_map(body, mesh=mesh, in_specs=in_specs, out_specs=out_specs, check_vma=False)
```

time: 1420 us -> 1190 us (0.84)
  waiting for transfers between devices: 938 us -> 593 us
  local copies, waits for them, and re-layouts: 49.4 us -> 110 us
  blocking collectives: 213 us -> 247 us
  other arithmetic: 46.4 us -> 77.8 us
  matrix products: 147 us -> 121 us
  starting transfers between devices: 1.47 us -> 19.1 us
    reduce_scatter x10 -> x5, waiting for transfers between devices: 523 us -> 106 us  [the longest x2 72.9 us: shards_sum(): lax.psum_scatter(partial.astype(BF), ('row', 'col'), scatter_dimension=0,...]
    unnamed x15 -> x25, waiting for transfers between devices: 0.75 us -> 184 us
    psum x1 -> x0, waiting for transfers between devices: 181 us -> none  [body(): lax.psum((grad_qkv, grad_bias, grad_w_out, grad_both, grad_w_down), 'dp')]
    all_gather x4 -> x12, waiting for transfers between devices: 233 us -> 286 us  [the longest x3 86.4 us: gather_dp(): return lax.all_gather(flip(mine, 2), 'dp', axis=0, tiled=True)]
    all_gather x6, blocking collectives: 59 us -> 109 us  [the longest x2 49.7 us: gather_dp(): return lax.all_gather(flip(mine, 2), 'dp', axis=0, tiled=True)]
    psum x6 -> x2, blocking collectives: 154 us -> 106 us  [the longest x1 67.8 us: body(): lax.psum(jnp.stack([grad_gain_attn, grad_gain_ffn]), ('dp', 'row', 'col'))]
    all_to_all x0 -> x3, blocking collectives: none -> 32.1 us  [sum_dp(): return lax.all_to_all(mine, 'col', 0, 0, tiled=True)]
    dot_general x19 -> x22, matrix products: 147 us -> 121 us  [the longest x16 83.4 us: dot(): lax.dot_general(left, right, (((left_dim,), (right_dim,)), ((), ())), pre...]
  transfers between devices with their start and end apart: 15 -> 37, of which waited for: 12 -> 20; matrix products, arithmetic and copies ran while one was open for 9% -> 20% of each run, Pallas kernels for 0% -> 0%
where the time goes in v1:
time: 1190 us; the launch traced here: 1180 us
  waiting for transfers between devices  593 us (50%)
  blocking collectives  247 us (21%)
  matrix products  121 us (10%)
  local copies, waits for them, and re-layouts  110 us (9%)
  other arithmetic  77.8 us (7%)
  starting transfers between devices  19.1 us (2%)
  between operations  17.4 us (1%)
    unnamed x25, waiting for transfers between devices  184 us
    all_gather x3, waiting for transfers between devices, gather_dp(): return lax.all_gather(flip(mine, 2), 'dp', axis=0, tiled=True)  86.4 us
    dot_general x16, matrix products, dot(): lax.dot_general(left, right, (((left_dim,), (right_dim,)), ((), ())), pre...  83.4 us
    reduce_scatter x2, waiting for transfers between devices, shards_sum(): lax.psum_scatter(partial.astype(BF), ('row', 'col'), scatter_dimension=0,...  72.9 us
    all_gather x2, waiting for transfers between devices, spread(): return lax.all_gather(grad, 'dp', axis=0, tiled=True).astype(F32)  70.4 us
    psum x1, blocking collectives, body(): lax.psum(jnp.stack([grad_gain_attn, grad_gain_ffn]), ('dp', 'row', 'col'))  67.8 us
    all_gather x2, blocking collectives, gather_dp(): return lax.all_gather(flip(mine, 2), 'dp', axis=0, tiled=True)  49.7 us
    all_gather x2, blocking collectives, spread(): return lax.all_gather(grad, 'dp', axis=0, tiled=True).astype(F32)  46.1 us
  transfers between devices with their start and end apart: 37, of which 20 were waited for; matrix products, arithmetic and copies ran while one was open for 20% of the time, Pallas kernels for 0%

profile of v1, /device:TPU:0, one launch (start us, length us, event | category | flops | bytes accessed | tf_op | source)
XLA Modules:
  0.0 1184.3 jit_solution(12220765604300554481)
XLA Ops:
  19.9 6.8 all-gather.3
  29.3 25.8 %all_gather.67 = bf16[768,384]{1,0:T(8,128)(2,1)S(1)} all-gather(bf16[48,384]{1,0:T(8,128)(2,1)S(1)} %collective-permute-done.4), channel_id=1, replica_groups=mesh['dp'=16,'row'=2,'col'=4] {'dp'}, dimensions={0}, use_global_device_ids=true | all-gather | bytes 626688 | tf_op jit(solution)/shard_map/all_gather | solution.py:56
  56.6 23.9 %all_gather.66 = bf16[384,1024]{1,0:T(8,128)(2,1)S(1)} all-gather(bf16[24,1024]{1,0:T(8,128)(2,1)S(1)} %collective-permute-done.1), channel_id=1, replica_groups=mesh['dp'=16,'row'=2,'col'=4] {'dp'}, dimensions={0}, use_global_device_ids=true | all-gather | bytes 835584 | tf_op jit(solution)/shard_map/all_gather | solution.py:56
  161.7 6.7 all-gather.4
  188.1 39.9 %all-gather.22.cloned.1.call-done = bf16[384,2304]{1,0:T(8,128)(2,1)} async-done(((bf16[24,2304]{1,0:T(8,128)(2,1)}), bf16[384,2304]{1,0:T(8,128)(2,1)}) %all-gather.22.cloned.1.call-update) | async-done | bytes 1769488 | tf_op jit(solution)/shard_map/all_gather | solution.py:56
  230.8 43.2 %all-gather.24.cloned.1.call-done = bf16[2304,384]{1,0:T(8,128)(2,1)} async-done(((bf16[144,384]{1,0:T(8,128)(2,1)}), bf16[2304,384]{1,0:T(8,128)(2,1)}) %all-gather.24.cloned.1.call-update) | async-done | bytes 1769488 | tf_op jit(solution)/shard_map/all_gather | solution.py:56
  309.0 9.2 all-gather.38.cloned.1.call-done
  329.1 34.8 %all-gather.18.cloned.1.call-done = bf16[1024,1536]{1,0:T(8,128)(2,1)} async-done(((bf16[128,1536]{1,0:T(8,128)(2,1)}), bf16[1024,1536]{1,0:T(8,128)(2,1)}) %all-gather.18.cloned.1.call-update) | async-done | bytes 3145744 | tf_op jit(solution)/shard_map/all_gather | solution.py:188
  363.9 7.3 fusion.86
  377.4 9.6 multiply_convert_fusion.1
  397.2 9.7 fusion.87
  406.9 35.6 %reduce-scatter.21.cloned.1.call-done = bf16[128,1536]{1,0:T(8,128)(2,1)} async-done(((bf16[1024,1536]{1,0:T(8,128)(2,1)}), bf16[128,1536]{1,0:T(8,128)(2,1)}) %reduce-scatter.21.cloned.1.call-update) | async-done | bytes 393232 | tf_op jit(solution)/shard_map/reduce_scatter | solution.py:201
  447.6 8.8 convolution_convert_fusion.1
  472.3 17.8 %all-gather.40.cloned.1.call-done = bf16[1024,1536]{1,0:T(8,128)(2,1)} async-done(((bf16[128,1536]{1,0:T(8,128)(2,1)}), bf16[1024,1536]{1,0:T(8,128)(2,1)}) %all-gather.40.cloned.1.call-update) | async-done | bytes 3145744 | tf_op jit(solution)/shard_map/all_gather | solution.py:231
  497.9 11.3 convolution_bitcast_fusion.2
  537.7 53.6 %all-reduce.11.cloned.1.call-done = (bf16[16,4,24,1152]{3,2,0,1:T(8,128)(2,1)}, bf16[16,4,24,1152]{3,2,0,1:T(8,128)(2,1)}) async-done(((bf16[16,4,24,1152]{3,2,0,1:T(8,128)(2,1)}, bf16[16,4,24,1152]{3,2,0,1:T(8,128)(2,1)}), (bf16[16,4,24,1152]{3,2,0,1:T(8,128)(2,1)}, bf16[16,4,24,1152]{3,2,0,1:T(8,128)(2,1)})) %all-reduce.11.cloned.1.call-update) | async-done | bytes 7077904
  592.9 11.2 all_to_all.20
  606.5 9.5 all_to_all.21
  616.8 54.0 %reduce-scatter.31.cloned.1.call-done = bf16[1,4,72,384]{3,2,1,0:T(8,128)(2,1)} async-done(((bf16[16,4,72,384]{3,2,1,0:T(8,128)(2,1)}), bf16[1,4,72,384]{3,2,1,0:T(8,128)(2,1)}) %reduce-scatter.31.cloned.1.call-update) | async-done | bytes 221200
  670.8 11.5 all_to_all.22
  682.6 13.5 %broadcast_multiply_fusion = (f32[256,6,128]{0,2,1:T(8,128)}, f32[256,6,128]{0,2,1:T(8,128)}) fusion(f32[256,128]{0,1:T(8,128)S(1)} %copy-done.42, f32[1024,256,6]{1,0,2:T(8,128)} %fusion.51, f32[1024,256,6]{1,0,2:T(8,128)} %copy-done, f32[6,256]{1,0:T(8,128)S(1)} %copy-done.51, pred[256,1024]{0,1:T(8,128)(4,1)} %copy-done.22, ...), kind=kOutput, calls=%fused_computation.139 | convolution fusion | flops 420153856 | bytes 14817280 | tf_op jit(solution)/shard_map/hts,sd->thd/dot_general | solution.py:245
  713.7 37.3 %reduce-scatter.19.cloned.1.call-done = bf16[512,384]{1,0:T(8,128)(2,1)} async-done(((bf16[4096,384]{1,0:T(8,128)(2,1)}), bf16[512,384]{1,0:T(8,128)(2,1)}) %reduce-scatter.19.cloned.1.call-update) | async-done | bytes 393232 | tf_op jit(solution)/shard_map/reduce_scatter | solution.py:201
  752.9 74.1 %reduce-scatter.29.cloned.1.call-done = bf16[48,384]{1,0:T(8,128)(2,1)} async-done(((bf16[768,384]{1,0:T(8,128)(2,1)}), bf16[48,384]{1,0:T(8,128)(2,1)}) %reduce-scatter.29.cloned.1.call-update) | async-done | bytes 36880
  827.1 23.9 %all_gather.80 = bf16[768,384]{1,0:T(8,128)(2,1)S(1)} all-gather(bf16[48,384]{1,0:T(8,128)(2,1)} %reduce-scatter.29.cloned.1.call-done), channel_id=1, replica_groups=mesh['dp'=16,'row'=2,'col'=4] {'dp'}, dimensions={0}, use_global_device_ids=true | all-gather | bytes 626688 | tf_op jit(solution)/shard_map/all_gather | solution.py:219
  852.1 25.5 %all-gather.30.cloned.1.call-done = bf16[384,4480]{1,0:T(8,128)(2,1)} async-done(((bf16[24,4480]{1,0:T(8,128)(2,1)}), bf16[384,4480]{1,0:T(8,128)(2,1)}) %all-gather.30.cloned.1.call-update) | async-done | bytes 3440656 | tf_op jit(solution)/shard_map/all_gather | solution.py:219
  882.9 44.8 %all-gather.32.cloned.1.call-done = bf16[384,4480]{1,0:T(8,128)(2,1)} async-done(((bf16[24,4480]{1,0:T(8,128)(2,1)}), bf16[384,4480]{1,0:T(8,128)(2,1)}) %all-gather.32.cloned.1.call-update) | async-done | bytes 3440656 | tf_op jit(solution)/shard_map/all_gather | solution.py:219
  933.1 45.1 %all-gather.34.cloned.1.call-done = bf16[4,1152,384]{2,1,0:T(8,128)(2,1)} async-done(((bf16[4,72,384]{2,1,0:T(8,128)(2,1)}), bf16[4,1152,384]{2,1,0:T(8,128)(2,1)}) %all-gather.34.cloned.1.call-update) | async-done | bytes 3538960 | tf_op jit(solution)/shard_map/all_gather | solution.py:289
  983.5 22.5 %all-gather.26.cloned.1.call-done = bf16[1024,1024]{0,1:T(8,128)(2,1)} async-done(((bf16[256,1024]{0,1:T(8,128)(2,1)}), bf16[1024,1024]{0,1:T(8,128)(2,1)}) %all-gather.26.cloned.1.call-update) | async-done | bytes 2097168 | tf_op jit(solution)/shard_map/all_gather | solution.py:259
  1009.6 26.9 %reduce-scatter.25.cloned.1.call-done = f32[128,1536]{1,0:T(8,128)} async-done(((f32[256,1536]{1,0:T(8,128)}), f32[128,1536]{1,0:T(8,128)}) %reduce-scatter.25.cloned.1.call-update) | async-done | bytes 786448 | tf_op jit(solution)/shard_map/reduce_scatter | solution.py:258
  1044.7 67.8 %psum.14 = f32[2,1536]{1,0:T(2,128)S(1)} all-reduce(f32[2,1536]{1,0:T(2,128)S(1)} %pad_maximum_fusion.18), channel_id=1, replica_groups=mesh['dp'=16,'row'=2,'col'=4] {'dp','row','col'}, use_global_device_ids=true, to_apply=%region_15.17 | all-reduce | flops 3072 | bytes 24576 | tf_op jit(solution)/shard_map/psum | solution.py:280
  1113.2 37.8 %psum.15 = f32[1024]{0:T(1024)S(1)} all-reduce(f32[1024]{0:T(1024)S(1)} %convert_reduce_fusion), channel_id=1, replica_groups=mesh['dp'=16,'row'=2,'col'=4] {'dp'}, use_global_device_ids=true, to_apply=%region_18.20 | all-reduce | flops 1024 | bytes 8192 | tf_op jit(solution)/shard_map/psum | solution.py:282
  1152.5 22.1 %all_gather.78 = bf16[384,1024]{1,0:T(8,128)(2,1)S(1)} all-gather(bf16[24,1024]{1,0:T(8,128)(2,1)} %reduce-scatter.27.cloned.1.call-done), channel_id=1, replica_groups=mesh['dp'=16,'row'=2,'col'=4] {'dp'}, dimensions={0}, use_global_device_ids=true | all-gather | bytes 835584 | tf_op jit(solution)/shard_map/all_gather | solution.py:219
  (366 shorter events, 295.3 us)
Async XLA Ops:
  8.0 91.4 %all-gather.36.cloned.1.call-start = ((), (), s32[]{:S(2)}) async-start(), calls=%async_computation.26 | async-start | bytes 3538944 | tf_op jit(solution)/shard_map/all_gather | solution.py:127
  8.8 159.6 %reduce-scatter.17.cloned.1.call-start = ((), (), s32[]{:S(2)}) async-start(), calls=%async_computation.12 | async-start | bytes 2359296 | tf_op jit(solution)/shard_map/reduce_scatter | solution.py:183
  8.8 71.9 %collective-permute-start.3 = (bf16[768,384]{1,0:T(8,128)(2,1)}, bf16[768,384]{1,0:T(8,128)(2,1)S(1)}, u32[]{:S(2)}, u32[]{:S(2)}) collective-permute-start(bf16[768,384]{1,0:T(8,128)(2,1)} %param.24), channel_id=1, source_target_pairs={{0,1},{1,0},{2,3},{3,2},{4,5},{5,4},{6,7},{7,6},{8,9},{9,8},{10,11... | collective-permute-start | bytes 1769480 | tf_op jit(solution)/shard_map/ppermute | solution.py:23
  9.7 19.5 %collective-permute-start.4 = (bf16[48,384]{1,0:T(8,128)(2,1)S(1)}, bf16[48,384]{1,0:T(8,128)(2,1)S(1)}, u32[]{:S(2)}, u32[]{:S(2)}) collective-permute-start(bf16[48,384]{1,0:T(8,128)(2,1)S(1)} %constant_dynamic-slice_fusion.8), channel_id=1, source_target_pairs={{0,2},{1,3},{2,0},{3,1},{4,6},{5,7},{6,4},{7,5},{8,10},{9,11},{10,... | collective-permute-start | bytes 110600 | tf_op jit(solution)/shard_map/ppermute | solution.py:23
  17.8 73.1 %collective-permute-start = (bf16[384,1024]{1,0:T(8,128)(2,1)}, bf16[384,1024]{1,0:T(8,128)(2,1)}, u32[]{:S(2)}, u32[]{:S(2)}) collective-permute-start(bf16[384,1024]{1,0:T(8,128)(2,1)} %constant_dynamic-update-slice_fusion), channel_id=1, source_target_pairs={{0,1},{1,0},{2,3},{3,2},{4,5},{5,4},{6,7},{7,6},{8,9},{9,8},{10,11... | collective-permute-start | bytes 2359304 | tf_op jit(solution)/shard_map/ppermute | solution.py:23
  18.8 37.8 %collective-permute-start.1 = (bf16[24,1024]{1,0:T(8,128)(2,1)S(1)}, bf16[24,1024]{1,0:T(8,128)(2,1)S(1)}, u32[]{:S(2)}, u32[]{:S(2)}) collective-permute-start(bf16[24,1024]{1,0:T(8,128)(2,1)S(1)} %constant_dynamic-slice_fusion.11), channel_id=1, source_target_pairs={{0,2},{1,3},{2,0},{3,1},{4,6},{5,7},{6,4},{7,5},{8,10},{9,11},{10,... | collective-permute-start | bytes 147464 | tf_op jit(solution)/shard_map/ppermute | solution.py:23
  55.1 25.7 %collective-permute-start.5 = (bf16[768,384]{1,0:T(8,128)(2,1)S(1)}, bf16[768,384]{1,0:T(8,128)(2,1)S(1)}, u32[]{:S(2)}, u32[]{:S(2)}) collective-permute-start(bf16[768,384]{1,0:T(8,128)(2,1)S(1)} %all_gather.67), channel_id=1, source_target_pairs={{0,1},{1,0},{2,3},{3,2},{4,5},{5,4},{6,7},{7,6},{8,9},{9,8},{10,11... | collective-permute-start | bytes 1769480 | tf_op jit(solution)/shard_map/ppermute | solution.py:23
  130.0 52.0 %all-gather.20.cloned.1.call-start = ((), (), s32[]{:S(2)}) async-start(), calls=%async_computation.14 | async-start | bytes 1880064 | tf_op jit(solution)/shard_map/all_gather | solution.py:56
  138.8 89.2 %all-gather.22.cloned.1.call-start = ((), (), s32[]{:S(2)}) async-start(), calls=%async_computation.15 | async-start | bytes 1880064 | tf_op jit(solution)/shard_map/all_gather | solution.py:56
  150.0 124.0 %all-gather.24.cloned.1.call-start = ((), (), s32[]{:S(2)}) async-start(), calls=%async_computation.16 | async-start | bytes 1880064 | tf_op jit(solution)/shard_map/all_gather | solution.py:56
  160.8 157.3 %all-gather.38.cloned.1.call-start = ((), (), s32[]{:S(2)}) async-start(), calls=%async_computation.27 | async-start | bytes 3538944 | tf_op jit(solution)/shard_map/all_gather | solution.py:127
  161.6 202.3 %all-gather.18.cloned.1.call-start = ((), (), s32[]{:S(2)}) async-start(), calls=%async_computation.13 | async-start | bytes 3538944 | tf_op jit(solution)/shard_map/all_gather | solution.py:188
  172.1 270.4 %reduce-scatter.21.cloned.1.call-start = ((), (), s32[]{:S(2)}) async-start(), calls=%async_computation.18 | async-start | bytes 3538944 | tf_op jit(solution)/shard_map/reduce_scatter | solution.py:201
  175.9 100.9 %collective-permute-start.6 = (bf16[384,1152]{1,0:T(8,128)(2,1)}, bf16[384,1152]{1,0:T(8,128)(2,1)}, u32[]{:S(2)}, u32[]{:S(2)}) collective-permute-start(bf16[384,1152]{1,0:T(8,128)(2,1)} %get-tuple-element.35), channel_id=1, source_target_pairs={{0,1},{1,0},{2,3},{3,2},{4,5},{5,4},{6,7},{7,6},{8,9},{9,8},{10,11... | collective-permute-start | bytes 2654216 | tf_op jit(solution)/shard_map/ppermute | solution.py:23
  178.5 104.4 %collective-permute-start.9 = (bf16[384,1152]{1,0:T(8,128)(2,1)}, bf16[384,1152]{1,0:T(8,128)(2,1)}, u32[]{:S(2)}, u32[]{:S(2)}) collective-permute-start(bf16[384,1152]{1,0:T(8,128)(2,1)} %get-tuple-element.37), channel_id=1, source_target_pairs={{0,1},{1,0},{2,3},{3,2},{4,5},{5,4},{6,7},{7,6},{8,9},{9,8},{10,11... | collective-permute-start | bytes 2654216 | tf_op jit(solution)/shard_map/ppermute | solution.py:23
  184.5 92.4 %collective-permute-start.8 = (bf16[384,1152]{1,0:T(8,128)(2,1)S(1)}, bf16[384,1152]{1,0:T(8,128)(2,1)S(1)}, u32[]{:S(2)}, u32[]{:S(2)}) collective-permute-start(bf16[384,1152]{1,0:T(8,128)(2,1)S(1)} %get-tuple-element.50), channel_id=1, source_target_pairs={{0,1},{1,0},{2,3},{3,2},{4,5},{5,4},{6,7},{7,6},{8,9},{9,8},{10,11... | collective-permute-start | bytes 2654216 | tf_op jit(solution)/shard_map/ppermute | solution.py:23
  187.6 100.4 %collective-permute-start.12 = (bf16[1152,384]{1,0:T(8,128)(2,1)}, bf16[1152,384]{1,0:T(8,128)(2,1)}, u32[]{:S(2)}, u32[]{:S(2)}) collective-permute-start(bf16[1152,384]{1,0:T(8,128)(2,1)} %get-tuple-element.33), channel_id=1, source_target_pairs={{0,1},{1,0},{2,3},{3,2},{4,5},{5,4},{6,7},{7,6},{8,9},{9,8},{10,11... | collective-permute-start | bytes 2654216 | tf_op jit(solution)/shard_map/ppermute | solution.py:23
  230.8 52.2 %collective-permute-start.11 = (bf16[384,1152]{1,0:T(8,128)(2,1)}, bf16[384,1152]{1,0:T(8,128)(2,1)}, u32[]{:S(2)}, u32[]{:S(2)}) collective-permute-start(bf16[384,1152]{1,0:T(8,128)(2,1)} %get-tuple-element.52), channel_id=1, source_target_pairs={{0,1},{1,0},{2,3},{3,2},{4,5},{5,4},{6,7},{7,6},{8,9},{9,8},{10,11... | collective-permute-start | bytes 2654216 | tf_op jit(solution)/shard_map/ppermute | solution.py:23
  397.1 93.1 %all-gather.40.cloned.1.call-start = ((), (), s32[]{:S(2)}) async-start(), calls=%async_computation.28 | async-start | bytes 3538944 | tf_op jit(solution)/shard_map/all_gather | solution.py:231
  446.8 86.9 %all-gather.28.cloned.1.call-start = ((), (), s32[]{:S(2)}) async-start(), calls=%async_computation.22 | async-start | bytes 1966080 | tf_op jit(solution)/shard_map/all_gather | solution.py:237
  447.4 144.0 %all-reduce.11.cloned.1.call-start = ((), (), s32[]{:S(2)}) async-start(), calls=%async_computation.32 | async-start | bytes 14155776
  462.3 208.5 %reduce-scatter.31.cloned.1.call-start = ((), (), s32[]{:S(2)}) async-start(), calls=%async_computation.31 | async-start | bytes 3760128
  472.1 232.6 %reduce-scatter.23.cloned.1.call-start = ((), (), s32[]{:S(2)}) async-start(), calls=%async_computation.19 | async-start | bytes 1310720 | tf_op jit(solution)/shard_map/reduce_scatter | solution.py:250
  518.1 232.9 %reduce-scatter.19.cloned.1.call-start = ((), (), s32[]{:S(2)}) async-start(), calls=%async_computation.17 | async-start | bytes 3538944 | tf_op jit(solution)/shard_map/reduce_scatter | solution.py:201
  532.3 294.7 %reduce-scatter.29.cloned.1.call-start = ((), (), s32[]{:S(2)}) async-start(), calls=%async_computation.30 | async-start | bytes 626688
  537.1 340.5 %all-gather.30.cloned.1.call-start = ((), (), s32[]{:S(2)}) async-start(), calls=%async_computation.23 | async-start | bytes 3655680 | tf_op jit(solution)/shard_map/all_gather | solution.py:219
  604.8 322.9 %all-gather.32.cloned.1.call-start = ((), (), s32[]{:S(2)}) async-start(), calls=%async_computation.24 | async-start | bytes 3655680 | tf_op jit(solution)/shard_map/all_gather | solution.py:219
  616.7 361.4 %all-gather.34.cloned.1.call-start = ((), (), s32[]{:S(2)}) async-start(), calls=%async_computation.25 | async-start | bytes 3760128 | tf_op jit(solution)/shard_map/all_gather | solution.py:289
  682.3 323.7 %all-gather.26.cloned.1.call-start = ((), (), s32[]{:S(2)}) async-start(), calls=%async_computation.21 | async-start | bytes 2621440 | tf_op jit(solution)/shard_map/all_gather | solution.py:259
  709.1 327.4 %reduce-scatter.25.cloned.1.call-start = ((), (), s32[]{:S(2)}) async-start(), calls=%async_computation.20 | async-start | bytes 2359296 | tf_op jit(solution)/shard_map/reduce_scatter | solution.py:258
  712.3 440.3 %reduce-scatter.27.cloned.1.call-start = ((), (), s32[]{:S(2)}) async-start(), calls=%async_computation.29 | async-start | bytes 835584
  1040.4 111.1 %all-to-all-start = ((bf16[4,128,384]{2,1,0:T(8,128)(2,1)}), bf16[4,128,384]{2,1,0:T(8,128)(2,1)S(1)}, u32[]{:S(2)}, u32[]{:S(2)}) async-start(bf16[4,128,384]{2,1,0:T(8,128)(2,1)} %bitcast.231), calls=%async_computation.5 | async-start | bytes 786432 | tf_op jit(solution)/shard_map/all_to_all | solution.py:269
  (73 other events, 1283.7 us)
Sparse Core Ops, SparseCore 0:
  10.5 45.7 all-gather.35
  130.1 31.7 reduce-scatter.16
  397.2 45.2 reduce-scatter.20
  446.9 43.2 all-gather.39
  492.4 23.6 all-gather.27
Sparse Core Ops, SparseCore 1:
  138.9 43.0 all-gather.19
  184.0 43.9 all-gather.21
  230.0 43.9 all-gather.23
  275.6 42.4 all-gather.37
  319.9 43.9 all-gather.17
  462.3 128.9 all-reduce.10
  594.6 76.2 reduce-scatter.30
  673.9 30.8 reduce-scatter.22
  707.1 43.8 reduce-scatter.18
  755.1 71.9 reduce-scatter.28
  829.3 48.2 all-gather.29
  880.0 47.7 all-gather.31
  930.1 48.1 all-gather.33
  980.5 25.4 all-gather.25
  1008.5 27.9 reduce-scatter.24
  1040.2 74.0 reduce-scatter.26

commit v2 on v1

v2 whole, which is shorter than its diff:
```python
import functools

import jax
import jax.numpy as jnp
from jax import lax
from jax.experimental import pallas as pl
from jax.experimental.pallas import tpu as pltpu
from jax.sharding import PartitionSpec as P

EPS = 1e-06
THETA = 1000000.0
NEG = -1e30
BF = jnp.bfloat16
F32 = jnp.float32
MESH = pl.DeviceIdType.MESH
HEAD = 128
HEADS = 6
SEQ = 1024
MODEL = 1536
FEAT = 384
BLOCK = 128
UNITS = 4480
PART = 1152
QCOLS = 768
QKV = 1024
VMEM_LIMIT = 62 * 2**20
SCALE = HEAD ** (-0.5)


def dot(left, right, left_dim=1, right_dim=0):
    return lax.dot_general(
        left, right, (((left_dim,), (right_dim,)), ((), ())), preferred_element_type=F32
    )


def aligned(index, step):
    return pl.multiple_of(index * step, step)


def block_of(row, col):
    return col + row * (7 - 2 * col)


def quarter_start(col):
    return pl.multiple_of(col * PART - (col // 3) * HEAD, HEAD)


class Place:
    def __init__(self):
        self.dp, self.row, self.col = (lax.axis_index(a) for a in ("dp", "row", "col"))
        self.hi, self.core = self.col // 2, self.col % 2
        self.z, self.y = self.dp // 4, self.dp % 4
        self.sib = 2 * self.hi + 1 - self.core
        self.far = 2 * (1 - self.hi) + self.core
        self.sibfar = 2 * (1 - self.hi) + 1 - self.core
        self.block = block_of(self.row, self.col)
        self.S = {"col": self.sib}
        self.O = {"col": self.far}
        self.OS = {"col": self.sibfar}
        self.N1 = {"row": 1 - self.row}
        self.N2 = {"row": 1 - self.row, "col": self.far}
        self.N1S = {"row": 1 - self.row, "col": self.sib}
        self.N2S = {"row": 1 - self.row, "col": self.sibfar}

        def dp_at(z, y):
            return {"dp": lax.rem(z + 4, 4) * 4 + lax.rem(y + 4, 4)}

        self.YP, self.YM = dp_at(self.z, self.y + 1), dp_at(self.z, self.y - 1)
        self.ZP, self.ZM = dp_at(self.z + 1, self.y), dp_at(self.z - 1, self.y)

    def meet(self, partners):
        barrier = pltpu.get_barrier_semaphore()
        for device in partners:
            pl.semaphore_signal(barrier, inc=1, device_id=device, device_id_type=MESH)
        pl.semaphore_wait(barrier, len(partners))


class Net:
    def __init__(self, send_sems, recv_sems, at):
        self.ss, self.rs, self.at, self.count, self.sent = send_sems, recv_sems, at, 0, []

    def key(self):
        self.count += 1
        return self.count - 1

    def copy(self, key, src, dst, device):
        return pltpu.make_async_remote_copy(
            src_ref=src,
            dst_ref=dst,
            send_sem=self.ss.at[key],
            recv_sem=self.rs.at[key],
            device_id=device,
            device_id_type=MESH,
        )

    def send(self, src, dst, device):
        key = self.key()
        copy = self.copy(key, src, dst, device)
        copy.start()
        self.sent.append(copy)
        return key

    def take(self, key, dst):
        self.copy(key, dst, dst, self.at.S).wait_recv()

    def finish(self):
        for copy in self.sent:
            copy.wait_send()


class Gather8:
    def __init__(self, net, at, place):
        self.net, self.at, self.place = net, at, place

    def start(self, src):
        net, at = self.net, self.at
        mine = self.place(at.row, at.col, None)
        self.k1 = net.send(src, mine, at.N1)
        self.k2 = net.send(src, mine, at.N2)
        self.k0 = net.send(src, mine, at.S)

    def middle(self):
        net, at, place = self.net, self.at, self.place
        near, away = place(1 - at.row, at.col, None), place(1 - at.row, at.far, None)
        first, last = place(1 - at.row, at.col, 0), place(1 - at.row, at.far, 1)
        net.take(self.k1, near)
        self.ka = net.send(first, first, at.N2)
        self.f1 = net.send(near, near, at.S)
        net.take(self.k2, away)
        self.kb = net.send(last, last, at.N1)
        self.f2 = net.send(away, away, at.S)

    def late(self):
        net, at, place = self.net, self.at, self.place
        first, last = place(at.row, at.far, 0), place(at.row, at.far, 1)
        net.take(self.ka, first)
        self.f3 = net.send(first, first, at.S)
        net.take(self.kb, last)
        self.f4 = net.send(last, last, at.S)

    def end(self):
        net, at, place = self.net, self.at, self.place
        net.take(self.k0, place(at.row, at.sib, None))
        net.take(self.f1, place(1 - at.row, at.sib, None))
        net.take(self.f2, place(1 - at.row, at.sibfar, None))
        net.take(self.f3, place(at.row, at.sibfar, 0))
        net.take(self.f4, place(at.row, at.sibfar, 1))


def ring_dp(net, at, halves):
    def wrap(index):
        return lax.rem(index + 4, 4)

    sides = (((at.YP, at.YM), (at.ZP, at.ZM)), ((at.ZP, at.ZM), (at.YP, at.YM)))
    firsts, seconds = (at.y, at.z), (at.z, at.y)

    def refs(i, a, b):
        return halves[i](b, a) if i == 0 else halves[i](a, b)

    def send(i, a, b, device):
        return [net.send(ref, ref, device) for ref in refs(i, a, b)]

    def take(i, a, b, keys):
        for key, ref in zip(keys, refs(i, a, b), strict=True):
            net.take(key, ref)

    one, two, onward = {}, {}, {}
    for i in (0, 1):
        one[i] = [send(i, firsts[i], seconds[i], side) for side in sides[i][0]]
    for i in (0, 1):
        two[i, 0] = [send(i, firsts[i], seconds[i], side) for side in sides[i][1]]
    yield
    for i in (0, 1):
        minus = wrap(firsts[i] - 1)
        take(i, minus, seconds[i], one[i][0])
        one[i].append(send(i, minus, seconds[i], sides[i][0][0]))
        two[i, 1] = [send(i, minus, seconds[i], side) for side in sides[i][1]]
    yield
    for i in (0, 1):
        plus = wrap(firsts[i] + 1)
        take(i, plus, seconds[i], one[i][1])
        two[i, 2] = [send(i, plus, seconds[i], side) for side in sides[i][1]]
    offsets = (0, -1, 1, 2)
    for q in (0, 1, 2, 3):
        yield
        for i in (0, 1):
            if q == 1:
                across = wrap(firsts[i] + 2)
                take(i, across, seconds[i], one[i][2])
                two[i, 3] = [send(i, across, seconds[i], side) for side in sides[i][1]]
            slot = wrap(firsts[i] + offsets[q])
            minus, plus = wrap(seconds[i] - 1), wrap(seconds[i] + 1)
            take(i, slot, minus, two[i, q][0])
            if q < 2:
                onward[i, q] = send(i, slot, minus, sides[i][1][0])
            take(i, slot, plus, two[i, q][1])
            if q >= 2:
                onward[i, q] = send(i, slot, plus, sides[i][1][1])
    for q in (0, 1, 2, 3):
        yield
        for i in (0, 1):
            slot = wrap(firsts[i] + offsets[q])
            take(i, slot, wrap(seconds[i] + 2), onward[i, q])


def drain(steps):
    for _ in steps:
        pass


def rms(values):
    return lax.rsqrt(jnp.mean(values * values, axis=1, keepdims=True) + EPS)


def turn(values):
    return pltpu.roll(values, HEAD // 2, 1)


def causal(scores, start):
    places = start + lax.broadcasted_iota(jnp.int32, scores.shape, 0)
    keys = lax.broadcasted_iota(jnp.int32, scores.shape, 1)
    return jnp.where(keys <= places, scores, NEG)


def forward_kernel(
    x_ref,
    og_ref,
    wqkv_ref,
    wout_ref,
    wg_ref,
    wu_ref,
    wd_ref,
    gains_ref,
    bias_ref,
    cos_ref,
    sin_ref,
    xs_ref,
    n1c_ref,
    og_all,
    n2_all,
    qw,
    ow,
    gw,
    uw,
    dw,
    q_ref,
    k_ref,
    v_ref,
    lse_ref,
    attn_ref,
    mid_ref,
    gains_all,
    x_all,
    n1,
    part_out,
    part_in,
    send_sems,
    recv_sems,
    local_sems,
):
    at = Place()
    net = Net(send_sems, recv_sems, at)
    at.meet((at.S, at.N1, at.N2, at.O, at.OS, at.YP, at.YM, at.ZP, at.ZM))
    local = []

    def move(src, dst):
        copy = pltpu.make_async_copy(src, dst, local_sems.at[len(local)])
        copy.start()
        local.append(copy)

    def tokens_of(array):
        def place(row, col, part):
            if part is None:
                rows = pl.ds(aligned(row, SEQ // 2), SEQ // 2)
            else:
                rows = pl.ds(aligned(row * 2 + part, SEQ // 4), SEQ // 4)
            return array.at[rows, pl.ds(aligned(col, FEAT), FEAT)]

        return place

    mine, mine_far = aligned(at.col, FEAT), aligned(1 - at.hi, 2 * FEAT)
    move(x_ref, tokens_of(x_all)(at.row, at.col, None))
    move(wqkv_ref, qw.at[pl.ds(mine, FEAT), :])
    move(wout_ref, ow.at[:, pl.ds(mine, FEAT)])
    move(gains_ref, gains_all.at[:, pl.ds(mine, FEAT)])
    start = quarter_start(at.col)
    move(wg_ref.at[:, pl.ds(start, PART)], gw.at[pl.ds(mine, FEAT), :])
    move(wu_ref.at[:, pl.ds(start, PART)], uw.at[pl.ds(mine, FEAT), :])
    move(wd_ref.at[pl.ds(start, PART), :], dw.at[:, pl.ds(mine, FEAT)])
    move(og_ref, tokens_of(og_all)(at.row, at.col, None))

    eighth = at.dp % 8
    across = [net.key() for _ in range(5)]

    def slice_copies(core, first, last):
        device = {"col": 2 * (1 - at.hi) + core}
        rows = pl.ds(aligned(eighth, 48), 48)
        target = pl.ds(pl.multiple_of(mine + eighth * 48, 16), 48)
        columns = pl.ds(core * 512, 512)
        out_rows = pl.ds(pl.multiple_of(core * FEAT + eighth * 48, 16), 48)
        theirs = quarter_start(2 * (1 - at.hi) + core)
        down_rows = pl.ds(pl.multiple_of(theirs + eighth * 144, 16), 144)
        down_target = pl.ds(aligned(eighth, 144), 144)
        pairs = (
            (wqkv_ref.at[rows, columns], qw.at[target, columns]),
            (wout_ref.at[out_rows, :], ow.at[out_rows, pl.ds(mine, FEAT)]),
            (wg_ref.at[rows, pl.ds(theirs, PART)], gw.at[target, :]),
            (wu_ref.at[rows, pl.ds(theirs, PART)], uw.at[target, :]),
            (wd_ref.at[down_rows, :], dw.at[down_target, pl.ds(mine, FEAT)]),
        )
        return [
            pltpu.make_async_remote_copy(
                src_ref=pairs[i][0],
                dst_ref=pairs[i][1],
                send_sem=net.ss.at[spare[core][i]],
                recv_sem=net.rs.at[across[i]],
                device_id=device,
                device_id_type=MESH,
            )
            for i in range(first, last)
        ]

    spare = ([net.key() for _ in range(5)], [net.key() for _ in range(5)])
    chosen = at.core == at.dp // 8

    @pl.when(chosen)
    def _():
        for core in (0, 1):
            for copy in slice_copies(core, 0, 2):
                copy.start()

    gather_x = Gather8(net, at, tokens_of(x_all))
    gather_x.start(x_ref)
    gain_far = net.send(gains_ref, gains_all.at[:, pl.ds(mine, FEAT)], at.N2)
    gain_sib = net.send(gains_ref, gains_all.at[:, pl.ds(mine, FEAT)], at.S)
    near_qw = net.send(wqkv_ref, qw.at[pl.ds(mine, FEAT), :], at.S)
    near_ow = net.send(wout_ref, ow.at[:, pl.ds(mine, FEAT)], at.S)

    @pl.when(chosen)
    def _():
        for core in (0, 1):
            for copy in slice_copies(core, 2, 5):
                copy.start()

    far_half = pl.ds(mine_far, 2 * FEAT)

    def qkv_slices(z, y):
        rows = pl.ds(pl.multiple_of(mine_far + (z * 4 + y) * 48, 16), 48)
        return [qw.at[rows, pl.ds(aligned(at.core, 512), 512)]]

    def out_slices(z, y):
        index = z * 4 + y
        rows = pl.ds(pl.multiple_of(at.core * FEAT + (index % 8) * 48, 16), 48)
        return [ow.at[rows, pl.ds(pl.multiple_of(mine_far + (index // 8) * FEAT, HEAD), FEAT)]]

    def ffn_slices(weights, first, count):
        def slices(z, y):
            index = z * 4 + y
            rows = pl.ds(pl.multiple_of(mine_far + index * 48, 16), 48)
            down_rows = pl.ds(pl.multiple_of((index % 8) * 144 + first, 16), count)
            lanes = pl.ds(pl.multiple_of(mine_far + (index // 8) * FEAT, HEAD), FEAT)
            return [weights.at[rows, :], dw.at[down_rows, lanes]]

        return slices

    net.take(across[0], qkv_slices(at.z, at.y)[0])
    net.take(across[1], out_slices(at.z, at.y)[0])
    ring = ring_dp(net, at, (qkv_slices, out_slices))
    next(ring)
    near = [
        net.send(wg_ref.at[:, pl.ds(quarter_start(at.sib), PART)], gw.at[pl.ds(mine, FEAT), :], at.S),
        net.send(wu_ref.at[:, pl.ds(quarter_start(at.sib), PART)], uw.at[pl.ds(mine, FEAT), :], at.S),
        net.send(wd_ref.at[pl.ds(quarter_start(at.sib), PART), :], dw.at[:, pl.ds(mine, FEAT)], at.S),
    ]
    next(ring)
    next(ring)
    gather_x.middle()
    gains_far = gains_all.at[:, pl.ds(aligned(at.far, FEAT), FEAT)]
    net.take(gain_far, gains_far)
    gain_sibfar = net.send(gains_far, gains_far, at.S)
    next(ring)
    gather_og = Gather8(net, at, tokens_of(og_all))
    gather_x.late()
    gather_og.start(og_ref)
    drain(ring)
    cols_half, rows_half = pl.ds(aligned(at.core, 512), 512), pl.ds(aligned(at.core, FEAT), FEAT)
    far_qw = net.send(qw.at[far_half, cols_half], qw.at[far_half, cols_half], at.S)
    far_ow = net.send(ow.at[rows_half, far_half], ow.at[rows_half, far_half], at.S)
    net.take(across[2], ffn_slices(gw, 0, 80)(at.z, at.y)[0])
    net.take(across[3], ffn_slices(uw, 80, 64)(at.z, at.y)[0])
    net.take(across[4], ffn_slices(uw, 0, 144)(at.z, at.y)[1])
    ring = ring_dp(net, at, (ffn_slices(gw, 0, 80), ffn_slices(uw, 80, 64)))
    next(ring)
    gather_x.end()
    net.take(gain_sib, gains_all.at[:, pl.ds(aligned(at.sib, FEAT), FEAT)])
    net.take(gain_sibfar, gains_all.at[:, pl.ds(aligned(at.sibfar, FEAT), FEAT)])
    for copy in local:
        copy.wait()

    gain1, gain2 = gains_all[0:1, :], gains_all[1:2, :]

    def norm_block(i, carry):
        rows = pl.ds(aligned(i, BLOCK), BLOCK)
        values = x_all[rows, :].astype(F32)
        n1[rows, :] = (values * rms(values) * gain1).astype(BF)
        return carry

    lax.fori_loop(0, SEQ // BLOCK, norm_block, 0)
    next(ring)
    gather_og.middle()
    my_rows = pl.ds(aligned(at.block, BLOCK), BLOCK)
    xs_ref[...] = x_all[my_rows, :]
    n1c_ref[...] = n1[:, pl.ds(mine, FEAT)]
    net.take(near_qw, qw.at[pl.ds(aligned(at.sib, FEAT), FEAT), :])
    other_cols = pl.ds(aligned(1 - at.core, 512), 512)
    net.take(far_qw, qw.at[far_half, other_cols])

    def kv_block(i, carry):
        rows = pl.ds(aligned(i, 256), 256)
        both = dot(n1[rows, :], qw[:, QCOLS:]) + bias_ref[:, QCOLS:]
        key = both[:, :HEAD]
        k_ref[rows, :] = (key * cos_ref[rows, :] + turn(key) * sin_ref[rows, :]).astype(BF)
        v_ref[rows, :] = both[:, HEAD:].astype(BF)
        return carry

    lax.fori_loop(0, SEQ // 256, kv_block, 0)
    next(ring)
    pair = (at.col, 7 - at.col)
    for j in (0, 1):
        rows = pl.ds(aligned(pair[j], BLOCK), BLOCK)
        queries = dot(n1[rows, :], qw[:, :QCOLS]) + bias_ref[:, :QCOLS]
        cosine, sine = cos_ref[rows, :], sin_ref[rows, :]
        for h in range(HEADS):
            one = queries[:, h * HEAD : (h + 1) * HEAD]
            q_ref[pl.ds(j * BLOCK, BLOCK), pl.ds(h * HEAD, HEAD)] = (
                one * cosine + turn(one) * sine
            ).astype(BF)
    next(ring)
    gather_og.late()

    for j in (0, 1):
        keys = SEQ // 2 * (j + 1)
        rows = pl.ds(j * BLOCK, BLOCK)

        def attend(h, carry):
            lanes = pl.ds(aligned(h, HEAD), HEAD)
            scores = dot(q_ref[rows, lanes], k_ref[:keys, :], 1, 1) * SCALE
            scores = causal(scores, pair[j] * BLOCK)
            top = jnp.max(scores, axis=1, keepdims=True)
            weights = jnp.exp(scores - top)
            total = jnp.sum(weights, axis=1, keepdims=True)
            lse_ref[j * HEADS + h] = top + jnp.log(total)
            probs = (weights * (1.0 / total)).astype(BF)
            attn_ref[rows, lanes] = dot(probs, v_ref[:keys, :]).astype(BF)
            return carry

        lax.fori_loop(0, HEADS, attend, 0)
        next(ring)

    net.take(near_ow, ow.at[:, pl.ds(aligned(at.sib, FEAT), FEAT)])
    other_rows = pl.ds(aligned(1 - at.core, FEAT), FEAT)
    net.take(far_ow, ow.at[other_rows, far_half])
    part_out[...] = dot(attn_ref[pl.ds(aligned(1 - at.row, BLOCK), BLOCK), :], ow[...]).astype(BF)
    part = net.send(part_out, part_in, at.N1)
    own = dot(attn_ref[pl.ds(aligned(at.row, BLOCK), BLOCK), :], ow[...])
    next(ring)
    net.take(part, part_in)
    mid = xs_ref[...].astype(F32) + own + part_in[...].astype(F32)
    mid_ref[...] = mid

    def place_n2(row, col, part):
        first = block_of(row, col) * BLOCK
        if part is None:
            return n2_all.at[pl.ds(pl.multiple_of(first, BLOCK), BLOCK), :]
        return n2_all.at[pl.ds(pl.multiple_of(first + part * 64, 64), 64), :]

    n2_all[my_rows, :] = (mid * rms(mid) * gain2).astype(BF)
    gather_n2 = Gather8(net, at, place_n2)
    gather_n2.start(place_n2(at.row, at.col, None))
    gather_og.end()
    next(ring)
    gather_n2.middle()
    drain(ring)
    gather_n2.late()
    net.take(near[0], gw.at[pl.ds(aligned(at.sib, FEAT), FEAT), :])
    net.take(near[1], uw.at[pl.ds(aligned(at.sib, FEAT), FEAT), :])
    net.take(near[2], dw.at[:, pl.ds(aligned(at.sib, FEAT), FEAT)])
    gather_n2.end()
    net.finish()

    @pl.when(chosen)
    def _():
        for core in (0, 1):
            for copy in slice_copies(core, 0, 5):
                copy.wait_send()


def vmem():
    return pl.BlockSpec(memory_space=pltpu.VMEM)


def anywhere():
    return pl.BlockSpec(memory_space=pl.ANY)


def run_forward(x, og, wqkv, wout, wg, wu, wd, gains, bias, cosine, sine):
    def out(shape, dtype):
        return jax.ShapeDtypeStruct(shape, dtype)

    outs = (
        out((BLOCK, MODEL), BF),
        out((SEQ, FEAT), BF),
        out((SEQ, MODEL), BF),
        out((SEQ, MODEL), BF),
        out((MODEL, QKV), BF),
        out((QCOLS, MODEL), BF),
        out((MODEL, PART), BF),
        out((MODEL, PART), BF),
        out((PART, MODEL), BF),
        out((2 * BLOCK, QCOLS), BF),
        out((SEQ, HEAD), BF),
        out((SEQ, HEAD), BF),
        out((2 * HEADS, BLOCK, 1), F32),
        out((2 * BLOCK, QCOLS), BF),
        out((BLOCK, MODEL), F32),
        out((8, MODEL), F32),
    )
    return pl.pallas_call(
        forward_kernel,
        out_shape=outs,
        in_specs=[vmem()] * 4 + [anywhere()] * 3 + [vmem()] * 4,
        out_specs=[vmem()] * len(outs),
        scratch_shapes=[
            pltpu.VMEM((SEQ, MODEL), BF),
            pltpu.VMEM((SEQ, MODEL), BF),
            pltpu.VMEM((BLOCK, MODEL), BF),
            pltpu.VMEM((BLOCK, MODEL), BF),
            pltpu.SemaphoreType.DMA((160,)),
            pltpu.SemaphoreType.DMA((160,)),
            pltpu.SemaphoreType.DMA((8,)),
        ],
        compiler_params=pltpu.CompilerParams(
            collective_id=0, has_side_effects=True, vmem_limit_bytes=VMEM_LIMIT
        ),
        cost_estimate=pl.CostEstimate(
            flops=8 * 10**9, bytes_accessed=60 * 10**6, transcendentals=2 * 10**6
        ),
        name="attention_forward",
    )(x, og, wqkv, wout, wg, wu, wd, gains, bias, cosine, sine)


class Reduce8:
    def __init__(self, net, at, own, other, sib_in, first_in, last_in, near_in, away_in):
        self.net, self.at, self.own, self.other, self.sib_in = net, at, own, other, sib_in
        self.first_in, self.last_in, self.near_in, self.away_in = first_in, last_in, near_in, away_in
        self.half = own.shape[1] // 2
        self.keys = {}

    def put(self, j, mine, theirs):
        self.own[j] = mine
        self.other[j] = theirs
        self.keys[j] = self.net.send(self.other.at[j], self.sib_in.at[j], self.at.S)

    def step(self, j):
        net, at, half = self.net, self.at, self.half
        net.take(self.keys[j], self.sib_in.at[j])
        total = self.own[j].astype(F32) + self.sib_in[j].astype(F32)
        if j == 0:
            self.own[j] = total.astype(BF)
            self.first = net.send(self.own.at[j, pl.ds(0, half)], self.first_in, at.N1)
            self.last = net.send(self.own.at[j, pl.ds(half, half)], self.last_in, at.N2)
        elif j == 1:
            net.take(self.last, self.last_in)
            self.own[j, :half] = total[:half].astype(BF)
            self.own[j, half:] = (total[half:] + self.last_in[...].astype(F32)).astype(BF)
            self.near = net.send(self.own.at[j], self.near_in, at.N1)
        elif j == 2:
            net.take(self.first, self.first_in)
            self.own[j, :half] = (total[:half] + self.first_in[...].astype(F32)).astype(BF)
            self.own[j, half:] = total[half:].astype(BF)
            self.away = net.send(self.own.at[j], self.away_in, at.N2)
        else:
            net.take(self.near, self.near_in)
            net.take(self.away, self.away_in)
            return total + self.near_in[...].astype(F32) + self.away_in[...].astype(F32)
        return None


def reduce8_scratch(rows, columns):
    return [
        pltpu.VMEM((4, rows, columns), BF),
        pltpu.VMEM((4, rows, columns), BF),
        pltpu.VMEM((4, rows, columns), BF),
        pltpu.VMEM((rows // 2, columns), BF),
        pltpu.VMEM((rows // 2, columns), BF),
        pltpu.VMEM((rows, columns), BF),
        pltpu.VMEM((rows, columns), BF),
    ]


def tiles_of(width, step):
    return [(first, min(step, width - first)) for first in range(0, width, step)]


def outer_sum(left, right, out):
    width = right.shape[1]
    height = left.shape[1] // 2

    def tile(lanes):
        for i in (0, 1):
            rows = pl.ds(i * height, height)
            out[rows, lanes] = dot(left[:, rows], right[:, lanes], 0, 0).astype(BF)

    def step(n, carry):
        tile(pl.ds(aligned(n, 256), 256))
        return carry

    lax.fori_loop(0, width // 256, step, 0)
    if width % 256:
        tile(pl.ds(width // 256 * 256, width % 256))


def ffn_kernel(
    n2,
    og,
    gw,
    uw,
    dw,
    mid_ref,
    dn2_ref,
    out_ref,
    grad_gate,
    grad_up,
    grad_down,
    hidden,
    d_gate,
    d_up,
    ffn,
    *rest,
):
    red_a, red_b, (send_sems, recv_sems) = rest[:7], rest[7:14], rest[14:]
    at = Place()
    net = Net(send_sems, recv_sems, at)
    at.meet((at.S, at.N1, at.N2))
    norms = Reduce8(net, at, *red_a)
    outs = Reduce8(net, at, *red_b)
    chips = ((at.row, 1 - at.hi), (1 - at.row, at.hi), (1 - at.row, 1 - at.hi), (at.row, at.hi))
    last_part = at.col == 3

    def tokens(j):
        row, hi = chips[j]
        first = 2 * hi + row * (6 - 4 * hi)
        return pl.ds(aligned(first, BLOCK), 256), at.core + row * (1 - 2 * at.core)

    for j in range(4):
        rows, place = tokens(j)
        for first, width in tiles_of(PART, 512):
            lanes = pl.ds(first, width)
            gate = dot(n2[rows, :], gw[:, lanes])
            up = dot(n2[rows, :], uw[:, lanes])
            d_hidden = dot(og[rows, :], dw[lanes, :], 1, 1)
            sig = jax.nn.sigmoid(gate)
            act = gate * sig
            d_act = d_hidden * up * sig * (1.0 + gate * (1.0 - sig))
            values = [act * up, d_act, d_hidden * act]
            if first == 0:
                lane = lax.broadcasted_iota(jnp.int32, (1, width), 1)
                fresh = jnp.logical_or(lane >= HEAD, jnp.logical_not(last_part))
                values = [jnp.where(fresh, value, 0.0) for value in values]
            for ref, value in zip((hidden, d_gate, d_up), values, strict=True):
                ref[rows, lanes] = value.astype(BF)
        own_rows = pl.ds(pl.multiple_of(rows.start + place * BLOCK, BLOCK), BLOCK)
        other_rows = pl.ds(pl.multiple_of(rows.start + (1 - place) * BLOCK, BLOCK), BLOCK)
        parts = [
            (dot(d_gate[r, :], gw[...], 1, 1) + dot(d_up[r, :], uw[...], 1, 1)).astype(BF)
            for r in (other_rows, own_rows)
        ]
        norms.put(j, parts[1], parts[0])
        if j:
            norms.step(j - 1)

    outer_sum(hidden, og, grad_down)

    for j in range(4):
        row, hi = chips[j]
        rows = pl.ds(aligned(row, SEQ // 2), SEQ // 2)
        lanes = pl.ds(aligned(hi, QCOLS), QCOLS)
        ffn[...] = dot(hidden[rows, :], dw[:, lanes])
        if j in (0, 3):
            mine = pl.ds(pl.multiple_of((at.block - 4 * at.row) * BLOCK, BLOCK), BLOCK)
            ffn[mine, :] += mid_ref[:, lanes]
        own = ffn[:, pl.ds(aligned(at.core, FEAT), FEAT)].astype(BF)
        outs.put(j, own, ffn[:, pl.ds(aligned(1 - at.core, FEAT), FEAT)].astype(BF))
        if j:
            outs.step(j - 1)
        if j == 1:
            dn2_ref[...] = norms.step(3)

    outer_sum(n2, d_gate, grad_gate)
    outer_sum(n2, d_up, grad_up)
    out_ref[...] = outs.step(3)
    net.finish()


def run_ffn(n2, og, gw, uw, dw, mid):
    def out(shape, dtype):
        return jax.ShapeDtypeStruct(shape, dtype)

    outs = (
        out((BLOCK, MODEL), F32),
        out((SEQ // 2, FEAT), F32),
        out((MODEL, PART), BF),
        out((MODEL, PART), BF),
        out((PART, MODEL), BF),
    )
    return pl.pallas_call(
        ffn_kernel,
        out_shape=outs,
        in_specs=[vmem()] * 6,
        out_specs=[vmem()] * len(outs),
        scratch_shapes=[pltpu.VMEM((SEQ, PART), BF)] * 3
        + [pltpu.VMEM((SEQ // 2, QCOLS), F32)]
        + reduce8_scratch(BLOCK, MODEL)
        + reduce8_scratch(SEQ // 2, FEAT)
        + [pltpu.SemaphoreType.DMA((32,)), pltpu.SemaphoreType.DMA((32,))],
        compiler_params=pltpu.CompilerParams(
            collective_id=1, has_side_effects=True, vmem_limit_bytes=VMEM_LIMIT
        ),
        cost_estimate=pl.CostEstimate(
            flops=29 * 10**9, bytes_accessed=60 * 10**6, transcendentals=2 * 10**6
        ),
        name="feed_forward",
    )(n2, og, gw, uw, dw, mid)


def backward_kernel(
    dn2_ref,
    mid_ref,
    og_ref,
    gains_all,
    xs_ref,
    n1c,
    attn_ref,
    q_ref,
    k_ref,
    v_ref,
    lse_ref,
    ow,
    qw,
    cos_ref,
    sin_ref,
    grad_in,
    grad_out,
    grad_qkv,
    sums_ref,
    bias_ref,
    attn_all,
    mid_cols,
    mid_pair,
    d_mid,
    d_attn,
    d_q,
    d_kv,
    kv_out,
    kv_in,
    d_qkv_all,
    part_out,
    part_in,
    gi_out,
    gi_in,
    send_sems,
    recv_sems,
):
    at = Place()
    net = Net(send_sems, recv_sems, at)
    at.meet((at.S, at.O, at.OS, at.N1, at.N2, at.N1S, at.N2S))
    peers = ((at.S, at.sib), (at.O, at.far), (at.OS, at.sibfar))
    pair = (at.col, 7 - at.col)

    def rows_at(block):
        return pl.ds(aligned(block, BLOCK), BLOCK)

    def cols_at(col):
        return pl.ds(aligned(col, FEAT), FEAT)

    class GatherCol:
        def __init__(self, array):
            self.array = array

        def rows(self, col, j):
            return self.array.at[rows_at(col + j * (7 - 2 * col)), :]

        def start(self):
            self.far = [net.send(self.rows(at.col, j), self.rows(at.col, j), at.O) for j in (0, 1)]
            self.sib = [net.send(self.rows(at.col, j), self.rows(at.col, j), at.S) for j in (0, 1)]

        def middle(self):
            self.onward = []
            for j in (0, 1):
                net.take(self.far[j], self.rows(at.far, j))
                self.onward.append(net.send(self.rows(at.far, j), self.rows(at.far, j), at.S))

        def end(self):
            for j in (0, 1):
                net.take(self.sib[j], self.rows(at.sib, j))
                net.take(self.onward[j], self.rows(at.sibfar, j))

    gather_attn = GatherCol(attn_all)
    for j in (0, 1):
        attn_all[rows_at(pair[j]), :] = attn_ref[pl.ds(j * BLOCK, BLOCK), :]

    gain1, gain2 = gains_all[0:1, :], gains_all[1:2, :]
    mid = mid_ref[...]
    scale = rms(mid)
    unit = mid * scale
    d_normed = dn2_ref[...]
    sums_ref[...] = jnp.zeros_like(sums_ref)
    sums_ref[1:2, :] = jnp.sum(d_normed * unit, axis=0, keepdims=True)
    bent = d_normed * gain2
    d_mid[...] = og_ref[rows_at(at.block), :].astype(F32) + scale * (
        bent - unit * jnp.mean(bent * unit, axis=1, keepdims=True)
    )
    mid_pair[at.row] = d_mid[...].astype(BF)
    to_pair = net.send(mid_pair.at[at.row], mid_pair.at[at.row], at.N1)
    mid_cols[rows_at(at.block), :] = d_mid[:, cols_at(at.col)].astype(BF)
    spread = []
    others = (
        (at.S, at.row, at.sib),
        (at.N1, 1 - at.row, at.col),
        (at.N1S, 1 - at.row, at.sib),
        (at.O, at.row, at.far),
        (at.OS, at.row, at.sibfar),
        (at.N2, 1 - at.row, at.far),
        (at.N2S, 1 - at.row, at.sibfar),
    )
    for device, row, col in others:
        spread.append(
            net.send(
                mid_pair.at[at.row, :, cols_at(col)], mid_cols.at[rows_at(at.block), :], device
            )
        )
    gather_attn.start()
    net.take(to_pair, mid_pair.at[1 - at.row])
    for j in (0, 1):
        d_attn[pl.ds(j * BLOCK, BLOCK), :] = dot(mid_pair[j], ow[...], 1, 1).astype(BF)
    d_kv[...] = jnp.zeros_like(d_kv)

    for j in (0, 1):
        keys = SEQ // 2 * (j + 1)
        rows = pl.ds(j * BLOCK, BLOCK)

        def back(h, carry):
            lanes = pl.ds(aligned(h, HEAD), HEAD)
            queries, d_out = q_ref[rows, lanes], d_attn[rows, lanes]
            scores = dot(queries, k_ref[:keys, :], 1, 1) * SCALE
            scores = causal(scores, pair[j] * BLOCK)
            probs = jnp.exp(scores - lse_ref[j * HEADS + h])
            d_probs = dot(d_out, v_ref[:keys, :], 1, 1)
            inner = jnp.sum(probs * d_probs, axis=1, keepdims=True)
            d_scores = (probs * (d_probs - inner) * SCALE).astype(BF)
            d_q[rows, lanes] = dot(d_scores, k_ref[:keys, :])
            d_kv[:keys, :HEAD] += dot(d_scores, queries, 0, 0)
            d_kv[:keys, HEAD:] += dot(probs.astype(BF), d_out, 0, 0)
            return carry

        lax.fori_loop(0, HEADS, back, 0)
    gather_attn.middle()

    kv_out[...] = d_kv[...].astype(BF)
    kv_keys = [
        [
            net.send(kv_out.at[rows_at(col + j * (7 - 2 * col)), :], kv_in.at[i, j], device)
            for j in (0, 1)
        ]
        for i, (device, col) in enumerate(peers)
    ]
    cosines = [cos_ref[rows_at(pair[j]), :] for j in (0, 1)]
    sines = [sin_ref[rows_at(pair[j]), :] for j in (0, 1)]
    for j in (0, 1):
        for h in range(HEADS):
            one = d_q[pl.ds(j * BLOCK, BLOCK), pl.ds(h * HEAD, HEAD)]
            d_qkv_all[rows_at(pair[j]), pl.ds(h * HEAD, HEAD)] = (
                one * cosines[j] - turn(one) * sines[j]
            ).astype(BF)
    gather_attn.end()
    for key, (_, row, col) in zip(spread, others, strict=True):
        net.take(key, mid_cols.at[rows_at(block_of(row, col)), :])
    grad_out[...] = dot(attn_all[...], mid_cols[...], 0, 0).astype(BF)
    for j in (0, 1):
        total = d_kv[rows_at(pair[j]), :]
        for i in range(3):
            net.take(kv_keys[i][j], kv_in.at[i, j])
            total = total + kv_in[i, j].astype(F32)
        key = total[:, :HEAD]
        d_qkv_all[rows_at(pair[j]), pl.ds(QCOLS, HEAD)] = (
            key * cosines[j] - turn(key) * sines[j]
        ).astype(BF)
        d_qkv_all[rows_at(pair[j]), pl.ds(QCOLS + HEAD, HEAD)] = total[:, HEAD:].astype(BF)
    gather_qkv = GatherCol(d_qkv_all)
    gather_qkv.start()

    part_out[...] = dot(d_qkv_all[rows_at(block_of(1 - at.row, at.col)), :], qw[...], 1, 1).astype(BF)
    part = net.send(part_out, part_in, at.N1)
    d_normed = dot(d_qkv_all[rows_at(at.block), :], qw[...], 1, 1)
    net.take(part, part_in)
    d_normed = d_normed + part_in[...].astype(F32)
    values = xs_ref[...].astype(F32)
    scale = rms(values)
    unit = values * scale
    sums_ref[0:1, :] = jnp.sum(d_normed * unit, axis=0, keepdims=True)
    bent = d_normed * gain1
    total = d_mid[...] + scale * (bent - unit * jnp.mean(bent * unit, axis=1, keepdims=True))
    gi_out[...] = total.astype(BF)
    half_rows = pl.ds(pl.multiple_of((at.block - 4 * at.row) * BLOCK, BLOCK), BLOCK)
    gi_keys = [
        net.send(gi_out.at[:, cols_at(col)], gi_in.at[half_rows, :], device)
        for device, col in peers
    ]
    gi_in[half_rows, :] = gi_out[:, cols_at(at.col)]
    gather_qkv.middle()
    gather_qkv.end()
    grad_qkv[...] = dot(n1c[...], d_qkv_all[...], 0, 0).astype(BF)
    ones = jnp.ones((8, SEQ), BF)
    bias_ref[...] = dot(ones, d_qkv_all[...])
    for key, (_, col) in zip(gi_keys, peers, strict=True):
        offset = block_of(at.row, col) - 4 * at.row
        net.take(key, gi_in.at[pl.ds(pl.multiple_of(offset * BLOCK, BLOCK), BLOCK), :])
    grad_in[...] = gi_in[...].astype(F32)
    net.finish()


def run_backward(*args):
    def out(shape, dtype):
        return jax.ShapeDtypeStruct(shape, dtype)

    outs = (
        out((SEQ // 2, FEAT), F32),
        out((QCOLS, FEAT), BF),
        out((FEAT, QKV), BF),
        out((8, MODEL), F32),
        out((8, QKV), F32),
    )
    return pl.pallas_call(
        backward_kernel,
        out_shape=outs,
        in_specs=[vmem()] * len(args),
        out_specs=[vmem()] * len(outs),
        scratch_shapes=[
            pltpu.VMEM((SEQ, QCOLS), BF),
            pltpu.VMEM((SEQ, FEAT), BF),
            pltpu.VMEM((2, BLOCK, MODEL), BF),
            pltpu.VMEM((BLOCK, MODEL), F32),
            pltpu.VMEM((2 * BLOCK, QCOLS), BF),
            pltpu.VMEM((2 * BLOCK, QCOLS), F32),
            pltpu.VMEM((SEQ, 2 * HEAD), F32),
            pltpu.VMEM((SEQ, 2 * HEAD), BF),
            pltpu.VMEM((3, 2, BLOCK, 2 * HEAD), BF),
            pltpu.VMEM((SEQ, QKV), BF),
            pltpu.VMEM((BLOCK, MODEL), BF),
            pltpu.VMEM((BLOCK, MODEL), BF),
            pltpu.VMEM((BLOCK, MODEL), BF),
            pltpu.VMEM((SEQ // 2, FEAT), BF),
            pltpu.SemaphoreType.DMA((40,)),
            pltpu.SemaphoreType.DMA((40,)),
        ],
        compiler_params=pltpu.CompilerParams(
            collective_id=2, has_side_effects=True, vmem_limit_bytes=VMEM_LIMIT
        ),
        cost_estimate=pl.CostEstimate(
            flops=10 * 10**9, bytes_accessed=40 * 10**6, transcendentals=2 * 10**6
        ),
        name="attention_backward",
    )(*args)


def rope_tables(count):
    places = jnp.arange(count, dtype=jnp.int32).astype(F32)
    inverse = 1.0 / THETA ** (jnp.arange(0, HEAD, 2).astype(F32) / HEAD)
    angles = places[:, None] * inverse[None, :]
    cosine, sine = jnp.cos(angles), jnp.sin(angles)
    return jnp.concatenate([cosine, cosine], axis=-1), jnp.concatenate([-sine, sine], axis=-1)


def body(
    layer_input,
    gain_attn,
    w_query,
    w_key,
    w_value,
    b_query,
    b_key,
    b_value,
    w_out,
    gain_ffn,
    w_gate,
    w_up,
    w_down,
    out_grad,
):
    n_dp = lax.axis_size("dp")
    feat, part, units, query_cols = FEAT, PART, UNITS, QCOLS

    cosine, sine = rope_tables(SEQ)
    w_qkv = jnp.concatenate([w_query, w_key, w_value], axis=1)
    bias = jnp.concatenate([b_query, b_key, b_value]).astype(F32)[None]
    gains = jnp.zeros((8, FEAT), F32).at[0].set(gain_attn.astype(F32)).at[1].set(gain_ffn.astype(F32))
    (
        xs,
        normed1_cols,
        grads_all,
        normed2_all,
        qkv_w,
        out_w,
        gate_w,
        up_w,
        down_w,
        queries,
        key,
        value,
        lse,
        attn,
        mid,
        gains_all,
    ) = run_forward(
        layer_input, out_grad, w_qkv, w_out, w_gate, w_up, w_down, gains, bias, cosine, sine
    )
    dn2, layer_output, grad_gate, grad_up, grad_down = run_ffn(
        normed2_all, grads_all, gate_w, up_w, down_w, mid
    )
    grad_input, grad_out, grad_qkv, sums, grad_bias = run_backward(
        dn2,
        mid,
        grads_all,
        gains_all,
        xs,
        normed1_cols,
        attn,
        queries,
        key,
        value,
        lse,
        out_w,
        qkv_w,
        cosine,
        sine,
    )

    def sum_dp(grad):
        rows = grad.shape[1] // n_dp
        sliced = grad.reshape(4, n_dp, rows, -1).transpose(1, 0, 2, 3)
        mine = lax.psum_scatter(sliced, "dp", scatter_dimension=0, tiled=True)[0]
        return lax.all_to_all(mine, "col", 0, 0, tiled=True)

    def spread(grad):
        return lax.all_gather(grad, "dp", axis=0, tiled=True).astype(F32)

    grad_down = sum_dp(grad_down.reshape(part, 4, feat).transpose(1, 0, 2))
    grad_gate = sum_dp(grad_gate.reshape(4, feat, part))
    grad_up = sum_dp(grad_up.reshape(4, feat, part))

    def sum_all(grad):
        mine = lax.psum_scatter(grad.astype(BF), "dp", scatter_dimension=0, tiled=True)
        return spread(mine)

    grad_qkv = sum_all(grad_qkv)
    grad_out = sum_all(grad_out)
    gains = lax.psum(sums[:2], ("dp", "row", "col"))
    gains = lax.dynamic_slice_in_dim(gains, lax.axis_index("col") * feat, feat, 1)
    grad_bias = lax.psum(grad_bias[0], "dp")

    def join(grad):
        joined = jnp.concatenate([grad[0], grad[1], grad[2], grad[3][:, HEAD:]], axis=1)
        return spread(joined)

    def join_down(grad):
        gathered = lax.all_gather(grad, "dp", axis=1, tiled=True)
        joined = jnp.concatenate([gathered[0], gathered[1], gathered[2], gathered[3][HEAD:]])
        return joined.astype(F32)

    return (
        layer_output,
        grad_input,
        gains[0],
        grad_qkv[:, :query_cols],
        grad_qkv[:, query_cols : query_cols + HEAD],
        grad_qkv[:, query_cols + HEAD :],
        grad_bias[:query_cols],
        grad_bias[query_cols : query_cols + HEAD],
        grad_bias[query_cols + HEAD :],
        grad_out,
        gains[1],
        join(grad_gate),
        join(grad_up),
        join_down(grad_down),
    )


def solution(mesh):
    in_specs = (
        P(("dp", "row"), "col"),
        P("col"),
        P("col", "row"),
        P("col", "row"),
        P("col", "row"),
        P("row"),
        P("row"),
        P("row"),
        P("row", "col"),
        P("col"),
        P("col", "row"),
        P("col", "row"),
        P("row", "col"),
        P(("dp", "row"), "col"),
    )
    out_specs = (
        P(("dp", "row"), "col"),
        P(("dp", "row"), "col"),
        P("col"),
        P("col", "row"),
        P("col", "row"),
        P("col", "row"),
        P("row"),
        P("row"),
        P("row"),
        P("row", "col"),
        P("col"),
        P("col", "row"),
        P("col", "row"),
        P("row", "col"),
    )
    return jax.shard_map(body, mesh=mesh, in_specs=in_specs, out_specs=out_specs, check_vma=False)
```

time: 1190 us -> 775 us (0.65)
  waiting for transfers between devices: 593 us -> 262 us
  Pallas kernels: 0 us -> 253 us
  matrix products: 121 us -> 0 us
  local copies, waits for them, and re-layouts: 110 us -> 27.3 us
  blocking collectives: 247 us -> 183 us
  other arithmetic: 77.8 us -> 28.9 us
  starting transfers between devices: 19.1 us -> 0.73 us
    pallas_call x0 -> x3, Pallas kernels: none -> 253 us  [the longest x1 99.3 us: run_forward(): pl.pallas_call(forward_kernel, out_shape=outs, in_specs=[vmem()] * 4 + [a...]
    all_gather x10 -> x1, waiting for transfers between devices: 216 us -> 24.6 us  [join_down(): gathered = lax.all_gather(grad, 'dp', axis=1, tiled=True)]
    dot_general x22 -> x0, matrix products: 121 us -> none  [the longest x16 83.4 us: dot(): lax.dot_general(left, right, (((left_dim,), (right_dim,)), ((), ())), pre...]
    reduce_scatter x5 -> x0, waiting for transfers between devices: 106 us -> none  [the longest x2 72.9 us: shards_sum(): lax.psum_scatter(partial.astype(BF), ('row', 'col'), scatter_dimension=0,...]
    all_gather x4 -> x0, blocking collectives: 63.1 us -> none  [the longest x2 49.7 us: gather_dp(): return lax.all_gather(flip(mine, 2), 'dp', axis=0, tiled=True)]
    unnamed x25 -> x13, waiting for transfers between devices: 184 us -> 155 us
    ppermute x15 -> x0, waiting for transfers between devices: 17.1 us -> none  [flip(): return lax.ppermute(values, 'col', [(i, i ^ bit) for i in range(count)])]
    another operation x10 -> x0, other arithmetic: 15.5 us -> none  [the longest x5 12.2 us: by_source(): stacked = jnp.stack(blocks)]
  transfers between devices with their start and end apart: 37 -> 8, of which waited for: 20 -> 7; matrix products, arithmetic and copies ran while one was open for 20% -> 4% of each run, Pallas kernels for 0% -> 10%
where the time goes in v2:
time: 775 us; the launch traced here: 769 us
  waiting for transfers between devices  262 us (34%)
  Pallas kernels  253 us (33%)
  blocking collectives  183 us (24%)
  other arithmetic  28.9 us (4%)
  local copies, waits for them, and re-layouts  27.3 us (4%)
  between operations  14.5 us (2%)
    unnamed x13, waiting for transfers between devices  155 us
    pallas_call x1, Pallas kernels, run_forward(): pl.pallas_call(forward_kernel, out_shape=outs, in_specs=[vmem()] * 4 + [a...  99.3 us
    all_gather x2, waiting for transfers between devices, spread(): return lax.all_gather(grad, 'dp', axis=0, tiled=True).astype(F32)  82.2 us
    pallas_call x1, Pallas kernels, run_ffn(): pl.pallas_call(ffn_kernel, out_shape=outs, in_specs=[vmem()] * 6, out_spe...  78.6 us
    pallas_call x1, Pallas kernels, run_backward(): pl.pallas_call(backward_kernel, out_shape=outs, in_specs=[vmem()] * len(a...  75.2 us
    psum x1, blocking collectives, body(): gains = lax.psum(sums[:2], ('dp', 'row', 'col'))  64.3 us
    all_gather x2, blocking collectives, spread(): return lax.all_gather(grad, 'dp', axis=0, tiled=True).astype(F32)  46.5 us
    psum x1, blocking collectives, body(): grad_bias = lax.psum(grad_bias[0], 'dp')  38.2 us
  transfers between devices with their start and end apart: 8, of which 7 were waited for; matrix products, arithmetic and copies ran while one was open for 4% of the time, Pallas kernels for 10%

profile of v2, /device:TPU:0, one launch (start us, length us, event | category | flops | bytes accessed | tf_op | source)
XLA Modules:
  0.0 769.3 jit_solution(3235811260451372300)
XLA Ops:
  9.4 1.9 fusion
  11.3 1.3 pad_maximum_fusion.1
  14.9 99.3 %attention_forward.1 = (bf16[128,1536]{1,0:T(8,128)(2,1)}, bf16[1024,384]{1,0:T(8,128)(2,1)}, bf16[1024,1536]{1,0:T(8,128)(2,1)}, bf16[1024,1536]{1,0:T(8,128)(2...) custom-call(bf16[512,384]{1,0:T(8,128)(2,1)} %x_ref.1, ...), custom_call_target="tpu_custom_call" | custom-call | flops 8000000000 | bytes 60000000 | tf_op jit(solution)/shard_map/attention_forward/pallas_call | solution.py:528
  114.2 78.6 %feed_forward.1 = (f32[128,1536]{1,0:T(8,128)}, f32[512,384]{1,0:T(8,128)}, bf16[1536,1152]{1,0:T(8,128)(2,1)}, bf16[1536,1152]{1,0:T(8,128)(2,1)}, bf16[1152,1536]{1,0:T(8,128)(2,1)}) custom-call(bf16[1024,1536]{1,0:T(8,128)(2,1)} %get-tuple-element.64.n2, bf16[1024,1536]{1,0:T(8,128)(2,1)} %get-tuple-element.65.og.og_ref, ...), custom_call_target="tpu_custom_call" | custom-call | flops 28999999488 | bytes 60000000 | tf_op jit(solution)/shard_map/feed_forward/pallas_call | solution.py:716
  192.8 4.1 copy.42
  197.0 1.9 copy-done.1
  199.0 2.1 copy.43
  201.1 2.6 copy-done
  203.7 2.1 copy.44
  206.2 75.2 %attention_backward.1 = (f32[512,384]{1,0:T(8,128)}, bf16[768,384]{1,0:T(8,128)(2,1)}, bf16[384,1024]{1,0:T(8,128)(2,1)}, f32[8,1536]{1,0:T(8,128)}, f32[8,1024]{1,0:T(8,128)}) custom-call(f32[128,1536]{1,0:T(8,128)} %get-tuple-element.71.dn2_ref, f32[128,1536]{1,0:T(8,128)} %get-tuple-element.69.mid_ref, bf16[1024,1536]{1,0:T(8,128)(2,1)} %get-tuple-element.65.og.og_ref, ...), custom_call_target="tpu_custom_call" | custom-call | flops 10000000000 | bytes 40000000 | tf_op jit(solution)/shard_map/attention_backward/pallas_call | solution.py:943
  282.7 9.6 %all-reduce.8.cloned.1.call-done = bf16[16,4,72,384]{3,2,0,1:T(8,128)(2,1)} async-done(((bf16[16,4,72,384]{3,2,0,1:T(8,128)(2,1)}), bf16[16,4,72,384]{3,2,0,1:T(8,128)(2,1)}) %all-reduce.8.cloned.1.call-update) | async-done | bytes 3538960
  292.3 1.6 dynamic-slice_bitcast_fusion
  294.0 11.3 %all_to_all.15 = bf16[4,72,384]{2,1,0:T(8,128)(2,1)} all-to-all(bf16[4,72,384]{2,1,0:T(8,128)(2,1)S(1)} %dynamic-slice_bitcast_fusion), channel_id=1, replica_groups=mesh['dp'=16,'row'=2,'col'=4] {'col'}, dimensions={0} | all-to-all | bytes 442368 | tf_op jit(solution)/shard_map/all_to_all | solution.py:1052
  305.3 67.0 %reduce-scatter.20.cloned.1.call-done = bf16[1,4,24,1152]{3,2,1,0:T(8,128)(2,1)} async-done(((bf16[16,4,24,1152]{3,2,1,0:T(8,128)(2,1)}), bf16[1,4,24,1152]{3,2,1,0:T(8,128)(2,1)}) %reduce-scatter.20.cloned.1.call-update) | async-done | bytes 221200
  372.3 11.3 %all_to_all.16 = bf16[4,24,1152]{2,1,0:T(8,128)(2,1)S(1)} all-to-all(bf16[4,24,1152]{2,1,0:T(8,128)(2,1)} %bitcast.59), channel_id=1, replica_groups=mesh['dp'=16,'row'=2,'col'=4] {'col'}, dimensions={0} | all-to-all | bytes 442368 | tf_op jit(solution)/shard_map/all_to_all | solution.py:1052
  384.5 67.8 %reduce-scatter.18.cloned.1.call-done = bf16[1,4,24,1152]{3,2,1,0:T(8,128)(2,1)} async-done(((bf16[16,4,24,1152]{3,2,1,0:T(8,128)(2,1)}), bf16[1,4,24,1152]{3,2,1,0:T(8,128)(2,1)}) %reduce-scatter.18.cloned.1.call-update) | async-done | bytes 221200
  452.3 11.4 %all_to_all.17 = bf16[4,24,1152]{2,1,0:T(8,128)(2,1)S(1)} all-to-all(bf16[4,24,1152]{2,1,0:T(8,128)(2,1)} %bitcast.58), channel_id=1, replica_groups=mesh['dp'=16,'row'=2,'col'=4] {'col'}, dimensions={0} | all-to-all | bytes 442368 | tf_op jit(solution)/shard_map/all_to_all | solution.py:1052
  466.0 64.3 %psum.14 = f32[2,1536]{1,0:T(2,128)S(1)} all-reduce(f32[2,1536]{1,0:T(2,128)S(1)} %slice.106), channel_id=1, replica_groups=mesh['dp'=16,'row'=2,'col'=4] {'dp','row','col'}, use_global_device_ids=true, to_apply=%region_0.0 | all-reduce | flops 3072 | bytes 24576 | tf_op jit(solution)/shard_map/psum | solution.py:1067
  531.0 38.2 %psum.15 = f32[1024]{0:T(1024)S(1)} all-reduce(f32[1024]{0:T(1024)S(1)} %bitcast.60), channel_id=1, replica_groups=mesh['dp'=16,'row'=2,'col'=4] {'dp'}, use_global_device_ids=true, to_apply=%region_2.0 | all-reduce | flops 1024 | bytes 8192 | tf_op jit(solution)/shard_map/psum | solution.py:1069
  569.7 21.8 %all_gather.16 = bf16[768,384]{1,0:T(8,128)(2,1)S(1)} all-gather(bf16[48,384]{1,0:T(8,128)(2,1)} %reduce-scatter.16.cloned.1.call-done), channel_id=1, replica_groups=mesh['dp'=16,'row'=2,'col'=4] {'dp'}, dimensions={0}, use_global_device_ids=true | all-gather | bytes 626688 | tf_op jit(solution)/shard_map/all_gather | solution.py:1055
  591.5 1.1 convert_element_type.57
  592.6 9.8 %reduce-scatter.14.cloned.1.call-done = bf16[24,1024]{1,0:T(8,128)(2,1)} async-done(((bf16[384,1024]{1,0:T(8,128)(2,1)}), bf16[24,1024]{1,0:T(8,128)(2,1)}) %reduce-scatter.14.cloned.1.call-update) | async-done | bytes 49168
  602.4 24.6 %all_gather.15 = bf16[384,1024]{1,0:T(8,128)(2,1)S(1)} all-gather(bf16[24,1024]{1,0:T(8,128)(2,1)} %reduce-scatter.14.cloned.1.call-done), channel_id=1, replica_groups=mesh['dp'=16,'row'=2,'col'=4] {'dp'}, dimensions={0}, use_global_device_ids=true | all-gather | bytes 835584 | tf_op jit(solution)/shard_map/all_gather | solution.py:1055
  627.0 1.1 slice.131
  628.9 24.6 %all-gather.8.cloned.1.call-done = bf16[4,1152,384]{2,1,0:T(8,128)(2,1)} async-done(((bf16[4,72,384]{2,1,0:T(8,128)(2,1)}), bf16[4,1152,384]{2,1,0:T(8,128)(2,1)}) %all-gather.8.cloned.1.call-update) | async-done | bytes 3538960 | tf_op jit(solution)/shard_map/all_gather | solution.py:1076
  653.4 1.2 slice_bitcast_fusion.3
  654.7 2.0 slice_bitcast_fusion.2
  656.6 11.0 %maximum_convert_fusion = f32[4480,384]{1,0:T(8,128)} fusion(bf16[1024,384]{1,0:T(8,128)(2,1)S(1)} %slice_bitcast_fusion.3, bf16[1152,384]{1,0:T(8,128)(2,1)S(1)} %get-tuple-element.93, bf16[1152,384]{1,0:T(8,128)(2,1)S(1)} %get-tuple-element.94, bf16[1152,384]{1,0:T(8,128)(2,1)S(1)} %get-tuple-element.92), kind=kLoop, calls=%fused_computation.3 | loop fusion | flops 13762560 | bytes 10321920 | tf_op jit(solution)/shard_map/convert_element_type | solution.py:1078
  667.6 36.7 %all-gather.6.cloned.1.call-done = bf16[384,4480]{1,0:T(8,128)(2,1)} async-done(((bf16[24,4480]{1,0:T(8,128)(2,1)}), bf16[384,4480]{1,0:T(8,128)(2,1)}) %all-gather.6.cloned.1.call-update) | async-done | bytes 3440656 | tf_op jit(solution)/shard_map/all_gather | solution.py:1055
  704.4 5.3 convert_element_type.59
  709.7 45.5 %all-gather.4.cloned.1.call-done = bf16[384,4480]{1,0:T(8,128)(2,1)} async-done(((bf16[24,4480]{1,0:T(8,128)(2,1)}), bf16[384,4480]{1,0:T(8,128)(2,1)}) %all-gather.4.cloned.1.call-update) | async-done | bytes 3440656 | tf_op jit(solution)/shard_map/all_gather | solution.py:1055
  755.2 5.3 convert_element_type.58
  (62 shorter events, 13.1 us)
Async XLA Ops:
  7.2 5.5 copy-start.4
  7.2 5.4 copy-start.6
  7.2 5.4 copy-start.5
  7.2 6.4 copy-start.10
  7.2 6.4 copy-start.9
  7.2 285.1 %all-reduce.8.cloned.1.call-start = ((), (), s32[]{:S(2)}) async-start(), calls=%async_computation.10 | async-start | bytes 7077888
  14.3 0.6 copy-start.7
  197.0 2.0 copy-start.1
  197.0 175.3 %reduce-scatter.20.cloned.1.call-start = ((), (), s32[]{:S(2)}) async-start(), calls=%async_computation.14 | async-start | bytes 3760128
  201.0 2.6 copy-start
  201.1 251.2 %reduce-scatter.18.cloned.1.call-start = ((), (), s32[]{:S(2)}) async-start(), calls=%async_computation.13 | async-start | bytes 3760128
  205.8 363.9 %reduce-scatter.16.cloned.1.call-start = ((), (), s32[]{:S(2)}) async-start(), calls=%async_computation.12 | async-start | bytes 626688
  206.2 75.9 %copy-start.11 = (u32[128]{0:T(128)S(1)}, u32[128]{0:T(128)}, u32[]{:S(2)}) copy-start(u32[128]{0:T(128)} %constant.79) | copy-start | bytes 1540
  281.5 320.9 %reduce-scatter.14.cloned.1.call-start = ((), (), s32[]{:S(2)}) async-start(), calls=%async_computation.11 | async-start | bytes 835584
  282.1 371.3 %all-gather.8.cloned.1.call-start = ((), (), s32[]{:S(2)}) async-start(), calls=%async_computation.9 | async-start | bytes 3760128 | tf_op jit(solution)/shard_map/all_gather | solution.py:1076
  305.2 399.1 %all-gather.6.cloned.1.call-start = ((), (), s32[]{:S(2)}) async-start(), calls=%async_computation.8 | async-start | bytes 3655680 | tf_op jit(solution)/shard_map/all_gather | solution.py:1055
  384.4 370.8 %all-gather.4.cloned.1.call-start = ((), (), s32[]{:S(2)}) async-start(), calls=%async_computation.7 | async-start | bytes 3655680 | tf_op jit(solution)/shard_map/all_gather | solution.py:1055
  569.1 85.5 %copy-start.8 = (f32[1024]{0:T(1024)}, f32[1024]{0:T(1024)S(1)}, u32[]{:S(2)}) copy-start(f32[1024]{0:T(1024)S(1)} %psum.15) | copy-start | bytes 12292
  709.7 50.8 %copy-start.2 = (f32[512,384]{1,0:T(8,128)S(1)}, f32[512,384]{1,0:T(8,128)}, u32[]{:S(2)}) copy-start(f32[512,384]{1,0:T(8,128)} %get-tuple-element.126) | copy-start | bytes 2359300
  709.7 51.7 %copy-start.3 = (f32[512,384]{1,0:T(8,128)S(1)}, f32[512,384]{1,0:T(8,128)}, u32[]{:S(2)}) copy-start(f32[512,384]{1,0:T(8,128)} %get-tuple-element.127) | copy-start | bytes 2359300
Sparse Core Ops, SparseCore 0:
  197.1 95.1 all-reduce.7
  296.7 75.6 reduce-scatter.19
  376.6 75.5 reduce-scatter.17
  455.7 71.1 reduce-scatter.15
  530.2 72.1 reduce-scatter.13
  604.6 48.7 all-gather.7
  656.4 47.9 all-gather.5
  707.3 47.8 all-gather.3

commit v3 on v2

--- a/solution.py
+++ b/solution.py
@@ -66,6 +66,7 @@
             return {"dp": lax.rem(z + 4, 4) * 4 + lax.rem(y + 4, 4)}
 
         self.YP, self.YM = dp_at(self.z, self.y + 1), dp_at(self.z, self.y - 1)
+        self.Y2, self.Z2 = dp_at(self.z, self.y + 2), dp_at(self.z + 2, self.y)
         self.ZP, self.ZM = dp_at(self.z + 1, self.y), dp_at(self.z - 1, self.y)
 
     def meet(self, partners):
@@ -629,8 +630,7 @@
     mid_ref,
     dn2_ref,
     out_ref,
-    grad_gate,
-    grad_up,
+    grad_gu,
     grad_down,
     hidden,
     d_gate,
@@ -696,8 +696,8 @@
         if j == 1:
             dn2_ref[...] = norms.step(3)
 
-    outer_sum(n2, d_gate, grad_gate)
-    outer_sum(n2, d_up, grad_up)
+    outer_sum(n2, d_gate, grad_gu.at[0])
+    outer_sum(n2, d_up, grad_gu.at[1])
     out_ref[...] = outs.step(3)
     net.finish()
 
@@ -709,8 +709,7 @@
     outs = (
         out((BLOCK, MODEL), F32),
         out((SEQ // 2, FEAT), F32),
-        out((MODEL, PART), BF),
-        out((MODEL, PART), BF),
+        out((2, MODEL, PART), BF),
         out((PART, MODEL), BF),
     )
     return pl.pallas_call(
@@ -733,6 +732,154 @@
     )(n2, og, gw, uw, dw, mid)
 
 
+def add_up(out, terms):
+    lead = out.shape[:-2]
+    if not lead:
+        total = terms[0][...].astype(F32)
+        for term in terms[1:]:
+            total = total + term[...].astype(F32)
+        out[...] = total.astype(out.dtype)
+        return
+    count = 1
+    for size in lead:
+        count *= size
+
+    def step(i, carry):
+        index = []
+        for size in reversed(lead):
+            index.insert(0, i % size)
+            i = i // size
+        index = tuple(index)
+        total = terms[0].at[index][...].astype(F32)
+        for term in terms[1:]:
+            total = total + term.at[index][...].astype(F32)
+        out.at[index][...] = total.astype(out.dtype)
+        return carry
+
+    lax.fori_loop(0, count, step, 0)
+
+
+class RingItem:
+    def __init__(self, net, sides, place, part, way, bufs, own):
+        self.net, self.part, self.own = net, part, own
+        self.relay, self.staged, self.from_last, self.from_next = bufs
+        self.onward, self.back = (sides[0], sides[1]) if way == 0 else (sides[1], sides[0])
+        step = 1 - 2 * way
+        self.here, self.next, self.across, self.last = (
+            lax.rem(place + 4 + step * i, 4) for i in (0, 1, 2, 3)
+        )
+
+    def start(self):
+        self.k_relay = self.net.send(self.part(self.across), self.relay, self.onward)
+
+    def direct(self):
+        self.k_next = self.net.send(self.part(self.last), self.from_next, self.back)
+
+    def middle(self):
+        self.net.take(self.k_relay, self.relay)
+        add_up(self.staged, [self.part(self.next), self.relay])
+        self.k_last = self.net.send(self.staged, self.from_last, self.onward)
+
+    def end(self):
+        self.net.take(self.k_next, self.from_next)
+        self.net.take(self.k_last, self.from_last)
+        add_up(self.own, [self.part(self.here), self.from_next, self.from_last])
+
+
+def begin(items):
+    for item in items:
+        item.start()
+    for item in items:
+        item.direct()
+
+
+LEFT, RIGHT = pl.ds(0, QCOLS), pl.ds(QCOLS, QCOLS)
+FFN_FIRST = (((2, 2, 48, PART), (2, 80, QCOLS)), ((2, 2, 48, PART), (144, QCOLS)))
+FFN_LAST = (((2, 48, PART), (80, QCOLS)), ((2, 48, PART), (80, QCOLS)))
+SMALL_FIRST = (((2, 48, 512),), ((2, 48, FEAT),))
+SMALL_LAST = (((48, 512),), ((48, FEAT),))
+
+
+def down_rows(k):
+    return pl.ds(pl.multiple_of(72 * k - 8 * (k % 2), 16), 80)
+
+
+def ring_scratch(first, last):
+    scratch = []
+    for i in (0, 1):
+        for dims in first[i]:
+            scratch += [pltpu.VMEM(dims, BF)] * 8
+            scratch.append(pltpu.VMEM((2,) + dims, BF))
+        for dims in last[i]:
+            scratch += [pltpu.VMEM(dims, BF)] * 4
+    return scratch
+
+
+def ring_items(net, at, first, last, parts, seconds, finals, bufs):
+    sides = (((at.YP, at.YM), (at.ZP, at.ZM)), ((at.ZP, at.ZM), (at.YP, at.YM)))
+    places = ((at.y, at.z), (at.z, at.y))
+    bufs = list(bufs)
+    one, two = ([], []), ([], [])
+    for i in (0, 1):
+        owns = []
+        for n in range(len(first[i])):
+            own = bufs[8]
+            for way in (0, 1):
+                part = functools.partial(lambda k, f, w: f(k, w), f=parts[i][n], w=way)
+                four = bufs[4 * way : 4 * way + 4]
+                one[i].append(
+                    RingItem(net, sides[i][0], places[i][0], part, way, four, own.at[way])
+                )
+            owns.append(own)
+            bufs = bufs[9:]
+        for n in range(len(last[i])):
+            part = functools.partial(lambda k, f, o: f(o, k), f=seconds[i][n], o=owns[n])
+            two[i].append(
+                RingItem(net, sides[i][1], places[i][1], part, n % 2, bufs[:4], finals[i][n])
+            )
+            bufs = bufs[4:]
+
+    def mix(pair):
+        return [item for items in zip(*pair, strict=True) for item in items]
+
+    return mix(one), mix(two)
+
+
+def ffn_items(net, at, gu, down, gu_own, down_own, bufs):
+    parts = (
+        (
+            lambda k, way: gu.at[way, pl.ds(0, 2), :, k],
+            lambda k, way: down.at[way, :, down_rows(k), LEFT],
+        ),
+        (
+            lambda k, way: gu.at[k // 2, pl.ds(2, 2), k % 2, pl.ds(2 * way, 2)],
+            lambda k, way: down.at[k // 2, k % 2, pl.ds(144 * way, 144), RIGHT],
+        ),
+    )
+    seconds = (
+        (lambda own, k: own.at[k // 2, :, k % 2], lambda own, k: own.at[k // 2, k % 2]),
+        (
+            lambda own, k: own.at[k // 2, :, k % 2],
+            lambda own, k: own.at[k // 2, pl.ds(pl.multiple_of((k % 2) * 64, 64), 80)],
+        ),
+    )
+    finals = (
+        (gu_own.at[pl.ds(0, 2)], down_own.at[:, LEFT]),
+        (gu_own.at[pl.ds(2, 2)], down_own.at[:, RIGHT]),
+    )
+    return ring_items(net, at, FFN_FIRST, FFN_LAST, parts, seconds, finals, bufs)
+
+
+def small_items(net, at, qkv, out, qkv_own, out_own, bufs):
+    parts = (
+        (lambda k, way: qkv.at[:, k, :, pl.ds(512 * way, 512)],),
+        (lambda k, way: out.at[k // 2, k % 2, pl.ds(2 * way, 2)],),
+    )
+    seconds = ((lambda own, k: own.at[k // 2, k % 2],), (lambda own, k: own.at[k // 2, k % 2],))
+    finals = ((qkv_own,), (out_own,))
+    return ring_items(net, at, SMALL_FIRST, SMALL_LAST, parts, seconds, finals, bufs)
+
+
 def backward_kernel(
     dn2_ref,
     mid_ref,
@@ -749,11 +896,16 @@
     qw,
     cos_ref,
     sin_ref,
+    gu,
+    down,
     grad_in,
     grad_out,
     grad_qkv,
+    small_ref,
+    gu_own,
+    down_own,
     sums_ref,
-    bias_ref,
+    sums_in,
     attn_all,
     mid_cols,
     mid_pair,
@@ -768,12 +920,16 @@
     part_in,
     gi_out,
     gi_in,
-    send_sems,
-    recv_sems,
+    *rest,
 ):
+    bufs, (send_sems, recv_sems) = rest[:-2], rest[-2:]
     at = Place()
     net = Net(send_sems, recv_sems, at)
-    at.meet((at.S, at.O, at.OS, at.N1, at.N2, at.N1S, at.N2S))
+    at.meet(
+        (at.S, at.O, at.OS, at.N1, at.N2, at.N1S, at.N2S, at.YP, at.YM, at.ZP, at.ZM)
+    )
+    first, last = ffn_items(net, at, gu, down, gu_own, down_own, bufs)
+    begin(first)
     peers = ((at.S, at.sib), (at.O, at.far), (at.OS, at.sibfar))
     pair = (at.col, 7 - at.col)
 
@@ -844,6 +1000,8 @@
     for j in (0, 1):
         d_attn[pl.ds(j * BLOCK, BLOCK), :] = dot(mid_pair[j], ow[...], 1, 1).astype(BF)
     d_kv[...] = jnp.zeros_like(d_kv)
+    for item in first:
+        item.middle()
 
     for j in (0, 1):
         keys = SEQ // 2 * (j + 1)
@@ -882,6 +1040,9 @@
             d_qkv_all[rows_at(pair[j]), pl.ds(h * HEAD, HEAD)] = (
                 one * cosines[j] - turn(one) * sines[j]
             ).astype(BF)
+    for item in first:
+        item.end()
+    begin(last)
     gather_attn.end()
     for key, (_, row, col) in zip(spread, others, strict=True):
         net.take(key, mid_cols.at[rows_at(block_of(row, col)), :])
@@ -911,20 +1072,35 @@
     bent = d_normed * gain1
     total = d_mid[...] + scale * (bent - unit * jnp.mean(bent * unit, axis=1, keepdims=True))
     gi_out[...] = total.astype(BF)
+    sums_in[at.row * 4 + at.col] = sums_ref[:, cols_at(at.col)]
+    sums_keys = [
+        net.send(sums_ref.at[:, cols_at(col)], sums_in.at[at.row * 4 + at.col], device)
+        for device, row, col in others
+    ]
     half_rows = pl.ds(pl.multiple_of((at.block - 4 * at.row) * BLOCK, BLOCK), BLOCK)
     gi_keys = [
         net.send(gi_out.at[:, cols_at(col)], gi_in.at[half_rows, :], device)
         for device, col in peers
     ]
     gi_in[half_rows, :] = gi_out[:, cols_at(at.col)]
+    for item in last:
+        item.middle()
     gather_qkv.middle()
     gather_qkv.end()
     grad_qkv[...] = dot(n1c[...], d_qkv_all[...], 0, 0).astype(BF)
     ones = jnp.ones((8, SEQ), BF)
-    bias_ref[...] = dot(ones, d_qkv_all[...])
+    small_ref[:, FEAT:] = dot(ones, d_qkv_all[...])
+    for key, (_, row, col) in zip(sums_keys, others, strict=True):
+        net.take(key, sums_in.at[row * 4 + col])
+    total = sums_in[0]
+    for i in range(1, 8):
+        total = total + sums_in[i]
+    small_ref[:, :FEAT] = total
     for key, (_, col) in zip(gi_keys, peers, strict=True):
         offset = block_of(at.row, col) - 4 * at.row
         net.take(key, gi_in.at[pl.ds(pl.multiple_of(offset * BLOCK, BLOCK), BLOCK), :])
+    for item in last:
+        item.end()
     grad_in[...] = gi_in[...].astype(F32)
     net.finish()
 
@@ -937,8 +1113,9 @@
         out((SEQ // 2, FEAT), F32),
         out((QCOLS, FEAT), BF),
         out((FEAT, QKV), BF),
-        out((8, MODEL), F32),
-        out((8, QKV), F32),
+        out((8, FEAT + QKV), F32),
+        out((4, 48, PART), BF),
+        out((80, MODEL), BF),
     )
     return pl.pallas_call(
         backward_kernel,
@@ -946,6 +1123,8 @@
         in_specs=[vmem()] * len(args),
         out_specs=[vmem()] * len(outs),
         scratch_shapes=[
+            pltpu.VMEM((8, MODEL), F32),
+            pltpu.VMEM((8, 8, FEAT), F32),
             pltpu.VMEM((SEQ, QCOLS), BF),
             pltpu.VMEM((SEQ, FEAT), BF),
             pltpu.VMEM((2, BLOCK, MODEL), BF),
@@ -960,9 +1139,9 @@
             pltpu.VMEM((BLOCK, MODEL), BF),
             pltpu.VMEM((BLOCK, MODEL), BF),
             pltpu.VMEM((SEQ // 2, FEAT), BF),
-            pltpu.SemaphoreType.DMA((40,)),
-            pltpu.SemaphoreType.DMA((40,)),
-        ],
+        ]
+        + ring_scratch(FFN_FIRST, FFN_LAST)
+        + [pltpu.SemaphoreType.DMA((80,)), pltpu.SemaphoreType.DMA((80,))],
         compiler_params=pltpu.CompilerParams(
             collective_id=2, has_side_effects=True, vmem_limit_bytes=VMEM_LIMIT
         ),
@@ -971,6 +1150,201 @@
         ),
         name="attention_backward",
     )(*args)
+
+
+def sums_kernel(
+    gu_own,
+    down_own,
+    qkv,
+    out,
+    small_ref,
+    all_gu,
+    all_down,
+    all_qkv,
+    all_out,
+    small_out,
+    small_y,
+    small_z,
+    *rest,
+):
+    bufs, (send_sems, recv_sems) = rest[:-2], rest[-2:]
+    at = Place()
+    net = Net(send_sems, recv_sems, at)
+    at.meet((at.S, at.O, at.OS, at.YP, at.YM, at.ZP, at.ZM, at.Y2, at.Z2))
+    z, y = at.z, at.y
+
+    def gu_piece(k, lanes):
+        rows = pl.ds(pl.multiple_of((k % 8) * 48, 16), 48)
+        return all_gu.at[k // 8, rows, lanes]
+
+    def part_lanes(col):
+        return pl.ds(aligned(col, PART), PART)
+
+    def down_piece(k):
+        return all_down.at[:, pl.ds(pl.multiple_of(k * 80, 16), 80), :]
+
+    def down_slot(col):
+        return all_down.at[col, pl.ds(pl.multiple_of(at.dp * 80, 16), 80), :]
+
+    def feat_lanes(col):
+        return pl.ds(aligned(col, FEAT), FEAT)
+
+    def qkv_piece(k):
+        rows = pl.ds(pl.multiple_of((k % 8) * 48, 16), 48)
+        return all_qkv.at[rows, pl.ds(pl.multiple_of((k // 8) * 512, 512), 512)]
+
+    def out_piece(k):
+        return all_out.at[pl.ds(pl.multiple_of(k * 48, 16), 48), :]
+
+    peers = ((at.O, at.far), (at.OS, at.sibfar), (at.S, at.sib))
+    keys = []
+    for device, col in peers:
+        keys.append(
+            (
+                net.send(gu_own.at[col], gu_piece(at.dp, part_lanes(at.col)), device),
+                net.send(down_own.at[:, feat_lanes(col)], down_slot(at.col), device),
+            )
+        )
+    small_y[y] = small_ref[...]
+    small_keys = [net.send(small_ref, small_y.at[y], d) for d in (at.YP, at.YM, at.Y2)]
+    first, last = small_items(net, at, qkv, out, qkv_piece(at.dp), out_piece(at.dp), bufs)
+    begin(first)
+    gu_piece(at.dp, part_lanes(at.col))[...] = gu_own[at.col]
+    down_slot(at.col)[...] = down_own[:, feat_lanes(at.col)]
+    for (one, two), (_, col) in zip(keys, peers, strict=True):
+        net.take(one, gu_piece(at.dp, part_lanes(col)))
+        net.take(two, down_slot(col))
+
+    def half0(zz, yy):
+        return [gu_piece(zz * 4 + yy, pl.ds(0, 3456))]
+
+    def half1(zz, yy):
+        return [gu_piece(zz * 4 + yy, pl.ds(3456, 1152)), down_piece(zz * 4 + yy)]
+
+    ring = ring_dp(net, at, (half0, half1))
+    next(ring)
+    for item in first:
+        item.middle()
+    for key, k in zip(small_keys, (y - 1, y + 1, y + 2), strict=True):
+        net.take(key, small_y.at[lax.rem(k + 4, 4)])
+    small_z[z] = (small_y[0] + small_y[1]) + (small_y[2] + small_y[3])
+    small_keys = [net.send(small_z.at[z], small_z.at[z], d) for d in (at.ZP, at.ZM, at.Z2)]
+    next(ring)
+    for item in first:
+        item.end()
+    begin(last)
+    next(ring)
+    for item in last:
+        item.middle()
+    for key, k in zip(small_keys, (z - 1, z + 1, z + 2), strict=True):
+        net.take(key, small_z.at[lax.rem(k + 4, 4)])
+    small_out[...] = (small_z[0] + small_z[1]) + (small_z[2] + small_z[3])
+    next(ring)
+    for item in last:
+        item.end()
+    after = ring_dp(
+        net,
+        at,
+        (lambda zz, yy: [qkv_piece(zz * 4 + yy)], lambda zz, yy: [out_piece(zz * 4 + yy)]),
+    )
+    next(after)
+    for _ in ring:
+        next(after, None)
+    drain(after)
+    net.finish()
+
+
+def run_sums(gu, down, qkv, out, small):
+    def shape(dims, dtype):
+        return jax.ShapeDtypeStruct(dims, dtype)
+
+    outs = (
+        shape((2, FEAT, 4 * PART), BF),
+        shape((4, 1280, FEAT), BF),
+        shape((FEAT, QKV), BF),
+        shape((QCOLS, FEAT), BF),
+        shape(small.shape, F32),
+    )
+    return pl.pallas_call(
+        sums_kernel,
+        out_shape=outs,
+        in_specs=[vmem()] * 5,
+        out_specs=[vmem()] * len(outs),
+        scratch_shapes=[pltpu.VMEM((4,) + small.shape, F32)] * 2
+        + ring_scratch(SMALL_FIRST, SMALL_LAST)
+        + [pltpu.SemaphoreType.DMA((128,)), pltpu.SemaphoreType.DMA((128,))],
+        compiler_params=pltpu.CompilerParams(
+            collective_id=3, has_side_effects=True, vmem_limit_bytes=VMEM_LIMIT
+        ),
+        cost_estimate=pl.CostEstimate(
+            flops=10**8, bytes_accessed=60 * 10**6, transcendentals=0
+        ),
+        name="sums_over_sequences",
+    )(gu, down, qkv, out, small)
+
+
+def widen_kernel(gu, down, gate_out, up_out, down_out, gate_buf, up_buf, down_buf, sems):
+    skip = 3 * PART
+    slots = [None, None]
+
+    def chunk(n):
+        rows = pl.ds(n * 48, 48)
+        place = n % 2
+        if slots[place] is not None:
+            for copy in slots[place]:
+                copy.wait()
+        copies = []
+        for i, (buf, out) in enumerate(((gate_buf, gate_out), (up_buf, up_out))):
+            buf[place, :, :skip] = gu[i, rows, :skip].astype(F32)
+            buf[place, :, skip:] = gu[i, rows, skip + HEAD :].astype(F32)
+            copies.append(pltpu.make_async_copy(buf.at[place], out.at[rows, :], sems.at[place, i]))
+        quarter, part = n // 2, n % 2
+        for m in range(4):
+            slot = 160 * (4 * part + m)
+            down_buf[place, pl.ds(144 * m, 80), :] = down[quarter, pl.ds(slot, 80), :].astype(F32)
+            down_buf[place, pl.ds(144 * m + 80, 64), :] = down[
+                quarter, pl.ds(slot + 96, 64), :
+            ].astype(F32)
+        drop = HEAD if quarter == 3 and part == 0 else 0
+        start = PART * quarter + 576 * part - (HEAD if quarter == 3 and part == 1 else 0)
+        copies.append(
+            pltpu.make_async_copy(
+                down_buf.at[place, pl.ds(drop, 576 - drop), :],
+                down_out.at[pl.ds(start, 576 - drop), :],
+                sems.at[place, 2],
+            )
+        )
+        for copy in copies:
+            copy.start()
+        slots[place] = copies
+
+    for n in range(8):
+        chunk(n)
+    for copies in slots:
+        for copy in copies:
+            copy.wait()
+
+
+def run_widen(gu, down):
+    outs = [jax.ShapeDtypeStruct((FEAT, UNITS), F32)] * 2
+    outs.append(jax.ShapeDtypeStruct((UNITS, FEAT), F32))
+    return pl.pallas_call(
+        widen_kernel,
+        out_shape=outs,
+        in_specs=[vmem()] * 2,
+        out_specs=[anywhere()] * 3,
+        scratch_shapes=[
+            pltpu.VMEM((2, 48, UNITS), F32),
+            pltpu.VMEM((2, 48, UNITS), F32),
+            pltpu.VMEM((2, 576, FEAT), F32),
+            pltpu.SemaphoreType.DMA((2, 3)),
+        ],
+        compiler_params=pltpu.CompilerParams(vmem_limit_bytes=VMEM_LIMIT),
+        cost_estimate=pl.CostEstimate(
+            flops=10**7, bytes_accessed=36 * 10**6, transcendentals=0
+        ),
+        name="widen",
+    )(gu, down)
 
 
 def rope_tables(count):
@@ -997,9 +1371,6 @@
     w_down,
     out_grad,
 ):
-    n_dp = lax.axis_size("dp")
-    feat, part, units, query_cols = FEAT, PART, UNITS, QCOLS
-
     cosine, sine = rope_tables(SEQ)
     w_qkv = jnp.concatenate([w_query, w_key, w_value], axis=1)
     bias = jnp.concatenate([b_query, b_key, b_value]).astype(F32)[None]
@@ -1024,10 +1395,10 @@
     ) = run_forward(
         layer_input, out_grad, w_qkv, w_out, w_gate, w_up, w_down, gains, bias, cosine, sine
     )
-    dn2, layer_output, grad_gate, grad_up, grad_down = run_ffn(
+    dn2, layer_output, grad_gu, grad_down = run_ffn(
         normed2_all, grads_all, gate_w, up_w, down_w, mid
     )
-    grad_input, grad_out, grad_qkv, sums, grad_bias = run_backward(
+    grad_input, grad_out, grad_qkv, small, grad_gu, grad_down = run_backward(
         dn2,
         mid,
         grads_all,
@@ -1043,55 +1414,34 @@
         qkv_w,
         cosine,
         sine,
-    )
-
-    def sum_dp(grad):
-        rows = grad.shape[1] // n_dp
-        sliced = grad.reshape(4, n_dp, rows, -1).transpose(1, 0, 2, 3)
-        mine = lax.psum_scatter(sliced, "dp", scatter_dimension=0, tiled=True)[0]
-        return lax.all_to_all(mine, "col", 0, 0, tiled=True)
-
-    def spread(grad):
-        return lax.all_gather(grad, "dp", axis=0, tiled=True).astype(F32)
-
-    grad_down = sum_dp(grad_down.reshape(part, 4, feat).transpose(1, 0, 2))
-    grad_gate = sum_dp(grad_gate.reshape(4, feat, part))
-    grad_up = sum_dp(grad_up.reshape(4, feat, part))
-
-    def sum_all(grad):
-        mine = lax.psum_scatter(grad.astype(BF), "dp", scatter_dimension=0, tiled=True)
-        return spread(mine)
-
-    grad_qkv = sum_all(grad_qkv)
-    grad_out = sum_all(grad_out)
-    gains = lax.psum(sums[:2], ("dp", "row", "col"))
-    gains = lax.dynamic_slice_in_dim(gains, lax.axis_index("col") * feat, feat, 1)
-    grad_bias = lax.psum(grad_bias[0], "dp")
-
-    def join(grad):
-        joined = jnp.concatenate([grad[0], grad[1], grad[2], grad[3][:, HEAD:]], axis=1)
-        return spread(joined)
-
-    def join_down(grad):
-        gathered = lax.all_gather(grad, "dp", axis=1, tiled=True)
-        joined = jnp.concatenate([gathered[0], gathered[1], gathered[2], gathered[3][HEAD:]])
-        return joined.astype(F32)
-
+        grad_gu.reshape(2, 4, 2, 4, 48, PART),
+        grad_down.reshape(2, 2, 288, MODEL),
+    )
+    grad_gu, grad_down, grad_qkv, grad_out, small = run_sums(
+        grad_gu,
+        grad_down,
+        grad_qkv.reshape(2, 4, 48, QKV),
+        grad_out.reshape(2, 2, 4, 48, FEAT),
+        small,
+    )
+    grad_gate, grad_up, grad_down = run_widen(grad_gu, grad_down)
+    grad_qkv = grad_qkv.astype(F32)
+    key_end, bias_start = QCOLS + HEAD, FEAT + QCOLS
     return (
         layer_output,
         grad_input,
-        gains[0],
-        grad_qkv[:, :query_cols],
-        grad_qkv[:, query_cols : query_cols + HEAD],
-        grad_qkv[:, query_cols + HEAD :],
-        grad_bias[:query_cols],
-        grad_bias[query_cols : query_cols + HEAD],
-        grad_bias[query_cols + HEAD :],
-        grad_out,
-        gains[1],
-        join(grad_gate),
-        join(grad_up),
-        join_down(grad_down),
+        small[0, :FEAT],
+        grad_qkv[:, :QCOLS],
+        grad_qkv[:, QCOLS:key_end],
+        grad_qkv[:, key_end:],
+        small[0, FEAT:bias_start],
+        small[0, bias_start : bias_start + HEAD],
+        small[0, bias_start + HEAD :],
+        grad_out.astype(F32),
+        small[1, :FEAT],
+        grad_gate,
+        grad_up,
+        grad_down,
     )
 
 

time: 775 us -> 403 us (0.52)
  waiting for transfers between devices: 262 us -> 0 us
  blocking collectives: 183 us -> 0 us
  Pallas kernels: 253 us -> 377 us
  other arithmetic: 28.9 us -> 7.74 us
  local copies, waits for them, and re-layouts: 27.3 us -> 11.7 us
  between operations: 14.5 us -> 1.18 us
    unnamed x13 -> x0, waiting for transfers between devices: 155 us -> none
    pallas_call x0 -> x2, Pallas kernels: none -> 108 us  [the longest x1 96.4 us: run_sums(): pl.pallas_call(sums_kernel, out_shape=outs, in_specs=[vmem()] * 5, out_sp...]
    all_gather x3 -> x0, waiting for transfers between devices: 107 us -> none  [the longest x2 82.2 us: spread(): return lax.all_gather(grad, 'dp', axis=0, tiled=True).astype(F32)]
    psum x2 -> x0, blocking collectives: 102 us -> none  [the longest x1 64.3 us: body(): gains = lax.psum(sums[:2], ('dp', 'row', 'col'))]
    all_gather x2 -> x0, blocking collectives: 46.5 us -> none  [spread(): return lax.all_gather(grad, 'dp', axis=0, tiled=True).astype(F32)]
    all_to_all x3 -> x0, blocking collectives: 33.9 us -> none  [sum_dp(): return lax.all_to_all(mine, 'col', 0, 0, tiled=True)]
    convert_element_type x4 -> x1, other arithmetic: 22.7 us -> 1.09 us  [body(): grad_out.astype(F32)]
    pallas_call x1, Pallas kernels: 75.2 us -> 91.9 us  [run_backward(): pl.pallas_call(backward_kernel, out_shape=outs, in_specs=[vmem()] * len(a...]
  transfers between devices with their start and end apart: 8 -> 0, of which waited for: 7 -> 0; matrix products, arithmetic and copies ran while one was open for 4% -> 0% of each run, Pallas kernels for 10% -> 0%
where the time goes in v3:
time: 403 us; the launch traced here: 398 us
  Pallas kernels  377 us (94%)
  local copies, waits for them, and re-layouts  11.7 us (3%)
  other arithmetic  7.74 us (2%)
    pallas_call x1, Pallas kernels, run_forward(): pl.pallas_call(forward_kernel, out_shape=outs, in_specs=[vmem()] * 4 + [a...  99 us
    pallas_call x1, Pallas kernels, run_sums(): pl.pallas_call(sums_kernel, out_shape=outs, in_specs=[vmem()] * 5, out_sp...  96.4 us
    pallas_call x1, Pallas kernels, run_backward(): pl.pallas_call(backward_kernel, out_shape=outs, in_specs=[vmem()] * len(a...  91.9 us
    pallas_call x1, Pallas kernels, run_ffn(): pl.pallas_call(ffn_kernel, out_shape=outs, in_specs=[vmem()] * 6, out_spe...  78.7 us
    pallas_call x1, Pallas kernels, run_widen(): pl.pallas_call(widen_kernel, out_shape=outs, in_specs=[vmem()] * 2, out_s...  11.3 us

profile of v3, /device:TPU:0, one launch (start us, length us, event | category | flops | bytes accessed | tf_op | source)
XLA Modules:
  0.0 398.0 jit_solution(13172875239682878544)
XLA Ops:
  0.7 0.7 reshape.148
  1.3 0.7 reshape.154
  2.0 0.7 concatenate.30
  2.7 1.3 maximum_convert_fusion.bias_ref
  4.0 0.0 copy-start.3
  4.1 2.2 pad_maximum_fusion.wqkv_ref
  6.2 1.9 fusion
  8.1 1.3 pad_maximum_fusion.1
  9.4 0.0 copy-done.3
  9.4 99.0 %attention_forward.1 = (bf16[128,1536]{1,0:T(8,128)(2,1)}, bf16[1024,384]{1,0:T(8,128)(2,1)}, bf16[1024,1536]{1,0:T(8,128)(2,1)}, bf16[1024,1536]{1,0:T(8,128)(2...) custom-call(bf16[512,384]{1,0:T(8,128)(2,1)} %x_ref.1, ...), custom_call_target="tpu_custom_call" | custom-call | flops 8000000000 | bytes 60000000 | tf_op jit(solution)/shard_map/attention_forward/pallas_call | solution.py:529
  108.5 78.7 %feed_forward.1 = (f32[128,1536]{1,0:T(8,128)}, f32[512,384]{1,0:T(8,128)}, bf16[2,1536,1152]{2,1,0:T(8,128)(2,1)}, bf16[1152,1536]{1,0:T(8,128)(2,1)}) custom-call(bf16[1024,1536]{1,0:T(8,128)(2,1)} %get-tuple-element.72.n2, bf16[1024,1536]{1,0:T(8,128)(2,1)} %get-tuple-element.73.og.og_ref, bf16[1536,1152]{1,0:T(8,128)(2,1)} %get-tuple-element.74.gw, ...), custom_call_target="tpu_custom_call" | custom-call | flops 28999999488 | bytes 60000000 | tf_op jit(solution)/shard_map/feed_forward/pallas_call | solution.py:715
  187.2 91.9 %attention_backward.1 = (f32[512,384]{1,0:T(8,128)}, bf16[768,384]{1,0:T(8,128)(2,1)}, bf16[384,1024]{1,0:T(8,128)(2,1)}, f32[8,1408]{1,0:T(8,128)}, bf16[4,48,1...) custom-call(f32[128,1536]{1,0:T(8,128)} %get-tuple-element.79.dn2_ref, f32[128,1536]{1,0:T(8,128)} %get-tuple-element.77.mid_ref, ...), custom_call_target="tpu_custom_call" | custom-call | flops 10000000000 | bytes 40000000 | tf_op jit(solution)/shard_map/attention_backward/pallas_call | solution.py:1120
  279.1 96.4 %sums_over_sequences.1 = (bf16[2,384,4608]{2,1,0:T(8,128)(2,1)}, bf16[4,1280,384]{2,1,0:T(8,128)(2,1)}, bf16[384,1024]{1,0:T(8,128)(2,1)}, bf16[768,384]{1,0:T(8,128)(2,1)}, f32[8,1408]{1,0:T(8,128)}) custom-call(bf16[4,48,1152]{2,1,0:T(8,128)(2,1)} %get-tuple-element.93.gu_own, bf16[80,1536]{1,0:T(8,128)(2,1)} %get-tuple-element.94.down_own, ...), custom_call_target="tpu_custom_call" | custom-call | flops 100000000 | bytes 60000000 | tf_op jit(solution)/shard_map/sums_over_sequences/pallas_call | solution.py:1268
  375.5 0.0 copy-start.2
  375.5 1.3 slice_bitcast_fusion
  376.8 1.3 slice_reduce_fusion
  378.1 1.4 slice_reduce_fusion.1
  379.5 1.7 fusion.1
  381.2 2.2 slice.61
  383.4 0.0 copy-done.2
  383.4 1.1 convert_element_type.48
  384.5 0.0 copy-start
  384.5 0.0 copy-start.1
  384.5 11.3 %widen.1 = (f32[384,4480]{1,0:T(8,128)}, f32[384,4480]{1,0:T(8,128)}, f32[4480,384]{1,0:T(8,128)}) custom-call(bf16[2,384,4608]{2,1,0:T(8,128)(2,1)} %get-tuple-element.101.gu, bf16[4,1280,384]{2,1,0:T(8,128)(2,1)} %get-tuple-element.102.down), custom_call_target="tpu_custom_call" | custom-call | flops 10000000 | bytes 36000000 | tf_op jit(solution)/shard_map/widen/pallas_call | solution.py:1331
  395.8 0.0 copy-done
  395.8 0.9 copy.31
  396.7 0.0 copy-done.1
  396.7 0.9 copy.32
  (4 shorter events, 0.1 us)
Async XLA Ops:
  4.0 5.4 %copy-start.3 = (f32[8,384]{1,0:T(8,128)}, f32[8,384]{1,0:T(8,128)S(1)}, u32[]{:S(2)}) copy-start(f32[8,384]{1,0:T(8,128)S(1)} %scatter.14.gains_ref) | copy-start | bytes 36868
  375.5 7.9 %copy-start.2 = (bf16[768,384]{1,0:T(8,128)(2,1)S(1)}, bf16[768,384]{1,0:T(8,128)(2,1)}, u32[]{:S(2)}) copy-start(bf16[768,384]{1,0:T(8,128)(2,1)} %get-tuple-element.100) | copy-start | bytes 1769476
  384.5 11.3 %copy-start = (f32[512,384]{1,0:T(8,128)S(1)}, f32[512,384]{1,0:T(8,128)}, u32[]{:S(2)}) copy-start(f32[512,384]{1,0:T(8,128)} %get-tuple-element.131) | copy-start | bytes 2359300
  384.5 12.2 %copy-start.1 = (f32[512,384]{1,0:T(8,128)S(1)}, f32[512,384]{1,0:T(8,128)}, u32[]{:S(2)}) copy-start(f32[512,384]{1,0:T(8,128)} %get-tuple-element.132) | copy-start | bytes 2359300

commit v4 on v3

--- a/solution.py
+++ b/solution.py
@@ -104,9 +104,11 @@
     def take(self, key, dst):
         self.copy(key, dst, dst, self.at.S).wait_recv()
 
-    def finish(self):
-        for copy in self.sent:
+    def finish(self, copies=None):
+        copies = list(self.sent) if copies is None else copies
+        for copy in copies:
             copy.wait_send()
+            self.sent.remove(copy)
 
 
 class Gather8:
@@ -139,13 +141,17 @@
         net.take(self.kb, last)
         self.f4 = net.send(last, last, at.S)
 
-    def end(self):
+    def end(self, chip=None):
         net, at, place = self.net, self.at, self.place
-        net.take(self.k0, place(at.row, at.sib, None))
-        net.take(self.f1, place(1 - at.row, at.sib, None))
-        net.take(self.f2, place(1 - at.row, at.sibfar, None))
-        net.take(self.f3, place(at.row, at.sibfar, 0))
-        net.take(self.f4, place(at.row, at.sibfar, 1))
+        if chip in (None, 3):
+            net.take(self.k0, place(at.row, at.sib, None))
+        if chip in (None, 1):
+            net.take(self.f1, place(1 - at.row, at.sib, None))
+        if chip in (None, 2):
+            net.take(self.f2, place(1 - at.row, at.sibfar, None))
+        if chip in (None, 0):
+            net.take(self.f3, place(at.row, at.sibfar, 0))
+            net.take(self.f4, place(at.row, at.sibfar, 1))
 
 
 def ring_dp(net, at, halves):
@@ -223,10 +229,73 @@
     return jnp.where(keys <= places, scores, NEG)
 
 
+def vmem():
+    return pl.BlockSpec(memory_space=pltpu.VMEM)
+
+
+def anywhere():
+    return pl.BlockSpec(memory_space=pl.ANY)
+
+
+class Reduce8:
+    def __init__(self, net, at, own, other, sib_in, first_in, last_in, near_in, away_in):
+        self.net, self.at, self.own, self.other, self.sib_in = net, at, own, other, sib_in
+        self.first_in, self.last_in, self.near_in, self.away_in = first_in, last_in, near_in, away_in
+        self.half = own.shape[1] // 2
+        self.keys = {}
+
+    def put(self, j, mine, theirs):
+        self.own[j] = mine
+        self.other[j] = theirs
+        self.keys[j] = self.net.send(self.other.at[j], self.sib_in.at[j], self.at.S)
+
+    def step(self, j):
+        net, at, half = self.net, self.at, self.half
+        net.take(self.keys[j], self.sib_in.at[j])
+        total = self.own[j].astype(F32) + self.sib_in[j].astype(F32)
+        if j == 0:
+            self.own[j] = total.astype(BF)
+            self.first = net.send(self.own.at[j, pl.ds(0, half)], self.first_in, at.N1)
+            self.last = net.send(self.own.at[j, pl.ds(half, half)], self.last_in, at.N2)
+        elif j == 1:
+            net.take(self.last, self.last_in)
+            self.own[j, :half] = total[:half].astype(BF)
+            self.own[j, half:] = (total[half:] + self.last_in[...].astype(F32)).astype(BF)
+            self.near = net.send(self.own.at[j], self.near_in, at.N1)
+        elif j == 2:
+            net.take(self.first, self.first_in)
+            self.own[j, :half] = (total[:half] + self.first_in[...].astype(F32)).astype(BF)
+            self.own[j, half:] = total[half:].astype(BF)
+            self.away = net.send(self.own.at[j], self.away_in, at.N2)
+        else:
+            net.take(self.near, self.near_in)
+            net.take(self.away, self.away_in)
+            return total + self.near_in[...].astype(F32) + self.away_in[...].astype(F32)
+        return None
+
+
+def reduce8_scratch(rows, columns):
+    return [
+        pltpu.VMEM((4, rows, columns), BF),
+        pltpu.VMEM((4, rows, columns), BF),
+        pltpu.VMEM((4, rows, columns), BF),
+        pltpu.VMEM((rows // 2, columns), BF),
+        pltpu.VMEM((rows // 2, columns), BF),
+        pltpu.VMEM((rows, columns), BF),
+        pltpu.VMEM((rows, columns), BF),
+    ]
+
+
+def tiles_of(width, step):
+    return [(first, min(step, width - first)) for first in range(0, width, step)]
+
+
 def forward_kernel(
     x_ref,
     og_ref,
-    wqkv_ref,
+    wq_ref,
+    wk_ref,
+    wv_ref,
     wout_ref,
     wg_ref,
     wu_ref,
@@ -237,6 +306,23 @@
     sin_ref,
     xs_ref,
     n1c_ref,
+    og_out,
+    qw_out,
+    ow_out,
+    q_ref,
+    k_ref,
+    v_ref,
+    lse_ref,
+    attn_ref,
+    mid_ref,
+    gains_all,
+    dn2_ref,
+    out_ref,
+    grad_gu,
+    grad_down,
+    wqkv_ref,
+    x_all,
+    n1,
     og_all,
     n2_all,
     qw,
@@ -244,30 +330,34 @@
     gw,
     uw,
     dw,
-    q_ref,
-    k_ref,
-    v_ref,
-    lse_ref,
-    attn_ref,
-    mid_ref,
-    gains_all,
-    x_all,
-    n1,
     part_out,
     part_in,
-    send_sems,
-    recv_sems,
-    local_sems,
+    d_up,
+    ffn,
+    tile_buf,
+    *rest,
 ):
+    red_a, red_b, sems = rest[:7], rest[7:14], rest[14:]
+    send_sems, recv_sems, local_sems, tile_sems = sems
     at = Place()
     net = Net(send_sems, recv_sems, at)
-    at.meet((at.S, at.N1, at.N2, at.O, at.OS, at.YP, at.YM, at.ZP, at.ZM))
-    local = []
+    local, local_count = [], iter(range(32))
 
     def move(src, dst):
-        copy = pltpu.make_async_copy(src, dst, local_sems.at[len(local)])
+        copy = pltpu.make_async_copy(src, dst, local_sems.at[next(local_count)])
         copy.start()
         local.append(copy)
+        return copy
+
+    joined = [
+        move(wq_ref, wqkv_ref.at[:, pl.ds(0, QCOLS)]),
+        move(wk_ref, wqkv_ref.at[:, pl.ds(QCOLS, HEAD)]),
+        move(wv_ref, wqkv_ref.at[:, pl.ds(QCOLS + HEAD, HEAD)]),
+    ]
+    at.meet((at.S, at.N1, at.N2, at.O, at.OS, at.YP, at.YM, at.ZP, at.ZM))
+    for copy in joined:
+        copy.wait()
+    local.clear()
 
     def tokens_of(array):
         def place(row, col, part):
@@ -365,8 +455,14 @@
         return slices
 
     net.take(across[0], qkv_slices(at.z, at.y)[0])
-    net.take(across[1], out_slices(at.z, at.y)[0])
-    ring = ring_dp(net, at, (qkv_slices, out_slices))
+    ring = ring_dp(
+        net,
+        at,
+        (
+            lambda z, y: [qkv_slices(z, y)[0].at[:, pl.ds(0, 256)]],
+            lambda z, y: [qkv_slices(z, y)[0].at[:, pl.ds(256, 256)]],
+        ),
+    )
     next(ring)
     near = [
         net.send(wg_ref.at[:, pl.ds(quarter_start(at.sib), PART)], gw.at[pl.ds(mine, FEAT), :], at.S),
@@ -380,23 +476,32 @@
     net.take(gain_far, gains_far)
     gain_sibfar = net.send(gains_far, gains_far, at.S)
     next(ring)
+    net.take(across[1], out_slices(at.z, at.y)[0])
+    net.take(across[2], ffn_slices(gw, 0, 80)(at.z, at.y)[0])
+    net.take(across[3], ffn_slices(uw, 80, 64)(at.z, at.y)[0])
+    net.take(across[4], ffn_slices(uw, 0, 144)(at.z, at.y)[1])
+    drain(ring)
+    ring = ring_dp(
+        net,
+        at,
+        (
+            ffn_slices(gw, 0, 80),
+            lambda z, y: ffn_slices(uw, 80, 64)(z, y) + out_slices(z, y),
+        ),
+    )
+    next(ring)
+    cols_half, rows_half = pl.ds(aligned(at.core, 512), 512), pl.ds(aligned(at.core, FEAT), FEAT)
+    far_qw = net.send(qw.at[far_half, cols_half], qw.at[far_half, cols_half], at.S)
     gather_og = Gather8(net, at, tokens_of(og_all))
     gather_x.late()
     gather_og.start(og_ref)
-    drain(ring)
-    cols_half, rows_half = pl.ds(aligned(at.core, 512), 512), pl.ds(aligned(at.core, FEAT), FEAT)
-    far_qw = net.send(qw.at[far_half, cols_half], qw.at[far_half, cols_half], at.S)
-    far_ow = net.send(ow.at[rows_half, far_half], ow.at[rows_half, far_half], at.S)
-    net.take(across[2], ffn_slices(gw, 0, 80)(at.z, at.y)[0])
-    net.take(across[3], ffn_slices(uw, 80, 64)(at.z, at.y)[0])
-    net.take(across[4], ffn_slices(uw, 0, 144)(at.z, at.y)[1])
-    ring = ring_dp(net, at, (ffn_slices(gw, 0, 80), ffn_slices(uw, 80, 64)))
-    next(ring)
     gather_x.end()
+    early = list(net.sent)
     net.take(gain_sib, gains_all.at[:, pl.ds(aligned(at.sib, FEAT), FEAT)])
     net.take(gain_sibfar, gains_all.at[:, pl.ds(aligned(at.sibfar, FEAT), FEAT)])
     for copy in local:
         copy.wait()
+    local.clear()
 
     gain1, gain2 = gains_all[0:1, :], gains_all[1:2, :]
 
@@ -406,7 +511,9 @@
         n1[rows, :] = (values * rms(values) * gain1).astype(BF)
         return carry
 
-    lax.fori_loop(0, SEQ // BLOCK, norm_block, 0)
+    lax.fori_loop(0, SEQ // BLOCK // 2, norm_block, 0)
+    next(ring)
+    lax.fori_loop(SEQ // BLOCK // 2, SEQ // BLOCK, norm_block, 0)
     next(ring)
     gather_og.middle()
     my_rows = pl.ds(aligned(at.block, BLOCK), BLOCK)
@@ -415,6 +522,7 @@
     net.take(near_qw, qw.at[pl.ds(aligned(at.sib, FEAT), FEAT), :])
     other_cols = pl.ds(aligned(1 - at.core, 512), 512)
     net.take(far_qw, qw.at[far_half, other_cols])
+    move(qw, qw_out)
 
     def kv_block(i, carry):
         rows = pl.ds(aligned(i, 256), 256)
@@ -455,16 +563,23 @@
             attn_ref[rows, lanes] = dot(probs, v_ref[:keys, :]).astype(BF)
             return carry
 
-        lax.fori_loop(0, HEADS, attend, 0)
+        lax.fori_loop(0, HEADS // 2, attend, 0)
         next(ring)
+        lax.fori_loop(HEADS // 2, HEADS, attend, 0)
+        next(ring)
+
+    drain(ring)
+    far_ow = net.send(ow.at[rows_half, far_half], ow.at[rows_half, far_half], at.S)
+    gather_og.end()
+    move(og_all.at[my_rows, :], og_out)
 
     net.take(near_ow, ow.at[:, pl.ds(aligned(at.sib, FEAT), FEAT)])
     other_rows = pl.ds(aligned(1 - at.core, FEAT), FEAT)
     net.take(far_ow, ow.at[other_rows, far_half])
+    move(ow, ow_out)
     part_out[...] = dot(attn_ref[pl.ds(aligned(1 - at.row, BLOCK), BLOCK), :], ow[...]).astype(BF)
     part = net.send(part_out, part_in, at.N1)
     own = dot(attn_ref[pl.ds(aligned(at.row, BLOCK), BLOCK), :], ow[...])
-    next(ring)
     net.take(part, part_in)
     mid = xs_ref[...].astype(F32) + own + part_in[...].astype(F32)
     mid_ref[...] = mid
@@ -478,170 +593,23 @@
     n2_all[my_rows, :] = (mid * rms(mid) * gain2).astype(BF)
     gather_n2 = Gather8(net, at, place_n2)
     gather_n2.start(place_n2(at.row, at.col, None))
-    gather_og.end()
-    next(ring)
+    net.take(near[2], dw.at[:, pl.ds(aligned(at.sib, FEAT), FEAT)])
+
+    def hidden_back(i, carry):
+        rows = pl.ds(aligned(i, 256), 256)
+        for first, width in tiles_of(PART, 512):
+            lanes = pl.ds(first, width)
+            d_up[rows, lanes] = dot(og_all[rows, :], dw[lanes, :], 1, 1).astype(BF)
+        return carry
+
+    lax.fori_loop(0, 3, hidden_back, 0)
     gather_n2.middle()
-    drain(ring)
-    gather_n2.late()
+    lax.fori_loop(3, 4, hidden_back, 0)
     net.take(near[0], gw.at[pl.ds(aligned(at.sib, FEAT), FEAT), :])
     net.take(near[1], uw.at[pl.ds(aligned(at.sib, FEAT), FEAT), :])
-    net.take(near[2], dw.at[:, pl.ds(aligned(at.sib, FEAT), FEAT)])
-    gather_n2.end()
-    net.finish()
-
-    @pl.when(chosen)
-    def _():
-        for core in (0, 1):
-            for copy in slice_copies(core, 0, 5):
-                copy.wait_send()
-
-
-def vmem():
-    return pl.BlockSpec(memory_space=pltpu.VMEM)
-
-
-def anywhere():
-    return pl.BlockSpec(memory_space=pl.ANY)
-
-
-def run_forward(x, og, wqkv, wout, wg, wu, wd, gains, bias, cosine, sine):
-    def out(shape, dtype):
-        return jax.ShapeDtypeStruct(shape, dtype)
-
-    outs = (
-        out((BLOCK, MODEL), BF),
-        out((SEQ, FEAT), BF),
-        out((SEQ, MODEL), BF),
-        out((SEQ, MODEL), BF),
-        out((MODEL, QKV), BF),
-        out((QCOLS, MODEL), BF),
-        out((MODEL, PART), BF),
-        out((MODEL, PART), BF),
-        out((PART, MODEL), BF),
-        out((2 * BLOCK, QCOLS), BF),
-        out((SEQ, HEAD), BF),
-        out((SEQ, HEAD), BF),
-        out((2 * HEADS, BLOCK, 1), F32),
-        out((2 * BLOCK, QCOLS), BF),
-        out((BLOCK, MODEL), F32),
-        out((8, MODEL), F32),
-    )
-    return pl.pallas_call(
-        forward_kernel,
-        out_shape=outs,
-        in_specs=[vmem()] * 4 + [anywhere()] * 3 + [vmem()] * 4,
-        out_specs=[vmem()] * len(outs),
-        scratch_shapes=[
-            pltpu.VMEM((SEQ, MODEL), BF),
-            pltpu.VMEM((SEQ, MODEL), BF),
-            pltpu.VMEM((BLOCK, MODEL), BF),
-            pltpu.VMEM((BLOCK, MODEL), BF),
-            pltpu.SemaphoreType.DMA((160,)),
-            pltpu.SemaphoreType.DMA((160,)),
-            pltpu.SemaphoreType.DMA((8,)),
-        ],
-        compiler_params=pltpu.CompilerParams(
-            collective_id=0, has_side_effects=True, vmem_limit_bytes=VMEM_LIMIT
-        ),
-        cost_estimate=pl.CostEstimate(
-            flops=8 * 10**9, bytes_accessed=60 * 10**6, transcendentals=2 * 10**6
-        ),
-        name="attention_forward",
-    )(x, og, wqkv, wout, wg, wu, wd, gains, bias, cosine, sine)
-
-
-class Reduce8:
-    def __init__(self, net, at, own, other, sib_in, first_in, last_in, near_in, away_in):
-        self.net, self.at, self.own, self.other, self.sib_in = net, at, own, other, sib_in
-        self.first_in, self.last_in, self.near_in, self.away_in = first_in, last_in, near_in, away_in
-        self.half = own.shape[1] // 2
-        self.keys = {}
-
-    def put(self, j, mine, theirs):
-        self.own[j] = mine
-        self.other[j] = theirs
-        self.keys[j] = self.net.send(self.other.at[j], self.sib_in.at[j], self.at.S)
-
-    def step(self, j):
-        net, at, half = self.net, self.at, self.half
-        net.take(self.keys[j], self.sib_in.at[j])
-        total = self.own[j].astype(F32) + self.sib_in[j].astype(F32)
-        if j == 0:
-            self.own[j] = total.astype(BF)
-            self.first = net.send(self.own.at[j, pl.ds(0, half)], self.first_in, at.N1)
-            self.last = net.send(self.own.at[j, pl.ds(half, half)], self.last_in, at.N2)
-        elif j == 1:
-            net.take(self.last, self.last_in)
-            self.own[j, :half] = total[:half].astype(BF)
-            self.own[j, half:] = (total[half:] + self.last_in[...].astype(F32)).astype(BF)
-            self.near = net.send(self.own.at[j], self.near_in, at.N1)
-        elif j == 2:
-            net.take(self.first, self.first_in)
-            self.own[j, :half] = (total[:half] + self.first_in[...].astype(F32)).astype(BF)
-            self.own[j, half:] = total[half:].astype(BF)
-            self.away = net.send(self.own.at[j], self.away_in, at.N2)
-        else:
-            net.take(self.near, self.near_in)
-            net.take(self.away, self.away_in)
-            return total + self.near_in[...].astype(F32) + self.away_in[...].astype(F32)
-        return None
-
-
-def reduce8_scratch(rows, columns):
-    return [
-        pltpu.VMEM((4, rows, columns), BF),
-        pltpu.VMEM((4, rows, columns), BF),
-        pltpu.VMEM((4, rows, columns), BF),
-        pltpu.VMEM((rows // 2, columns), BF),
-        pltpu.VMEM((rows // 2, columns), BF),
-        pltpu.VMEM((rows, columns), BF),
-        pltpu.VMEM((rows, columns), BF),
-    ]
-
-
-def tiles_of(width, step):
-    return [(first, min(step, width - first)) for first in range(0, width, step)]
-
-
-def outer_sum(left, right, out):
-    width = right.shape[1]
-    height = left.shape[1] // 2
-
-    def tile(lanes):
-        for i in (0, 1):
-            rows = pl.ds(i * height, height)
-            out[rows, lanes] = dot(left[:, rows], right[:, lanes], 0, 0).astype(BF)
-
-    def step(n, carry):
-        tile(pl.ds(aligned(n, 256), 256))
-        return carry
-
-    lax.fori_loop(0, width // 256, step, 0)
-    if width % 256:
-        tile(pl.ds(width // 256 * 256, width % 256))
-
-
-def ffn_kernel(
-    n2,
-    og,
-    gw,
-    uw,
-    dw,
-    mid_ref,
-    dn2_ref,
-    out_ref,
-    grad_gu,
-    grad_down,
-    hidden,
-    d_gate,
-    d_up,
-    ffn,
-    *rest,
-):
-    red_a, red_b, (send_sems, recv_sems) = rest[:7], rest[7:14], rest[14:]
-    at = Place()
-    net = Net(send_sems, recv_sems, at)
-    at.meet((at.S, at.N1, at.N2))
+
+    net.finish(early)
+    hidden, d_gate = x_all.at[:, pl.ds(0, PART)], n1.at[:, pl.ds(0, PART)]
     norms = Reduce8(net, at, *red_a)
     outs = Reduce8(net, at, *red_b)
     chips = ((at.row, 1 - at.hi), (1 - at.row, at.hi), (1 - at.row, 1 - at.hi), (at.row, at.hi))
@@ -652,13 +620,16 @@
         first = 2 * hi + row * (6 - 4 * hi)
         return pl.ds(aligned(first, BLOCK), 256), at.core + row * (1 - 2 * at.core)
 
-    for j in range(4):
-        rows, place = tokens(j)
+    for j in (3, 1, 2, 0):
+        if j == 0:
+            gather_n2.late()
+        gather_n2.end(j)
+        rows, _ = tokens(j)
         for first, width in tiles_of(PART, 512):
             lanes = pl.ds(first, width)
-            gate = dot(n2[rows, :], gw[:, lanes])
-            up = dot(n2[rows, :], uw[:, lanes])
-            d_hidden = dot(og[rows, :], dw[lanes, :], 1, 1)
+            gate = dot(n2_all[rows, :], gw[:, lanes])
+            up = dot(n2_all[rows, :], uw[:, lanes])
+            d_hidden = d_up[rows, lanes].astype(F32)
             sig = jax.nn.sigmoid(gate)
             act = gate * sig
             d_act = d_hidden * up * sig * (1.0 + gate * (1.0 - sig))
@@ -669,6 +640,8 @@
                 values = [jnp.where(fresh, value, 0.0) for value in values]
             for ref, value in zip((hidden, d_gate, d_up), values, strict=True):
                 ref[rows, lanes] = value.astype(BF)
+    for j in range(4):
+        rows, place = tokens(j)
         own_rows = pl.ds(pl.multiple_of(rows.start + place * BLOCK, BLOCK), BLOCK)
         other_rows = pl.ds(pl.multiple_of(rows.start + (1 - place) * BLOCK, BLOCK), BLOCK)
         parts = [
@@ -679,57 +652,116 @@
         if j:
             norms.step(j - 1)
 
-    outer_sum(hidden, og, grad_down)
-
+    writes = []
+
+    def outer_sum(left, right, out):
+        height = left.shape[1] // 2
+        for first, width in tiles_of(right.shape[1], 256):
+            place = len(writes) % 2
+            if len(writes) > 1:
+                writes[-2].wait()
+            for i in (0, 1):
+                rows = pl.ds(i * height, height)
+                tile_buf[place, rows, :width] = dot(
+                    left[:, rows], right[:, pl.ds(first, width)], 0, 0
+                ).astype(BF)
+            writes.append(
+                pltpu.make_async_copy(
+                    tile_buf.at[place, pl.ds(0, 2 * height), pl.ds(0, width)],
+                    out.at[:, pl.ds(first, width)],
+                    tile_sems.at[place],
+                )
+            )
+            writes[-1].start()
+
+    outer_sum(hidden, og_all, grad_down)
     for j in range(4):
         row, hi = chips[j]
         rows = pl.ds(aligned(row, SEQ // 2), SEQ // 2)
         lanes = pl.ds(aligned(hi, QCOLS), QCOLS)
         ffn[...] = dot(hidden[rows, :], dw[:, lanes])
         if j in (0, 3):
-            mine = pl.ds(pl.multiple_of((at.block - 4 * at.row) * BLOCK, BLOCK), BLOCK)
-            ffn[mine, :] += mid_ref[:, lanes]
+            mine_mid = pl.ds(pl.multiple_of((at.block - 4 * at.row) * BLOCK, BLOCK), BLOCK)
+            ffn[mine_mid, :] += mid_ref[:, lanes]
         own = ffn[:, pl.ds(aligned(at.core, FEAT), FEAT)].astype(BF)
         outs.put(j, own, ffn[:, pl.ds(aligned(1 - at.core, FEAT), FEAT)].astype(BF))
         if j:
             outs.step(j - 1)
         if j == 1:
             dn2_ref[...] = norms.step(3)
-
-    outer_sum(n2, d_gate, grad_gu.at[0])
-    outer_sum(n2, d_up, grad_gu.at[1])
+    outer_sum(n2_all, d_gate, grad_gu.at[0])
+    outer_sum(n2_all, d_up, grad_gu.at[1])
     out_ref[...] = outs.step(3)
+    for copy in writes[-2:]:
+        copy.wait()
+    for copy in local:
+        copy.wait()
     net.finish()
 
-
-def run_ffn(n2, og, gw, uw, dw, mid):
-    def out(shape, dtype):
-        return jax.ShapeDtypeStruct(shape, dtype)
-
+    @pl.when(chosen)
+    def _():
+        for core in (0, 1):
+            for copy in slice_copies(core, 0, 5):
+                copy.wait_send()
+
+
+def run_forward(x, og, wq, wk, wv, wout, wg, wu, wd, gains, bias, cosine, sine):
     outs = (
-        out((BLOCK, MODEL), F32),
-        out((SEQ // 2, FEAT), F32),
-        out((2, MODEL, PART), BF),
-        out((PART, MODEL), BF),
+        ((BLOCK, MODEL), BF, vmem),
+        ((SEQ, FEAT), BF, vmem),
+        ((BLOCK, MODEL), BF, anywhere),
+        ((MODEL, QKV), BF, anywhere),
+        ((QCOLS, MODEL), BF, anywhere),
+        ((2 * BLOCK, QCOLS), BF, vmem),
+        ((SEQ, HEAD), BF, vmem),
+        ((SEQ, HEAD), BF, vmem),
+        ((2 * HEADS, BLOCK, 1), F32, vmem),
+        ((2 * BLOCK, QCOLS), BF, vmem),
+        ((BLOCK, MODEL), F32, vmem),
+        ((8, MODEL), F32, vmem),
+        ((BLOCK, MODEL), F32, vmem),
+        ((SEQ // 2, FEAT), F32, vmem),
+        ((2, MODEL, PART), BF, anywhere),
+        ((PART, MODEL), BF, anywhere),
     )
     return pl.pallas_call(
-        ffn_kernel,
-        out_shape=outs,
-        in_specs=[vmem()] * 6,
-        out_specs=[vmem()] * len(outs),
-        scratch_shapes=[pltpu.VMEM((SEQ, PART), BF)] * 3
-        + [pltpu.VMEM((SEQ // 2, QCOLS), F32)]
+        forward_kernel,
+        out_shape=[jax.ShapeDtypeStruct(dims, dtype) for dims, dtype, _ in outs],
+        in_specs=[anywhere()] * 9 + [vmem()] * 4,
+        out_specs=[place() for _, _, place in outs],
+        scratch_shapes=[
+            pltpu.VMEM((FEAT, QKV), BF),
+            pltpu.VMEM((SEQ, MODEL), BF),
+            pltpu.VMEM((SEQ, MODEL), BF),
+            pltpu.VMEM((SEQ, MODEL), BF),
+            pltpu.VMEM((SEQ, MODEL), BF),
+            pltpu.VMEM((MODEL, QKV), BF),
+            pltpu.VMEM((QCOLS, MODEL), BF),
+            pltpu.VMEM((MODEL, PART), BF),
+            pltpu.VMEM((MODEL, PART), BF),
+            pltpu.VMEM((PART, MODEL), BF),
+            pltpu.VMEM((BLOCK, MODEL), BF),
+            pltpu.VMEM((BLOCK, MODEL), BF),
+            pltpu.VMEM((SEQ, PART), BF),
+            pltpu.VMEM((SEQ // 2, QCOLS), F32),
+            pltpu.VMEM((2, MODEL, 256), BF),
+        ]
         + reduce8_scratch(BLOCK, MODEL)
         + reduce8_scratch(SEQ // 2, FEAT)
-        + [pltpu.SemaphoreType.DMA((32,)), pltpu.SemaphoreType.DMA((32,))],
+        + [
+            pltpu.SemaphoreType.DMA((200,)),
+            pltpu.SemaphoreType.DMA((200,)),
+            pltpu.SemaphoreType.DMA((32,)),
+            pltpu.SemaphoreType.DMA((2,)),
+        ],
         compiler_params=pltpu.CompilerParams(
-            collective_id=1, has_side_effects=True, vmem_limit_bytes=VMEM_LIMIT
+            collective_id=0, has_side_effects=True, vmem_limit_bytes=VMEM_LIMIT
         ),
         cost_estimate=pl.CostEstimate(
-            flops=29 * 10**9, bytes_accessed=60 * 10**6, transcendentals=2 * 10**6
+            flops=37 * 10**9, bytes_accessed=80 * 10**6, transcendentals=4 * 10**6
         ),
-        name="feed_forward",
-    )(n2, og, gw, uw, dw, mid)
+        name="forward_and_feed_forward",
+    )(x, og, wq, wk, wv, wout, wg, wu, wd, gains, bias, cosine, sine)
 
 
 def add_up(out, terms):
@@ -973,7 +1005,7 @@
     sums_ref[...] = jnp.zeros_like(sums_ref)
     sums_ref[1:2, :] = jnp.sum(d_normed * unit, axis=0, keepdims=True)
     bent = d_normed * gain2
-    d_mid[...] = og_ref[rows_at(at.block), :].astype(F32) + scale * (
+    d_mid[...] = og_ref[...].astype(F32) + scale * (
         bent - unit * jnp.mean(bent * unit, axis=1, keepdims=True)
     )
     mid_pair[at.row] = d_mid[...].astype(BF)
@@ -1372,19 +1404,14 @@
     out_grad,
 ):
     cosine, sine = rope_tables(SEQ)
-    w_qkv = jnp.concatenate([w_query, w_key, w_value], axis=1)
     bias = jnp.concatenate([b_query, b_key, b_value]).astype(F32)[None]
     gains = jnp.zeros((8, FEAT), F32).at[0].set(gain_attn.astype(F32)).at[1].set(gain_ffn.astype(F32))
     (
         xs,
         normed1_cols,
-        grads_all,
-        normed2_all,
+        grads_block,
         qkv_w,
         out_w,
-        gate_w,
-        up_w,
-        down_w,
         queries,
         key,
         value,
@@ -1392,16 +1419,29 @@
         attn,
         mid,
         gains_all,
+        dn2,
+        layer_output,
+        grad_gu,
+        grad_down,
     ) = run_forward(
-        layer_input, out_grad, w_qkv, w_out, w_gate, w_up, w_down, gains, bias, cosine, sine
-    )
-    dn2, layer_output, grad_gu, grad_down = run_ffn(
-        normed2_all, grads_all, gate_w, up_w, down_w, mid
+        layer_input,
+        out_grad,
+        w_query,
+        w_key,
+        w_value,
+        w_out,
+        w_gate,
+        w_up,
+        w_down,
+        gains,
+        bias,
+        cosine,
+        sine,
     )
     grad_input, grad_out, grad_qkv, small, grad_gu, grad_down = run_backward(
         dn2,
         mid,
-        grads_all,
+        grads_block,
         gains_all,
         xs,
         normed1_cols,

time: 403 us -> 383 us (0.950)
  Pallas kernels: 377 us -> 362 us
    pallas_call x2 -> x1, Pallas kernels: 178 us -> 160 us  [run_forward(): pl.pallas_call(forward_kernel, out_shape=[jax.ShapeDtypeStruct(dims, dtyp...]
where the time goes in v4:
time: 383 us; the launch traced here: 376 us
  Pallas kernels  362 us (95%)
  local copies, waits for them, and re-layouts  7.68 us (2%)
  other arithmetic  4.92 us (1%)
    pallas_call x1, Pallas kernels, run_forward(): pl.pallas_call(forward_kernel, out_shape=[jax.ShapeDtypeStruct(dims, dtyp...  160 us
    pallas_call x1, Pallas kernels, run_sums(): pl.pallas_call(sums_kernel, out_shape=outs, in_specs=[vmem()] * 5, out_sp...  97.3 us
    pallas_call x1, Pallas kernels, run_backward(): pl.pallas_call(backward_kernel, out_shape=outs, in_specs=[vmem()] * len(a...  93.2 us
    pallas_call x1, Pallas kernels, run_widen(): pl.pallas_call(widen_kernel, out_shape=outs, in_specs=[vmem()] * 2, out_s...  11.3 us

profile of v4, /device:TPU:0, one launch (start us, length us, event | category | flops | bytes accessed | tf_op | source)
XLA Modules:
  0.0 376.2 jit_solution(898589223322490182)
XLA Ops:
  0.6 0.0 copy-start.6
  0.7 0.0 copy-start.7
  0.7 0.0 copy-start.5
  0.7 0.0 copy-start.9
  0.7 0.0 copy-start.8
  0.7 1.9 fusion
  2.6 1.3 pad_maximum_fusion
  3.9 0.0 copy-done.6
  4.0 0.0 copy-done.7
  4.0 0.0 copy-done.5
  4.0 0.0 copy-start.4
  4.1 0.0 copy-done.9
  4.1 0.0 copy-done.8
  4.1 0.6 maximum_convert_fusion.bias_ref
  4.7 0.0 copy-done.4
  4.7 160.5 %forward_and_feed_forward.1 = (bf16[128,1536]{1,0:T(8,128)(2,1)}, bf16[1024,384]{1,0:T(8,128)(2,1)}, bf16[128,1536]{1,0:T(8,128)(2,1)}, bf16[1536,1024]{1,0:T(8,...) custom-call(bf16[512,384]{1,0:T(8,128)(2,1)} %x_ref.1, ...), custom_call_target="tpu_custom_call" | custom-call | flops 36999999488 | bytes 80000000 | tf_op jit(solution)/shard_map/forward_and_feed_forward/pallas_call | solution.py:727
  165.1 93.2 %attention_backward.1 = (f32[512,384]{1,0:T(8,128)}, bf16[768,384]{1,0:T(8,128)(2,1)}, bf16[384,1024]{1,0:T(8,128)(2,1)}, f32[8,1408]{1,0:T(8,128)}, bf16[4,48,1...) custom-call(f32[128,1536]{1,0:T(8,128)} %get-tuple-element.69.dn2_ref, f32[128,1536]{1,0:T(8,128)} %get-tuple-element.70.mid_ref, ...), custom_call_target="tpu_custom_call" | custom-call | flops 10000000000 | bytes 40000000 | tf_op jit(solution)/shard_map/attention_backward/pallas_call | solution.py:1152
  258.4 97.3 %sums_over_sequences.1 = (bf16[2,384,4608]{2,1,0:T(8,128)(2,1)}, bf16[4,1280,384]{2,1,0:T(8,128)(2,1)}, bf16[384,1024]{1,0:T(8,128)(2,1)}, bf16[768,384]{1,0:T(8,128)(2,1)}, f32[8,1408]{1,0:T(8,128)}) custom-call(bf16[4,48,1152]{2,1,0:T(8,128)(2,1)} %get-tuple-element.85.gu_own, bf16[80,1536]{1,0:T(8,128)(2,1)} %get-tuple-element.86.down_own, ...), custom_call_target="tpu_custom_call" | custom-call | flops 100000000 | bytes 60000000 | tf_op jit(solution)/shard_map/sums_over_sequences/pallas_call | solution.py:1300
  355.7 0.0 copy-start.3
  355.7 0.0 copy-start
  355.7 11.3 %widen.1 = (f32[384,4480]{1,0:T(8,128)}, f32[384,4480]{1,0:T(8,128)}, f32[4480,384]{1,0:T(8,128)}) custom-call(bf16[2,384,4608]{2,1,0:T(8,128)(2,1)} %get-tuple-element.93.gu, bf16[4,1280,384]{2,1,0:T(8,128)(2,1)} %get-tuple-element.94.down), custom_call_target="tpu_custom_call" | custom-call | flops 10000000 | bytes 36000000 | tf_op jit(solution)/shard_map/widen/pallas_call | solution.py:1363
  367.1 0.0 copy-start.1
  367.1 0.0 copy-start.2
  367.1 0.0 copy-done.3
  367.1 1.1 convert_element_type.48
  368.2 1.1 slice.61
  369.3 0.8 fusion.1
  370.1 1.4 slice_reduce_fusion.1
  371.4 1.3 slice_reduce_fusion
  372.8 1.2 slice_bitcast_fusion
  374.0 0.9 copy.31
  374.9 0.9 copy.32
  (10 shorter events, 0.1 us)
Async XLA Ops:
  0.6 3.3 copy-start.6
  0.7 3.3 copy-start.7
  0.7 3.4 copy-start.5
  0.7 3.4 copy-start.9
  0.7 3.4 copy-start.8
  4.0 0.6 copy-start.4
  355.7 11.4 %copy-start.3 = (bf16[768,384]{1,0:T(8,128)(2,1)S(1)}, bf16[768,384]{1,0:T(8,128)(2,1)}, u32[]{:S(2)}) copy-start(bf16[768,384]{1,0:T(8,128)(2,1)} %get-tuple-element.92) | copy-start | bytes 1769476
  355.7 12.5 %copy-start = (bf16[384,1024]{1,0:T(8,128)(2,1)S(1)}, bf16[384,1024]{1,0:T(8,128)(2,1)}, u32[]{:S(2)}) copy-start(bf16[384,1024]{1,0:T(8,128)(2,1)} %get-tuple-element.91) | copy-start | bytes 2359300
  367.1 6.9 %copy-start.1 = (f32[512,384]{1,0:T(8,128)S(1)}, f32[512,384]{1,0:T(8,128)}, u32[]{:S(2)}) copy-start(f32[512,384]{1,0:T(8,128)} %get-tuple-element.123) | copy-start | bytes 2359300
  367.1 7.8 %copy-start.2 = (f32[512,384]{1,0:T(8,128)S(1)}, f32[512,384]{1,0:T(8,128)}, u32[]{:S(2)}) copy-start(f32[512,384]{1,0:T(8,128)} %get-tuple-element.124) | copy-start | bytes 2359300

commit v5 on v4

--- a/solution.py
+++ b/solution.py
@@ -2,6 +2,7 @@
 
 import jax
 import jax.numpy as jnp
+import numpy as np
 from jax import lax
 from jax.experimental import pallas as pl
 from jax.experimental.pallas import tpu as pltpu
@@ -154,7 +155,7 @@
             net.take(self.f4, place(at.row, at.sibfar, 1))
 
 
-def ring_dp(net, at, halves):
+def ring_dp(net, at, halves, ready=(None, None)):
     def wrap(index):
         return lax.rem(index + 4, 4)
 
@@ -173,9 +174,14 @@
 
     one, two, onward = {}, {}, {}
     for i in (0, 1):
+        if ready[i]:
+            ready[i]()
         one[i] = [send(i, firsts[i], seconds[i], side) for side in sides[i][0]]
+        if ready[i]:
+            two[i, 0] = [send(i, firsts[i], seconds[i], side) for side in sides[i][1]]
     for i in (0, 1):
-        two[i, 0] = [send(i, firsts[i], seconds[i], side) for side in sides[i][1]]
+        if not ready[i]:
+            two[i, 0] = [send(i, firsts[i], seconds[i], side) for side in sides[i][1]]
     yield
     for i in (0, 1):
         minus = wrap(firsts[i] - 1)
@@ -792,8 +798,8 @@
 
 
 class RingItem:
-    def __init__(self, net, sides, place, part, way, bufs, own):
-        self.net, self.part, self.own = net, part, own
+    def __init__(self, net, sides, place, part, held, way, bufs, own):
+        self.net, self.part, self.held, self.own = net, part, held, own
         self.relay, self.staged, self.from_last, self.from_next = bufs
         self.onward, self.back = (sides[0], sides[1]) if way == 0 else (sides[1], sides[0])
         step = 1 - 2 * way
@@ -809,13 +815,13 @@
 
     def middle(self):
         self.net.take(self.k_relay, self.relay)
-        add_up(self.staged, [self.part(self.next), self.relay])
+        add_up(self.staged, [self.held(self.next), self.relay])
         self.k_last = self.net.send(self.staged, self.from_last, self.onward)
 
     def end(self):
         self.net.take(self.k_next, self.from_next)
         self.net.take(self.k_last, self.from_last)
-        add_up(self.own, [self.part(self.here), self.from_next, self.from_last])
+        add_up(self.own, [self.held(self.here), self.from_next, self.from_last])
 
 
 def begin(items):
@@ -847,7 +853,7 @@
     return scratch
 
 
-def ring_items(net, at, first, last, parts, seconds, finals, bufs):
+def ring_items(net, at, first, last, parts, helds, seconds, finals, bufs):
     sides = (((at.YP, at.YM), (at.ZP, at.ZM)), ((at.ZP, at.ZM), (at.YP, at.YM)))
     places = ((at.y, at.z), (at.z, at.y))
     bufs = list(bufs)
@@ -858,16 +864,17 @@
             own = bufs[8]
             for way in (0, 1):
                 part = functools.partial(lambda k, f, w: f(k, w), f=parts[i][n], w=way)
+                held = functools.partial(lambda k, f, w: f(k, w), f=helds[i][n], w=way)
                 four = bufs[4 * way : 4 * way + 4]
                 one[i].append(
-                    RingItem(net, sides[i][0], places[i][0], part, way, four, own.at[way])
+                    RingItem(net, sides[i][0], places[i][0], part, held, way, four, own.at[way])
                 )
             owns.append(own)
             bufs = bufs[9:]
         for n in range(len(last[i])):
             part = functools.partial(lambda k, f, o: f(o, k), f=seconds[i][n], o=owns[n])
             two[i].append(
-                RingItem(net, sides[i][1], places[i][1], part, n % 2, bufs[:4], finals[i][n])
+                RingItem(net, sides[i][1], places[i][1], part, part, n % 2, bufs[:4], finals[i][n])
             )
             bufs = bufs[4:]
 
@@ -877,17 +884,20 @@
     return mix(one), mix(two)
 
 
-def ffn_items(net, at, gu, down, gu_own, down_own, bufs):
-    parts = (
-        (
-            lambda k, way: gu.at[way, pl.ds(0, 2), :, k],
-            lambda k, way: down.at[way, :, down_rows(k), LEFT],
-        ),
-        (
-            lambda k, way: gu.at[k // 2, pl.ds(2, 2), k % 2, pl.ds(2 * way, 2)],
-            lambda k, way: down.at[k // 2, k % 2, pl.ds(144 * way, 144), RIGHT],
-        ),
-    )
+def ffn_items(net, at, far_refs, near_refs, gu_own, down_own, bufs):
+    def parts_of(gu, down):
+        return (
+            (
+                lambda k, way: gu.at[way, pl.ds(0, 2), :, k],
+                lambda k, way: down.at[way, :, down_rows(k), LEFT],
+            ),
+            (
+                lambda k, way: gu.at[k // 2, pl.ds(2, 2), k % 2, pl.ds(2 * way, 2)],
+                lambda k, way: down.at[k // 2, k % 2, pl.ds(144 * way, 144), RIGHT],
+            ),
+        )
+
+    parts, helds = parts_of(*far_refs), parts_of(*near_refs)
     seconds = (
         (lambda own, k: own.at[k // 2, :, k % 2], lambda own, k: own.at[k // 2, k % 2]),
         (
@@ -899,7 +909,7 @@
         (gu_own.at[pl.ds(0, 2)], down_own.at[:, LEFT]),
         (gu_own.at[pl.ds(2, 2)], down_own.at[:, RIGHT]),
     )
-    return ring_items(net, at, FFN_FIRST, FFN_LAST, parts, seconds, finals, bufs)
+    return ring_items(net, at, FFN_FIRST, FFN_LAST, parts, helds, seconds, finals, bufs)
 
 
 def small_items(net, at, qkv, out, qkv_own, out_own, bufs):
@@ -909,7 +919,7 @@
     )
     seconds = ((lambda own, k: own.at[k // 2, k % 2],), (lambda own, k: own.at[k // 2, k % 2],))
     finals = ((qkv_own,), (out_own,))
-    return ring_items(net, at, SMALL_FIRST, SMALL_LAST, parts, seconds, finals, bufs)
+    return ring_items(net, at, SMALL_FIRST, SMALL_LAST, parts, parts, seconds, finals, bufs)
 
 
 def backward_kernel(
@@ -924,12 +934,12 @@
     k_ref,
     v_ref,
     lse_ref,
-    ow,
-    qw,
     cos_ref,
     sin_ref,
-    gu,
-    down,
+    ow_far,
+    qw_far,
+    gu_far,
+    down_far,
     grad_in,
     grad_out,
     grad_qkv,
@@ -952,15 +962,27 @@
     part_in,
     gi_out,
     gi_in,
+    ow,
+    qw,
+    gu,
+    down,
     *rest,
 ):
-    bufs, (send_sems, recv_sems) = rest[:-2], rest[-2:]
+    bufs, (send_sems, recv_sems, local_sems) = rest[:-3], rest[-3:]
     at = Place()
     net = Net(send_sems, recv_sems, at)
+    held = [
+        pltpu.make_async_copy(src, dst, local_sems.at[i])
+        for i, (src, dst) in enumerate(
+            ((ow_far, ow), (gu_far, gu), (down_far, down), (qw_far, qw))
+        )
+    ]
+    for copy in held:
+        copy.start()
     at.meet(
         (at.S, at.O, at.OS, at.N1, at.N2, at.N1S, at.N2S, at.YP, at.YM, at.ZP, at.ZM)
     )
-    first, last = ffn_items(net, at, gu, down, gu_own, down_own, bufs)
+    first, last = ffn_items(net, at, (gu_far, down_far), (gu, down), gu_own, down_own, bufs)
     begin(first)
     peers = ((at.S, at.sib), (at.O, at.far), (at.OS, at.sibfar))
     pair = (at.col, 7 - at.col)
@@ -1029,9 +1051,12 @@
         )
     gather_attn.start()
     net.take(to_pair, mid_pair.at[1 - at.row])
+    held[0].wait()
     for j in (0, 1):
         d_attn[pl.ds(j * BLOCK, BLOCK), :] = dot(mid_pair[j], ow[...], 1, 1).astype(BF)
     d_kv[...] = jnp.zeros_like(d_kv)
+    held[1].wait()
+    held[2].wait()
     for item in first:
         item.middle()
 
@@ -1092,6 +1117,7 @@
     gather_qkv = GatherCol(d_qkv_all)
     gather_qkv.start()
 
+    held[3].wait()
     part_out[...] = dot(d_qkv_all[rows_at(block_of(1 - at.row, at.col)), :], qw[...], 1, 1).astype(BF)
     part = net.send(part_out, part_in, at.N1)
     d_normed = dot(d_qkv_all[rows_at(at.block), :], qw[...], 1, 1)
@@ -1152,7 +1178,7 @@
     return pl.pallas_call(
         backward_kernel,
         out_shape=outs,
-        in_specs=[vmem()] * len(args),
+        in_specs=[vmem()] * (len(args) - 4) + [anywhere()] * 4,
         out_specs=[vmem()] * len(outs),
         scratch_shapes=[
             pltpu.VMEM((8, MODEL), F32),
@@ -1171,9 +1197,14 @@
             pltpu.VMEM((BLOCK, MODEL), BF),
             pltpu.VMEM((BLOCK, MODEL), BF),
             pltpu.VMEM((SEQ // 2, FEAT), BF),
+            pltpu.VMEM((QCOLS, MODEL), BF),
+            pltpu.VMEM((MODEL, QKV), BF),
+            pltpu.VMEM((2, 4, 2, 4, 48, PART), BF),
+            pltpu.VMEM((2, 2, 288, MODEL), BF),
         ]
         + ring_scratch(FFN_FIRST, FFN_LAST)
-        + [pltpu.SemaphoreType.DMA((80,)), pltpu.SemaphoreType.DMA((80,))],
+        + [pltpu.SemaphoreType.DMA((80,)), pltpu.SemaphoreType.DMA((80,))]
+        + [pltpu.SemaphoreType.DMA((4,))],
         compiler_params=pltpu.CompilerParams(
             collective_id=2, has_side_effects=True, vmem_limit_bytes=VMEM_LIMIT
         ),
@@ -1199,7 +1230,7 @@
     small_z,
     *rest,
 ):
-    bufs, (send_sems, recv_sems) = rest[:-2], rest[-2:]
+    bufs, (send_sems, recv_sems, local_sems) = rest[:-3], rest[-3:]
     at = Place()
     net = Net(send_sems, recv_sems, at)
     at.meet((at.S, at.O, at.OS, at.YP, at.YM, at.ZP, at.ZM, at.Y2, at.Z2))
@@ -1211,9 +1242,6 @@
 
     def part_lanes(col):
         return pl.ds(aligned(col, PART), PART)
-
-    def down_piece(k):
-        return all_down.at[:, pl.ds(pl.multiple_of(k * 80, 16), 80), :]
 
     def down_slot(col):
         return all_down.at[col, pl.ds(pl.multiple_of(at.dp * 80, 16), 80), :]
@@ -1241,19 +1269,44 @@
     small_keys = [net.send(small_ref, small_y.at[y], d) for d in (at.YP, at.YM, at.Y2)]
     first, last = small_items(net, at, qkv, out, qkv_piece(at.dp), out_piece(at.dp), bufs)
     begin(first)
-    gu_piece(at.dp, part_lanes(at.col))[...] = gu_own[at.col]
-    down_slot(at.col)[...] = down_own[:, feat_lanes(at.col)]
-    for (one, two), (_, col) in zip(keys, peers, strict=True):
-        net.take(one, gu_piece(at.dp, part_lanes(col)))
-        net.take(two, down_slot(col))
-
-    def half0(zz, yy):
-        return [gu_piece(zz * 4 + yy, pl.ds(0, 3456))]
-
-    def half1(zz, yy):
-        return [gu_piece(zz * 4 + yy, pl.ds(3456, 1152)), down_piece(zz * 4 + yy)]
-
-    ring = ring_dp(net, at, (half0, half1))
+    own_copies = [
+        pltpu.make_async_copy(
+            gu_own.at[at.col], gu_piece(at.dp, part_lanes(at.col)), local_sems.at[0]
+        ),
+        pltpu.make_async_copy(
+            down_own.at[:, feat_lanes(at.col)], down_slot(at.col), local_sems.at[1]
+        ),
+    ]
+    for copy in own_copies:
+        copy.start()
+
+    def take_from(i):
+        net.take(keys[i][0], gu_piece(at.dp, part_lanes(peers[i][1])))
+        net.take(keys[i][1], down_slot(peers[i][1]))
+
+    def chip_ready():
+        for copy in own_copies:
+            copy.wait()
+        take_from(2)
+
+    def far_ready():
+        take_from(0)
+        take_from(1)
+
+    def half_of(hi):
+        def half(zz, yy):
+            k = zz * 4 + yy
+            rows = pl.ds(pl.multiple_of(k * 80, 16), 80)
+            return [
+                gu_piece(k, pl.ds(aligned(hi, 2 * PART), 2 * PART)),
+                all_down.at[pl.ds(2 * hi, 2), rows, :],
+            ]
+
+        return half
+
+    ring = ring_dp(
+        net, at, (half_of(at.hi), half_of(1 - at.hi)), (chip_ready, far_ready)
+    )
     next(ring)
     for item in first:
         item.middle()
@@ -1301,10 +1354,11 @@
         sums_kernel,
         out_shape=outs,
         in_specs=[vmem()] * 5,
-        out_specs=[vmem()] * len(outs),
+        out_specs=[anywhere()] * 2 + [vmem()] * 3,
         scratch_shapes=[pltpu.VMEM((4,) + small.shape, F32)] * 2
         + ring_scratch(SMALL_FIRST, SMALL_LAST)
-        + [pltpu.SemaphoreType.DMA((128,)), pltpu.SemaphoreType.DMA((128,))],
+        + [pltpu.SemaphoreType.DMA((128,)), pltpu.SemaphoreType.DMA((128,))]
+        + [pltpu.SemaphoreType.DMA((2,))],
         compiler_params=pltpu.CompilerParams(
             collective_id=3, has_side_effects=True, vmem_limit_bytes=VMEM_LIMIT
         ),
@@ -1315,60 +1369,120 @@
     )(gu, down, qkv, out, small)
 
 
-def widen_kernel(gu, down, gate_out, up_out, down_out, gate_buf, up_buf, down_buf, sems):
+def widen_kernel(
+    gu,
+    down,
+    qkv,
+    out,
+    small,
+    gate_out,
+    up_out,
+    down_out,
+    query_out,
+    key_out,
+    value_out,
+    proj_out,
+    gain1_out,
+    gain2_out,
+    bq_out,
+    bk_out,
+    bv_out,
+    gu_in,
+    down_in,
+    gate_buf,
+    up_buf,
+    down_buf,
+    in_sems,
+    out_sems,
+):
     skip = 3 * PART
-    slots = [None, None]
-
-    def chunk(n):
+
+    def loads(n):
+        place = n % 2
+        rows = pl.ds(640 * (n % 2), 640)
+        return [
+            pltpu.make_async_copy(gu.at[:, pl.ds(n * 48, 48), :], gu_in.at[place], in_sems.at[place, 0]),
+            pltpu.make_async_copy(down.at[n // 2, rows, :], down_in.at[place], in_sems.at[place, 1]),
+        ]
+
+    def stores(n):
+        place, quarter, part = n % 2, n // 2, n % 2
         rows = pl.ds(n * 48, 48)
-        place = n % 2
-        if slots[place] is not None:
-            for copy in slots[place]:
-                copy.wait()
-        copies = []
-        for i, (buf, out) in enumerate(((gate_buf, gate_out), (up_buf, up_out))):
-            buf[place, :, :skip] = gu[i, rows, :skip].astype(F32)
-            buf[place, :, skip:] = gu[i, rows, skip + HEAD :].astype(F32)
-            copies.append(pltpu.make_async_copy(buf.at[place], out.at[rows, :], sems.at[place, i]))
-        quarter, part = n // 2, n % 2
-        for m in range(4):
-            slot = 160 * (4 * part + m)
-            down_buf[place, pl.ds(144 * m, 80), :] = down[quarter, pl.ds(slot, 80), :].astype(F32)
-            down_buf[place, pl.ds(144 * m + 80, 64), :] = down[
-                quarter, pl.ds(slot + 96, 64), :
-            ].astype(F32)
         drop = HEAD if quarter == 3 and part == 0 else 0
         start = PART * quarter + 576 * part - (HEAD if quarter == 3 and part == 1 else 0)
-        copies.append(
+        return [
+            pltpu.make_async_copy(gate_buf.at[place], gate_out.at[rows, :], out_sems.at[place, 0]),
+            pltpu.make_async_copy(up_buf.at[place], up_out.at[rows, :], out_sems.at[place, 1]),
             pltpu.make_async_copy(
                 down_buf.at[place, pl.ds(drop, 576 - drop), :],
                 down_out.at[pl.ds(start, 576 - drop), :],
-                sems.at[place, 2],
-            )
-        )
+                out_sems.at[place, 2],
+            ),
+        ]
+
+    def run(copies):
         for copy in copies:
             copy.start()
-        slots[place] = copies
-
-    for n in range(8):
-        chunk(n)
-    for copies in slots:
+        return copies
+
+    def wait(copies):
         for copy in copies:
             copy.wait()
 
-
-def run_widen(gu, down):
-    outs = [jax.ShapeDtypeStruct((FEAT, UNITS), F32)] * 2
-    outs.append(jax.ShapeDtypeStruct((UNITS, FEAT), F32))
+    arriving = {0: run(loads(0)), 1: run(loads(1))}
+    query_out[...] = qkv[:, :QCOLS].astype(F32)
+    key_out[...] = qkv[:, QCOLS : QCOLS + HEAD].astype(F32)
+    value_out[...] = qkv[:, QCOLS + HEAD :].astype(F32)
+    proj_out[...] = out[...].astype(F32)
+    first = 0
+    for ref, row, width in (
+        (gain1_out, 0, FEAT),
+        (bq_out, 0, QCOLS),
+        (bk_out, 0, HEAD),
+        (bv_out, 0, HEAD),
+    ):
+        ref[...] = small[row : row + 1, first : first + width]
+        first += width
+    gain2_out[...] = small[1:2, :FEAT]
+    leaving = {}
+    for n in range(8):
+        place = n % 2
+        wait(arriving[n])
+        if n > 1:
+            wait(leaving[n - 2])
+        for i, buf in enumerate((gate_buf, up_buf)):
+            buf[place, :, :skip] = gu_in[place, i, :, :skip].astype(F32)
+            buf[place, :, skip:] = gu_in[place, i, :, skip + HEAD :].astype(F32)
+        for m in range(4):
+            down_buf[place, pl.ds(144 * m, 80), :] = down_in[
+                place, pl.ds(160 * m, 80), :
+            ].astype(F32)
+            down_buf[place, pl.ds(144 * m + 80, 64), :] = down_in[
+                place, pl.ds(160 * m + 96, 64), :
+            ].astype(F32)
+        leaving[n] = run(stores(n))
+        if n + 2 < 8:
+            arriving[n + 2] = run(loads(n + 2))
+    wait(leaving[6])
+    wait(leaving[7])
+
+
+def run_widen(gu, down, qkv, out, small):
+    shapes = [(FEAT, UNITS)] * 2 + [(UNITS, FEAT)]
+    shapes += [(FEAT, QCOLS), (FEAT, HEAD), (FEAT, HEAD), (QCOLS, FEAT)]
+    shapes += [(1, FEAT), (1, FEAT), (1, QCOLS), (1, HEAD), (1, HEAD)]
     return pl.pallas_call(
         widen_kernel,
-        out_shape=outs,
-        in_specs=[vmem()] * 2,
-        out_specs=[anywhere()] * 3,
+        out_shape=[jax.ShapeDtypeStruct(dims, F32) for dims in shapes],
+        in_specs=[anywhere()] * 2 + [vmem()] * 3,
+        out_specs=[anywhere()] * 3 + [vmem()] * 9,
         scratch_shapes=[
+            pltpu.VMEM((2, 2, 48, 4 * PART), BF),
+            pltpu.VMEM((2, 640, FEAT), BF),
             pltpu.VMEM((2, 48, UNITS), F32),
             pltpu.VMEM((2, 48, UNITS), F32),
             pltpu.VMEM((2, 576, FEAT), F32),
+            pltpu.SemaphoreType.DMA((2, 2)),
             pltpu.SemaphoreType.DMA((2, 3)),
         ],
         compiler_params=pltpu.CompilerParams(vmem_limit_bytes=VMEM_LIMIT),
@@ -1376,15 +1490,16 @@
             flops=10**7, bytes_accessed=36 * 10**6, transcendentals=0
         ),
         name="widen",
-    )(gu, down)
+    )(gu, down, qkv, out, small)
 
 
 def rope_tables(count):
-    places = jnp.arange(count, dtype=jnp.int32).astype(F32)
-    inverse = 1.0 / THETA ** (jnp.arange(0, HEAD, 2).astype(F32) / HEAD)
+    places = np.arange(count, dtype=np.float32)
+    inverse = (1.0 / THETA ** (np.arange(0, HEAD, 2) / HEAD)).astype(np.float32)
     angles = places[:, None] * inverse[None, :]
-    cosine, sine = jnp.cos(angles), jnp.sin(angles)
-    return jnp.concatenate([cosine, cosine], axis=-1), jnp.concatenate([-sine, sine], axis=-1)
+    cosine, sine = np.cos(angles), np.sin(angles)
+    tables = np.concatenate([cosine, cosine], axis=-1), np.concatenate([-sine, sine], axis=-1)
+    return tuple(jnp.asarray(table, F32) for table in tables)
 
 
 def body(
@@ -1450,10 +1565,10 @@
         key,
         value,
         lse,
+        cosine,
+        sine,
         out_w,
         qkv_w,
-        cosine,
-        sine,
         grad_gu.reshape(2, 4, 2, 4, 48, PART),
         grad_down.reshape(2, 2, 288, MODEL),
     )
@@ -1464,21 +1579,29 @@
         grad_out.reshape(2, 2, 4, 48, FEAT),
         small,
     )
-    grad_gate, grad_up, grad_down = run_widen(grad_gu, grad_down)
-    grad_qkv = grad_qkv.astype(F32)
-    key_end, bias_start = QCOLS + HEAD, FEAT + QCOLS
+    (
+        grad_gate,
+        grad_up,
+        grad_down,
+        grad_query,
+        grad_key,
+        grad_value,
+        grad_out,
+        *vectors,
+    ) = run_widen(grad_gu, grad_down, grad_qkv, grad_out, small)
+    gain1, gain2, bias_query, bias_key, bias_value = (vector[0] for vector in vectors)
     return (
         layer_output,
         grad_input,
-        small[0, :FEAT],
-        grad_qkv[:, :QCOLS],
-        grad_qkv[:, QCOLS:key_end],
-        grad_qkv[:, key_end:],
-        small[0, FEAT:bias_start],
-        small[0, bias_start : bias_start + HEAD],
-        small[0, bias_start + HEAD :],
-        grad_out.astype(F32),
-        small[1, :FEAT],
+        gain1,
+        grad_query,
+        grad_key,
+        grad_value,
+        bias_query,
+        bias_key,
+        bias_value,
+        grad_out,
+        gain2,
         grad_gate,
         grad_up,
         grad_down,

time: 383 us -> 371 us (0.969)
  Pallas kernels: 362 us -> 355 us
    pallas_call x1, Pallas kernels: 97.3 us -> 90.9 us  [run_sums(): pl.pallas_call(sums_kernel, out_shape=outs, in_specs=[vmem()] * 5, out_sp...]
    slice x4 -> x0, local copies, waits for them, and re-layouts: 4.58 us -> none  [the longest x1 1.38 us: body(): small[1, :FEAT]]
    pallas_call x0 -> x3, other arithmetic: none -> 3.84 us  [run_widen(): pl.pallas_call(widen_kernel, out_shape=[jax.ShapeDtypeStruct(dims, F32) f...]
where the time goes in v5:
time: 371 us; the launch traced here: 366 us
  Pallas kernels  355 us (96%)
  other arithmetic  5.11 us (1%)
  local copies, waits for them, and re-layouts  4.44 us (1%)
    pallas_call x1, Pallas kernels, run_forward(): pl.pallas_call(forward_kernel, out_shape=[jax.ShapeDtypeStruct(dims, dtyp...  160 us
    pallas_call x1, Pallas kernels, run_sums(): pl.pallas_call(sums_kernel, out_shape=outs, in_specs=[vmem()] * 5, out_sp...  90.9 us
    pallas_call x1, Pallas kernels, run_backward(): pl.pallas_call(backward_kernel, out_shape=outs, in_specs=[vmem()] * (len(...  88.8 us
    pallas_call x1, Pallas kernels, run_widen(): pl.pallas_call(widen_kernel, out_shape=[jax.ShapeDtypeStruct(dims, F32) f...  15.1 us

profile of v5, /device:TPU:0, one launch (start us, length us, event | category | flops | bytes accessed | tf_op | source)
XLA Modules:
  0.0 365.8 jit_solution(14027340903199916725)
XLA Ops:
  0.6 0.7 reshape.136
  1.3 0.7 reshape.142
  2.0 0.7 concatenate.20
  2.7 1.3 maximum_convert_fusion.bias_ref
  4.0 0.0 copy-start.2
  4.0 0.6 copy-done.2
  4.6 160.4 %forward_and_feed_forward.1 = (bf16[128,1536]{1,0:T(8,128)(2,1)}, bf16[1024,384]{1,0:T(8,128)(2,1)}, bf16[128,1536]{1,0:T(8,128)(2,1)}, bf16[1536,1024]{1,0:T(8,...) custom-call(bf16[512,384]{1,0:T(8,128)(2,1)} %x_ref.1, ...), custom_call_target="tpu_custom_call" | custom-call | flops 36999999488 | bytes 80000000 | tf_op jit(solution)/shard_map/forward_and_feed_forward/pallas_call | solution.py:733
  165.0 88.8 %attention_backward.1 = (f32[512,384]{1,0:T(8,128)}, bf16[768,384]{1,0:T(8,128)(2,1)}, bf16[384,1024]{1,0:T(8,128)(2,1)}, f32[8,1408]{1,0:T(8,128)}, bf16[4,48,1...) custom-call(f32[128,1536]{1,0:T(8,128)} %get-tuple-element.78.dn2_ref, f32[128,1536]{1,0:T(8,128)} %get-tuple-element.79.mid_ref, ...), custom_call_target="tpu_custom_call" | custom-call | flops 10000000000 | bytes 40000000 | tf_op jit(solution)/shard_map/attention_backward/pallas_call | solution.py:1178
  253.8 90.9 %sums_over_sequences.1 = (bf16[2,384,4608]{2,1,0:T(8,128)(2,1)}, bf16[4,1280,384]{2,1,0:T(8,128)(2,1)}, bf16[384,1024]{1,0:T(8,128)(2,1)}, bf16[768,384]{1,0:T(8,128)(2,1)}, f32[8,1408]{1,0:T(8,128)}) custom-call(bf16[4,48,1152]{2,1,0:T(8,128)(2,1)} %get-tuple-element.94.gu_own, bf16[80,1536]{1,0:T(8,128)(2,1)} %get-tuple-element.95.down_own, ...), custom_call_target="tpu_custom_call" | custom-call | flops 100000000 | bytes 60000000 | tf_op jit(solution)/shard_map/sums_over_sequences/pallas_call | solution.py:1353
  344.7 0.0 copy-start
  344.7 0.0 copy-start.1
  344.7 15.1 %widen.1 = (f32[384,4480]{1,0:T(8,128)}, f32[384,4480]{1,0:T(8,128)}, f32[4480,384]{1,0:T(8,128)}, f32[384,768]{1,0:T(8,128)}, f32[384,128]{1,0:T(8,128)}, /*ind...) custom-call(bf16[2,384,4608]{2,1,0:T(8,128)(2,1)} %get-tuple-element, ...), custom_call_target="tpu_custom_call" | custom-call | flops 10000000 | bytes 36000000 | tf_op jit(solution)/shard_map/widen/pallas_call | solution.py:1474
  359.8 1.3 reduce.4
  361.1 1.3 reduce.6
  362.3 1.3 reduce.5
  363.6 0.0 copy-done
  363.6 0.9 copy.33
  364.5 0.0 copy-done.1
  364.5 0.9 copy.34
  (2 shorter events, 0.0 us)
Async XLA Ops:
  4.0 0.6 copy-start.2
  344.7 18.9 %copy-start = (f32[512,384]{1,0:T(8,128)S(1)}, f32[512,384]{1,0:T(8,128)}, u32[]{:S(2)}) copy-start(f32[512,384]{1,0:T(8,128)} %get-tuple-element.130) | copy-start | bytes 2359300
  344.7 19.8 %copy-start.1 = (f32[512,384]{1,0:T(8,128)S(1)}, f32[512,384]{1,0:T(8,128)}, u32[]{:S(2)}) copy-start(f32[512,384]{1,0:T(8,128)} %get-tuple-element.131) | copy-start | bytes 2359300

commit v6 on v5

--- a/solution.py
+++ b/solution.py
@@ -55,6 +55,12 @@
         self.far = 2 * (1 - self.hi) + self.core
         self.sibfar = 2 * (1 - self.hi) + 1 - self.core
         self.block = block_of(self.row, self.col)
+        self.chips = (
+            (self.row, 1 - self.hi),
+            (1 - self.row, self.hi),
+            (1 - self.row, 1 - self.hi),
+            (self.row, self.hi),
+        )
         self.S = {"col": self.sib}
         self.O = {"col": self.far}
         self.OS = {"col": self.sibfar}
@@ -323,7 +329,8 @@
     mid_ref,
     gains_all,
     dn2_ref,
-    out_ref,
+    hidden_out,
+    dw_out,
     grad_gu,
     grad_down,
     wqkv_ref,
@@ -339,11 +346,10 @@
     part_out,
     part_in,
     d_up,
-    ffn,
     tile_buf,
     *rest,
 ):
-    red_a, red_b, sems = rest[:7], rest[7:14], rest[14:]
+    red_a, sems = rest[:7], rest[7:]
     send_sems, recv_sems, local_sems, tile_sems = sems
     at = Place()
     net = Net(send_sems, recv_sems, at)
@@ -433,12 +439,6 @@
     near_qw = net.send(wqkv_ref, qw.at[pl.ds(mine, FEAT), :], at.S)
     near_ow = net.send(wout_ref, ow.at[:, pl.ds(mine, FEAT)], at.S)
 
-    @pl.when(chosen)
-    def _():
-        for core in (0, 1):
-            for copy in slice_copies(core, 2, 5):
-                copy.start()
-
     far_half = pl.ds(mine_far, 2 * FEAT)
 
     def qkv_slices(z, y):
@@ -461,20 +461,9 @@
         return slices
 
     net.take(across[0], qkv_slices(at.z, at.y)[0])
-    ring = ring_dp(
-        net,
-        at,
-        (
-            lambda z, y: [qkv_slices(z, y)[0].at[:, pl.ds(0, 256)]],
-            lambda z, y: [qkv_slices(z, y)[0].at[:, pl.ds(256, 256)]],
-        ),
-    )
+    net.take(across[1], out_slices(at.z, at.y)[0])
+    ring = ring_dp(net, at, (qkv_slices, out_slices))
     next(ring)
-    near = [
-        net.send(wg_ref.at[:, pl.ds(quarter_start(at.sib), PART)], gw.at[pl.ds(mine, FEAT), :], at.S),
-        net.send(wu_ref.at[:, pl.ds(quarter_start(at.sib), PART)], uw.at[pl.ds(mine, FEAT), :], at.S),
-        net.send(wd_ref.at[pl.ds(quarter_start(at.sib), PART), :], dw.at[:, pl.ds(mine, FEAT)], at.S),
-    ]
     next(ring)
     next(ring)
     gather_x.middle()
@@ -482,24 +471,24 @@
     net.take(gain_far, gains_far)
     gain_sibfar = net.send(gains_far, gains_far, at.S)
     next(ring)
-    net.take(across[1], out_slices(at.z, at.y)[0])
-    net.take(across[2], ffn_slices(gw, 0, 80)(at.z, at.y)[0])
-    net.take(across[3], ffn_slices(uw, 80, 64)(at.z, at.y)[0])
-    net.take(across[4], ffn_slices(uw, 0, 144)(at.z, at.y)[1])
-    drain(ring)
-    ring = ring_dp(
-        net,
-        at,
-        (
-            ffn_slices(gw, 0, 80),
-            lambda z, y: ffn_slices(uw, 80, 64)(z, y) + out_slices(z, y),
-        ),
-    )
-    next(ring)
     cols_half, rows_half = pl.ds(aligned(at.core, 512), 512), pl.ds(aligned(at.core, FEAT), FEAT)
-    far_qw = net.send(qw.at[far_half, cols_half], qw.at[far_half, cols_half], at.S)
     gather_og = Gather8(net, at, tokens_of(og_all))
     gather_x.late()
+
+    @pl.when(chosen)
+    def _():
+        for core in (0, 1):
+            for copy in slice_copies(core, 2, 5):
+                copy.start()
+
+    drain(ring)
+    far_qw = net.send(qw.at[far_half, cols_half], qw.at[far_half, cols_half], at.S)
+    far_ow = net.send(ow.at[rows_half, far_half], ow.at[rows_half, far_half], at.S)
+    near = [
+        net.send(wg_ref.at[:, pl.ds(quarter_start(at.sib), PART)], gw.at[pl.ds(mine, FEAT), :], at.S),
+        net.send(wu_ref.at[:, pl.ds(quarter_start(at.sib), PART)], uw.at[pl.ds(mine, FEAT), :], at.S),
+        net.send(wd_ref.at[pl.ds(quarter_start(at.sib), PART), :], dw.at[:, pl.ds(mine, FEAT)], at.S),
+    ]
     gather_og.start(og_ref)
     gather_x.end()
     early = list(net.sent)
@@ -518,6 +507,10 @@
         return carry
 
     lax.fori_loop(0, SEQ // BLOCK // 2, norm_block, 0)
+    net.take(across[2], ffn_slices(gw, 0, 80)(at.z, at.y)[0])
+    net.take(across[3], ffn_slices(uw, 80, 64)(at.z, at.y)[0])
+    net.take(across[4], ffn_slices(uw, 0, 144)(at.z, at.y)[1])
+    ring = ring_dp(net, at, (ffn_slices(gw, 0, 80), ffn_slices(uw, 80, 64)))
     next(ring)
     lax.fori_loop(SEQ // BLOCK // 2, SEQ // BLOCK, norm_block, 0)
     next(ring)
@@ -569,15 +562,8 @@
             attn_ref[rows, lanes] = dot(probs, v_ref[:keys, :]).astype(BF)
             return carry
 
-        lax.fori_loop(0, HEADS // 2, attend, 0)
+        lax.fori_loop(0, HEADS, attend, 0)
         next(ring)
-        lax.fori_loop(HEADS // 2, HEADS, attend, 0)
-        next(ring)
-
-    drain(ring)
-    far_ow = net.send(ow.at[rows_half, far_half], ow.at[rows_half, far_half], at.S)
-    gather_og.end()
-    move(og_all.at[my_rows, :], og_out)
 
     net.take(near_ow, ow.at[:, pl.ds(aligned(at.sib, FEAT), FEAT)])
     other_rows = pl.ds(aligned(1 - at.core, FEAT), FEAT)
@@ -599,6 +585,15 @@
     n2_all[my_rows, :] = (mid * rms(mid) * gain2).astype(BF)
     gather_n2 = Gather8(net, at, place_n2)
     gather_n2.start(place_n2(at.row, at.col, None))
+    gather_og.end()
+    move(og_all.at[my_rows, :], og_out)
+    next(ring)
+    next(ring)
+    gather_n2.middle()
+    next(ring)
+    next(ring)
+    gather_n2.late()
+    drain(ring)
     net.take(near[2], dw.at[:, pl.ds(aligned(at.sib, FEAT), FEAT)])
 
     def hidden_back(i, carry):
@@ -608,17 +603,15 @@
             d_up[rows, lanes] = dot(og_all[rows, :], dw[lanes, :], 1, 1).astype(BF)
         return carry
 
-    lax.fori_loop(0, 3, hidden_back, 0)
-    gather_n2.middle()
-    lax.fori_loop(3, 4, hidden_back, 0)
+    lax.fori_loop(0, 4, hidden_back, 0)
+    move(dw, dw_out)
     net.take(near[0], gw.at[pl.ds(aligned(at.sib, FEAT), FEAT), :])
     net.take(near[1], uw.at[pl.ds(aligned(at.sib, FEAT), FEAT), :])
 
     net.finish(early)
     hidden, d_gate = x_all.at[:, pl.ds(0, PART)], n1.at[:, pl.ds(0, PART)]
     norms = Reduce8(net, at, *red_a)
-    outs = Reduce8(net, at, *red_b)
-    chips = ((at.row, 1 - at.hi), (1 - at.row, at.hi), (1 - at.row, 1 - at.hi), (at.row, at.hi))
+    chips = at.chips
     last_part = at.col == 3
 
     def tokens(j):
@@ -627,8 +620,6 @@
         return pl.ds(aligned(first, BLOCK), 256), at.core + row * (1 - 2 * at.core)
 
     for j in (3, 1, 2, 0):
-        if j == 0:
-            gather_n2.late()
         gather_n2.end(j)
         rows, _ = tokens(j)
         for first, width in tiles_of(PART, 512):
@@ -646,6 +637,7 @@
                 values = [jnp.where(fresh, value, 0.0) for value in values]
             for ref, value in zip((hidden, d_gate, d_up), values, strict=True):
                 ref[rows, lanes] = value.astype(BF)
+    move(hidden, hidden_out)
     for j in range(4):
         rows, place = tokens(j)
         own_rows = pl.ds(pl.multiple_of(rows.start + place * BLOCK, BLOCK), BLOCK)
@@ -681,23 +673,9 @@
             writes[-1].start()
 
     outer_sum(hidden, og_all, grad_down)
-    for j in range(4):
-        row, hi = chips[j]
-        rows = pl.ds(aligned(row, SEQ // 2), SEQ // 2)
-        lanes = pl.ds(aligned(hi, QCOLS), QCOLS)
-        ffn[...] = dot(hidden[rows, :], dw[:, lanes])
-        if j in (0, 3):
-            mine_mid = pl.ds(pl.multiple_of((at.block - 4 * at.row) * BLOCK, BLOCK), BLOCK)
-            ffn[mine_mid, :] += mid_ref[:, lanes]
-        own = ffn[:, pl.ds(aligned(at.core, FEAT), FEAT)].astype(BF)
-        outs.put(j, own, ffn[:, pl.ds(aligned(1 - at.core, FEAT), FEAT)].astype(BF))
-        if j:
-            outs.step(j - 1)
-        if j == 1:
-            dn2_ref[...] = norms.step(3)
     outer_sum(n2_all, d_gate, grad_gu.at[0])
+    dn2_ref[...] = norms.step(3)
     outer_sum(n2_all, d_up, grad_gu.at[1])
-    out_ref[...] = outs.step(3)
     for copy in writes[-2:]:
         copy.wait()
     for copy in local:
@@ -726,7 +704,8 @@
         ((BLOCK, MODEL), F32, vmem),
         ((8, MODEL), F32, vmem),
         ((BLOCK, MODEL), F32, vmem),
-        ((SEQ // 2, FEAT), F32, vmem),
+        ((SEQ, PART), BF, anywhere),
+        ((PART, MODEL), BF, anywhere),
         ((2, MODEL, PART), BF, anywhere),
         ((PART, MODEL), BF, anywhere),
     )
@@ -749,11 +728,9 @@
             pltpu.VMEM((BLOCK, MODEL), BF),
             pltpu.VMEM((BLOCK, MODEL), BF),
             pltpu.VMEM((SEQ, PART), BF),
-            pltpu.VMEM((SEQ // 2, QCOLS), F32),
             pltpu.VMEM((2, MODEL, 256), BF),
         ]
         + reduce8_scratch(BLOCK, MODEL)
-        + reduce8_scratch(SEQ // 2, FEAT)
         + [
             pltpu.SemaphoreType.DMA((200,)),
             pltpu.SemaphoreType.DMA((200,)),
@@ -1221,19 +1198,49 @@
     qkv,
     out,
     small_ref,
+    mid_ref,
+    hidden_far,
+    dw_far,
     all_gu,
     all_down,
     all_qkv,
     all_out,
     small_out,
+    out_ref,
     small_y,
     small_z,
+    hidden,
+    dw,
+    ffn,
     *rest,
 ):
-    bufs, (send_sems, recv_sems, local_sems) = rest[:-3], rest[-3:]
+    red, bufs, (send_sems, recv_sems, local_sems) = rest[:7], rest[7:-3], rest[-3:]
     at = Place()
     net = Net(send_sems, recv_sems, at)
-    at.meet((at.S, at.O, at.OS, at.YP, at.YM, at.ZP, at.ZM, at.Y2, at.Z2))
+    held = [
+        pltpu.make_async_copy(hidden_far, hidden, local_sems.at[2]),
+        pltpu.make_async_copy(dw_far, dw, local_sems.at[3]),
+    ]
+    for copy in held:
+        copy.start()
+    at.meet(
+        (at.S, at.O, at.OS, at.N1, at.N2, at.YP, at.YM, at.ZP, at.ZM, at.Y2, at.Z2)
+    )
+    outs = Reduce8(net, at, *red)
+
+    def project(j):
+        row, hi = at.chips[j]
+        rows = pl.ds(aligned(row, SEQ // 2), SEQ // 2)
+        lanes = pl.ds(aligned(hi, QCOLS), QCOLS)
+        ffn[...] = dot(hidden[rows, :], dw[:, lanes])
+        if j in (0, 3):
+            mine = pl.ds(pl.multiple_of((at.block - 4 * at.row) * BLOCK, BLOCK), BLOCK)
+            ffn[mine, :] += mid_ref[:, lanes]
+        own = ffn[:, pl.ds(aligned(at.core, FEAT), FEAT)].astype(BF)
+        outs.put(j, own, ffn[:, pl.ds(aligned(1 - at.core, FEAT), FEAT)].astype(BF))
+        if j:
+            outs.step(j - 1)
+
     z, y = at.z, at.y
 
     def gu_piece(k, lanes):
@@ -1308,6 +1315,9 @@
         net, at, (half_of(at.hi), half_of(1 - at.hi)), (chip_ready, far_ready)
     )
     next(ring)
+    for copy in held:
+        copy.wait()
+    project(0)
     for item in first:
         item.middle()
     for key, k in zip(small_keys, (y - 1, y + 1, y + 2), strict=True):
@@ -1315,16 +1325,19 @@
     small_z[z] = (small_y[0] + small_y[1]) + (small_y[2] + small_y[3])
     small_keys = [net.send(small_z.at[z], small_z.at[z], d) for d in (at.ZP, at.ZM, at.Z2)]
     next(ring)
+    project(1)
     for item in first:
         item.end()
     begin(last)
     next(ring)
+    project(2)
     for item in last:
         item.middle()
     for key, k in zip(small_keys, (z - 1, z + 1, z + 2), strict=True):
         net.take(key, small_z.at[lax.rem(k + 4, 4)])
     small_out[...] = (small_z[0] + small_z[1]) + (small_z[2] + small_z[3])
     next(ring)
+    project(3)
     for item in last:
         item.end()
     after = ring_dp(
@@ -1336,10 +1349,11 @@
     for _ in ring:
         next(after, None)
     drain(after)
+    out_ref[...] = outs.step(3)
     net.finish()
 
 
-def run_sums(gu, down, qkv, out, small):
+def run_sums(gu, down, qkv, out, small, mid, hidden, dw):
     def shape(dims, dtype):
         return jax.ShapeDtypeStruct(dims, dtype)
 
@@ -1349,24 +1363,31 @@
         shape((FEAT, QKV), BF),
         shape((QCOLS, FEAT), BF),
         shape(small.shape, F32),
+        shape((SEQ // 2, FEAT), F32),
     )
     return pl.pallas_call(
         sums_kernel,
         out_shape=outs,
-        in_specs=[vmem()] * 5,
-        out_specs=[anywhere()] * 2 + [vmem()] * 3,
+        in_specs=[vmem()] * 6 + [anywhere()] * 2,
+        out_specs=[anywhere()] * 2 + [vmem()] * 4,
         scratch_shapes=[pltpu.VMEM((4,) + small.shape, F32)] * 2
+        + [
+            pltpu.VMEM((SEQ, PART), BF),
+            pltpu.VMEM((PART, MODEL), BF),
+            pltpu.VMEM((SEQ // 2, QCOLS), F32),
+        ]
+        + reduce8_scratch(SEQ // 2, FEAT)
         + ring_scratch(SMALL_FIRST, SMALL_LAST)
         + [pltpu.SemaphoreType.DMA((128,)), pltpu.SemaphoreType.DMA((128,))]
-        + [pltpu.SemaphoreType.DMA((2,))],
+        + [pltpu.SemaphoreType.DMA((4,))],
         compiler_params=pltpu.CompilerParams(
             collective_id=3, has_side_effects=True, vmem_limit_bytes=VMEM_LIMIT
         ),
         cost_estimate=pl.CostEstimate(
-            flops=10**8, bytes_accessed=60 * 10**6, transcendentals=0
+            flops=4 * 10**9, bytes_accessed=60 * 10**6, transcendentals=0
         ),
         name="sums_over_sequences",
-    )(gu, down, qkv, out, small)
+    )(gu, down, qkv, out, small, mid, hidden, dw)
 
 
 def widen_kernel(
@@ -1535,7 +1556,8 @@
         mid,
         gains_all,
         dn2,
-        layer_output,
+        hidden,
+        down_w,
         grad_gu,
         grad_down,
     ) = run_forward(
@@ -1572,12 +1594,15 @@
         grad_gu.reshape(2, 4, 2, 4, 48, PART),
         grad_down.reshape(2, 2, 288, MODEL),
     )
-    grad_gu, grad_down, grad_qkv, grad_out, small = run_sums(
+    grad_gu, grad_down, grad_qkv, grad_out, small, layer_output = run_sums(
         grad_gu,
         grad_down,
         grad_qkv.reshape(2, 4, 48, QKV),
         grad_out.reshape(2, 2, 4, 48, FEAT),
         small,
+        mid,
+        hidden,
+        down_w,
     )
     (
         grad_gate,

time: 371 us -> 351 us (0.946)
  Pallas kernels: 355 us -> 336 us
    pallas_call x1, Pallas kernels: 160 us -> 146 us  [run_forward(): pl.pallas_call(forward_kernel, out_shape=[jax.ShapeDtypeStruct(dims, dtyp...]
where the time goes in v6:
time: 351 us; the launch traced here: 347 us
  Pallas kernels  336 us (96%)
  other arithmetic  5.11 us (1%)
  local copies, waits for them, and re-layouts  4.44 us (1%)
    pallas_call x1, Pallas kernels, run_forward(): pl.pallas_call(forward_kernel, out_shape=[jax.ShapeDtypeStruct(dims, dtyp...  146 us
    pallas_call x1, Pallas kernels, run_sums(): pl.pallas_call(sums_kernel, out_shape=outs, in_specs=[vmem()] * 6 + [anyw...  89.6 us
    pallas_call x1, Pallas kernels, run_backward(): pl.pallas_call(backward_kernel, out_shape=outs, in_specs=[vmem()] * (len(...  85.7 us
    pallas_call x1, Pallas kernels, run_widen(): pl.pallas_call(widen_kernel, out_shape=[jax.ShapeDtypeStruct(dims, F32) f...  15.1 us

profile of v6, /device:TPU:0, one launch (start us, length us, event | category | flops | bytes accessed | tf_op | source)
XLA Modules:
  0.0 346.6 jit_solution(10323229606468608759)
XLA Ops:
  0.6 0.7 reshape.136
  1.3 0.7 reshape.142
  2.0 0.7 concatenate.20
  2.7 1.3 maximum_convert_fusion.bias_ref
  4.0 0.0 copy-start.2
  4.0 0.6 copy-done.2
  4.6 145.8 %forward_and_feed_forward.1 = (bf16[128,1536]{1,0:T(8,128)(2,1)}, bf16[1024,384]{1,0:T(8,128)(2,1)}, bf16[128,1536]{1,0:T(8,128)(2,1)}, bf16[1536,1024]{1,0:T(8,...) custom-call(bf16[512,384]{1,0:T(8,128)(2,1)} %x_ref.1, ...), custom_call_target="tpu_custom_call" | custom-call | flops 36999999488 | bytes 80000000 | tf_op jit(solution)/shard_map/forward_and_feed_forward/pallas_call | solution.py:712
  150.4 85.7 %attention_backward.1 = (f32[512,384]{1,0:T(8,128)}, bf16[768,384]{1,0:T(8,128)(2,1)}, bf16[384,1024]{1,0:T(8,128)(2,1)}, f32[8,1408]{1,0:T(8,128)}, bf16[4,48,1...) custom-call(f32[128,1536]{1,0:T(8,128)} %get-tuple-element.79.dn2_ref, f32[128,1536]{1,0:T(8,128)} %get-tuple-element.80.mid_ref, ...), custom_call_target="tpu_custom_call" | custom-call | flops 10000000000 | bytes 40000000 | tf_op jit(solution)/shard_map/attention_backward/pallas_call | solution.py:1155
  236.1 89.6 %sums_over_sequences.1 = (bf16[2,384,4608]{2,1,0:T(8,128)(2,1)}, bf16[4,1280,384]{2,1,0:T(8,128)(2,1)}, bf16[384,1024]{1,0:T(8,128)(2,1)}, bf16[768,384]{1,0:T(8...) custom-call(bf16[4,48,1152]{2,1,0:T(8,128)(2,1)} %get-tuple-element.94.gu_own, ...), custom_call_target="tpu_custom_call" | custom-call | flops 4000000000 | bytes 60000000 | tf_op jit(solution)/shard_map/sums_over_sequences/pallas_call | solution.py:1368
  325.7 0.0 copy-start.1
  325.7 0.0 copy-start
  325.7 15.1 %widen.1 = (f32[384,4480]{1,0:T(8,128)}, f32[384,4480]{1,0:T(8,128)}, f32[4480,384]{1,0:T(8,128)}, f32[384,768]{1,0:T(8,128)}, f32[384,128]{1,0:T(8,128)}, /*ind...) custom-call(bf16[2,384,4608]{2,1,0:T(8,128)(2,1)} %get-tuple-element, ...), custom_call_target="tpu_custom_call" | custom-call | flops 10000000 | bytes 36000000 | tf_op jit(solution)/shard_map/widen/pallas_call | solution.py:1495
  340.8 1.3 reduce.4
  342.1 1.3 reduce.6
  343.3 1.3 reduce.5
  344.6 0.0 copy-done.1
  344.6 0.9 copy.33
  345.5 0.0 copy-done
  345.5 0.9 copy.34
  (2 shorter events, 0.0 us)
Async XLA Ops:
  4.0 0.6 copy-start.2
  325.7 18.9 %copy-start.1 = (f32[512,384]{1,0:T(8,128)S(1)}, f32[512,384]{1,0:T(8,128)}, u32[]{:S(2)}) copy-start(f32[512,384]{1,0:T(8,128)} %get-tuple-element.134) | copy-start | bytes 2359300
  325.7 19.8 %copy-start = (f32[512,384]{1,0:T(8,128)S(1)}, f32[512,384]{1,0:T(8,128)}, u32[]{:S(2)}) copy-start(f32[512,384]{1,0:T(8,128)} %get-tuple-element.135) | copy-start | bytes 2359300

commit v7 on v6

--- a/solution.py
+++ b/solution.py
@@ -302,6 +302,160 @@
     return [(first, min(step, width - first)) for first in range(0, width, step)]
 
 
+def add_up(out, terms):
+    lead = out.shape[:-2]
+    if not lead:
+        total = terms[0][...].astype(F32)
+        for term in terms[1:]:
+            total = total + term[...].astype(F32)
+        out[...] = total.astype(out.dtype)
+        return
+    count = 1
+    for size in lead:
+        count *= size
+
+    def step(i, carry):
+        index = []
+        for size in reversed(lead):
+            index.insert(0, i % size)
+            i = i // size
+        index = tuple(index)
+        total = terms[0].at[index][...].astype(F32)
+        for term in terms[1:]:
+            total = total + term.at[index][...].astype(F32)
+        out.at[index][...] = total.astype(out.dtype)
+        return carry
+
+    lax.fori_loop(0, count, step, 0)
+
+
+class RingItem:
+    def __init__(self, net, sides, place, part, held, way, bufs, own):
+        self.net, self.part, self.held, self.own = net, part, held, own
+        self.relay, self.staged, self.from_last, self.from_next = bufs
+        self.onward, self.back = (sides[0], sides[1]) if way == 0 else (sides[1], sides[0])
+        step = 1 - 2 * way
+        self.here, self.next, self.across, self.last = (
+            lax.rem(place + 4 + step * i, 4) for i in (0, 1, 2, 3)
+        )
+
+    def start(self):
+        self.k_relay = self.net.send(self.part(self.across), self.relay, self.onward)
+
+    def direct(self):
+        self.k_next = self.net.send(self.part(self.last), self.from_next, self.back)
+
+    def middle(self):
+        self.net.take(self.k_relay, self.relay)
+        add_up(self.staged, [self.held(self.next), self.relay])
+        self.k_last = self.net.send(self.staged, self.from_last, self.onward)
+
+    def end(self):
+        self.net.take(self.k_next, self.from_next)
+        self.net.take(self.k_last, self.from_last)
+        add_up(self.own, [self.held(self.here), self.from_next, self.from_last])
+
+
+def begin(items):
+    for item in items:
+        item.start()
+    for item in items:
+        item.direct()
+
+
+LEFT, RIGHT = pl.ds(0, QCOLS), pl.ds(QCOLS, QCOLS)
+GU_FIRST = (((2, 2, 48, PART),), ((2, 2, 48, PART),))
+GU_LAST = (((48, PART),) * 2,) * 2
+DOWN_FIRST = (((2, 80, QCOLS),), ((144, QCOLS),))
+DOWN_LAST = (((80, QCOLS),),) * 2
+SMALL_FIRST = (((2, 48, 512),), ((2, 48, FEAT),))
+SMALL_LAST = (((48, 512),), ((48, FEAT),))
+
+
+def down_rows(k):
+    return pl.ds(pl.multiple_of(72 * k - 8 * (k % 2), 16), 80)
+
+
+def ring_scratch(first, last):
+    scratch = []
+    for i in (0, 1):
+        for dims in first[i]:
+            scratch += [pltpu.VMEM(dims, BF)] * 8
+            scratch.append(pltpu.VMEM((2,) + dims, BF))
+        for dims in last[i]:
+            scratch += [pltpu.VMEM(dims, BF)] * 4
+    return scratch
+
+
+def ring_items(net, at, first, last, parts, helds, seconds, finals, bufs):
+    sides = (((at.YP, at.YM), (at.ZP, at.ZM)), ((at.ZP, at.ZM), (at.YP, at.YM)))
+    places = ((at.y, at.z), (at.z, at.y))
+    bufs = list(bufs)
+    one, two = ([], []), ([], [])
+    for i in (0, 1):
+        owns = []
+        for n in range(len(first[i])):
+            own = bufs[8]
+            for way in (0, 1):
+                part = functools.partial(lambda k, f, w: f(k, w), f=parts[i][n], w=way)
+                held = functools.partial(lambda k, f, w: f(k, w), f=helds[i][n], w=way)
+                four = bufs[4 * way : 4 * way + 4]
+                one[i].append(
+                    RingItem(net, sides[i][0], places[i][0], part, held, way, four, own.at[way])
+                )
+            owns.append(own)
+            bufs = bufs[9:]
+        for n in range(len(last[i])):
+            part = functools.partial(lambda k, f, o: f(o, k), f=seconds[i][n], o=owns[min(n, len(owns) - 1)])
+            two[i].append(
+                RingItem(net, sides[i][1], places[i][1], part, part, n % 2, bufs[:4], finals[i][n])
+            )
+            bufs = bufs[4:]
+
+    def mix(pair):
+        return [item for items in zip(*pair, strict=True) for item in items]
+
+    return mix(one), mix(two)
+
+
+def gu_items(net, at, far_ref, near_ref, gu_own, bufs):
+    def parts_of(gu):
+        return (
+            (lambda k, way: gu.at[way, pl.ds(0, 2), :, k],),
+            (lambda k, way: gu.at[k // 2, pl.ds(2, 2), k % 2, pl.ds(2 * way, 2)],),
+        )
+
+    seconds = (
+        (lambda own, k: own.at[k // 2, 0, k % 2], lambda own, k: own.at[k // 2, 1, k % 2]),
+    ) * 2
+    finals = ((gu_own.at[0], gu_own.at[1]), (gu_own.at[2], gu_own.at[3]))
+    helds = parts_of(near_ref)
+    return ring_items(net, at, GU_FIRST, GU_LAST, parts_of(far_ref), helds, seconds, finals, bufs)
+
+
+def down_items(net, at, down, down_own, bufs):
+    parts = (
+        (lambda k, way: down.at[way, :, down_rows(k), LEFT],),
+        (lambda k, way: down.at[k // 2, k % 2, pl.ds(144 * way, 144), RIGHT],),
+    )
+    seconds = (
+        (lambda own, k: own.at[k // 2, k % 2],),
+        (lambda own, k: own.at[k // 2, pl.ds(pl.multiple_of((k % 2) * 64, 64), 80)],),
+    )
+    finals = ((down_own.at[:, LEFT],), (down_own.at[:, RIGHT],))
+    return ring_items(net, at, DOWN_FIRST, DOWN_LAST, parts, parts, seconds, finals, bufs)
+
+
+def small_items(net, at, qkv, out, qkv_own, out_own, bufs):
+    parts = (
+        (lambda k, way: qkv.at[:, k, :, pl.ds(512 * way, 512)],),
+        (lambda k, way: out.at[k // 2, k % 2, pl.ds(2 * way, 2)],),
+    )
+    seconds = ((lambda own, k: own.at[k // 2, k % 2],), (lambda own, k: own.at[k // 2, k % 2],))
+    finals = ((qkv_own,), (out_own,))
+    return ring_items(net, at, SMALL_FIRST, SMALL_LAST, parts, parts, seconds, finals, bufs)
+
+
 def forward_kernel(
     x_ref,
     og_ref,
@@ -332,7 +486,7 @@
     hidden_out,
     dw_out,
     grad_gu,
-    grad_down,
+    down_own,
     wqkv_ref,
     x_all,
     n1,
@@ -347,9 +501,10 @@
     part_in,
     d_up,
     tile_buf,
+    down,
     *rest,
 ):
-    red_a, sems = rest[:7], rest[7:]
+    red_a, bufs, sems = rest[:7], rest[7:-4], rest[-4:]
     send_sems, recv_sems, local_sems, tile_sems = sems
     at = Place()
     net = Net(send_sems, recv_sems, at)
@@ -439,6 +594,12 @@
     near_qw = net.send(wqkv_ref, qw.at[pl.ds(mine, FEAT), :], at.S)
     near_ow = net.send(wout_ref, ow.at[:, pl.ds(mine, FEAT)], at.S)
 
+    @pl.when(chosen)
+    def _():
+        for core in (0, 1):
+            for copy in slice_copies(core, 2, 5):
+                copy.start()
+
     far_half = pl.ds(mine_far, 2 * FEAT)
 
     def qkv_slices(z, y):
@@ -475,15 +636,14 @@
     gather_og = Gather8(net, at, tokens_of(og_all))
     gather_x.late()
 
-    @pl.when(chosen)
-    def _():
-        for core in (0, 1):
-            for copy in slice_copies(core, 2, 5):
-                copy.start()
-
     drain(ring)
     far_qw = net.send(qw.at[far_half, cols_half], qw.at[far_half, cols_half], at.S)
     far_ow = net.send(ow.at[rows_half, far_half], ow.at[rows_half, far_half], at.S)
+    net.take(across[2], ffn_slices(gw, 0, 80)(at.z, at.y)[0])
+    net.take(across[3], ffn_slices(uw, 80, 64)(at.z, at.y)[0])
+    net.take(across[4], ffn_slices(uw, 0, 144)(at.z, at.y)[1])
+    ring = ring_dp(net, at, (ffn_slices(gw, 0, 80), ffn_slices(uw, 80, 64)))
+    next(ring)
     near = [
         net.send(wg_ref.at[:, pl.ds(quarter_start(at.sib), PART)], gw.at[pl.ds(mine, FEAT), :], at.S),
         net.send(wu_ref.at[:, pl.ds(quarter_start(at.sib), PART)], uw.at[pl.ds(mine, FEAT), :], at.S),
@@ -507,10 +667,6 @@
         return carry
 
     lax.fori_loop(0, SEQ // BLOCK // 2, norm_block, 0)
-    net.take(across[2], ffn_slices(gw, 0, 80)(at.z, at.y)[0])
-    net.take(across[3], ffn_slices(uw, 80, 64)(at.z, at.y)[0])
-    net.take(across[4], ffn_slices(uw, 0, 144)(at.z, at.y)[1])
-    ring = ring_dp(net, at, (ffn_slices(gw, 0, 80), ffn_slices(uw, 80, 64)))
     next(ring)
     lax.fori_loop(SEQ // BLOCK // 2, SEQ // BLOCK, norm_block, 0)
     next(ring)
@@ -587,7 +743,6 @@
     gather_n2.start(place_n2(at.row, at.col, None))
     gather_og.end()
     move(og_all.at[my_rows, :], og_out)
-    next(ring)
     next(ring)
     gather_n2.middle()
     next(ring)
@@ -638,6 +793,13 @@
             for ref, value in zip((hidden, d_gate, d_up), values, strict=True):
                 ref[rows, lanes] = value.astype(BF)
     move(hidden, hidden_out)
+    for first, width in tiles_of(MODEL, 256):
+        lanes = pl.ds(first, width)
+        tile = dot(hidden[...], og_all[:, lanes], 0, 0).astype(BF)
+        for q in range(4):
+            down[q // 2, q % 2, :, lanes] = tile[288 * q : 288 * (q + 1)]
+    sums, last_sums = down_items(net, at, down, down_own, bufs)
+    begin(sums)
     for j in range(4):
         rows, place = tokens(j)
         own_rows = pl.ds(pl.multiple_of(rows.start + place * BLOCK, BLOCK), BLOCK)
@@ -672,10 +834,18 @@
             )
             writes[-1].start()
 
-    outer_sum(hidden, og_all, grad_down)
+    for item in sums:
+        item.middle()
     outer_sum(n2_all, d_gate, grad_gu.at[0])
     dn2_ref[...] = norms.step(3)
+    for item in sums:
+        item.end()
+    begin(last_sums)
     outer_sum(n2_all, d_up, grad_gu.at[1])
+    for item in last_sums:
+        item.middle()
+    for item in last_sums:
+        item.end()
     for copy in writes[-2:]:
         copy.wait()
     for copy in local:
@@ -707,7 +877,7 @@
         ((SEQ, PART), BF, anywhere),
         ((PART, MODEL), BF, anywhere),
         ((2, MODEL, PART), BF, anywhere),
-        ((PART, MODEL), BF, anywhere),
+        ((80, MODEL), BF, vmem),
     )
     return pl.pallas_call(
         forward_kernel,
@@ -729,8 +899,10 @@
             pltpu.VMEM((BLOCK, MODEL), BF),
             pltpu.VMEM((SEQ, PART), BF),
             pltpu.VMEM((2, MODEL, 256), BF),
+            pltpu.VMEM((2, 2, 288, MODEL), BF),
         ]
         + reduce8_scratch(BLOCK, MODEL)
+        + ring_scratch(DOWN_FIRST, DOWN_LAST)
         + [
             pltpu.SemaphoreType.DMA((200,)),
             pltpu.SemaphoreType.DMA((200,)),
@@ -745,158 +917,6 @@
         ),
         name="forward_and_feed_forward",
     )(x, og, wq, wk, wv, wout, wg, wu, wd, gains, bias, cosine, sine)
-
-
-def add_up(out, terms):
-    lead = out.shape[:-2]
-    if not lead:
-        total = terms[0][...].astype(F32)
-        for term in terms[1:]:
-            total = total + term[...].astype(F32)
-        out[...] = total.astype(out.dtype)
-        return
-    count = 1
-    for size in lead:
-        count *= size
-
-    def step(i, carry):
-        index = []
-        for size in reversed(lead):
-            index.insert(0, i % size)
-            i = i // size
-        index = tuple(index)
-        total = terms[0].at[index][...].astype(F32)
-        for term in terms[1:]:
-            total = total + term.at[index][...].astype(F32)
-        out.at[index][...] = total.astype(out.dtype)
-        return carry
-
-    lax.fori_loop(0, count, step, 0)
-
-
-class RingItem:
-    def __init__(self, net, sides, place, part, held, way, bufs, own):
-        self.net, self.part, self.held, self.own = net, part, held, own
-        self.relay, self.staged, self.from_last, self.from_next = bufs
-        self.onward, self.back = (sides[0], sides[1]) if way == 0 else (sides[1], sides[0])
-        step = 1 - 2 * way
-        self.here, self.next, self.across, self.last = (
-            lax.rem(place + 4 + step * i, 4) for i in (0, 1, 2, 3)
-        )
-
-    def start(self):
-        self.k_relay = self.net.send(self.part(self.across), self.relay, self.onward)
-
-    def direct(self):
-        self.k_next = self.net.send(self.part(self.last), self.from_next, self.back)
-
-    def middle(self):
-        self.net.take(self.k_relay, self.relay)
-        add_up(self.staged, [self.held(self.next), self.relay])
-        self.k_last = self.net.send(self.staged, self.from_last, self.onward)
-
-    def end(self):
-        self.net.take(self.k_next, self.from_next)
-        self.net.take(self.k_last, self.from_last)
-        add_up(self.own, [self.held(self.here), self.from_next, self.from_last])
-
-
-def begin(items):
-    for item in items:
-        item.start()
-    for item in items:
-        item.direct()
-
-
-LEFT, RIGHT = pl.ds(0, QCOLS), pl.ds(QCOLS, QCOLS)
-FFN_FIRST = (((2, 2, 48, PART), (2, 80, QCOLS)), ((2, 2, 48, PART), (144, QCOLS)))
-FFN_LAST = (((2, 48, PART), (80, QCOLS)), ((2, 48, PART), (80, QCOLS)))
-SMALL_FIRST = (((2, 48, 512),), ((2, 48, FEAT),))
-SMALL_LAST = (((48, 512),), ((48, FEAT),))
-
-
-def down_rows(k):
-    return pl.ds(pl.multiple_of(72 * k - 8 * (k % 2), 16), 80)
-
-
-def ring_scratch(first, last):
-    scratch = []
-    for i in (0, 1):
-        for dims in first[i]:
-            scratch += [pltpu.VMEM(dims, BF)] * 8
-            scratch.append(pltpu.VMEM((2,) + dims, BF))
-        for dims in last[i]:
-            scratch += [pltpu.VMEM(dims, BF)] * 4
-    return scratch
-
-
-def ring_items(net, at, first, last, parts, helds, seconds, finals, bufs):
-    sides = (((at.YP, at.YM), (at.ZP, at.ZM)), ((at.ZP, at.ZM), (at.YP, at.YM)))
-    places = ((at.y, at.z), (at.z, at.y))
-    bufs = list(bufs)
-    one, two = ([], []), ([], [])
-    for i in (0, 1):
-        owns = []
-        for n in range(len(first[i])):
-            own = bufs[8]
-            for way in (0, 1):
-                part = functools.partial(lambda k, f, w: f(k, w), f=parts[i][n], w=way)
-                held = functools.partial(lambda k, f, w: f(k, w), f=helds[i][n], w=way)
-                four = bufs[4 * way : 4 * way + 4]
-                one[i].append(
-                    RingItem(net, sides[i][0], places[i][0], part, held, way, four, own.at[way])
-                )
-            owns.append(own)
-            bufs = bufs[9:]
-        for n in range(len(last[i])):
-            part = functools.partial(lambda k, f, o: f(o, k), f=seconds[i][n], o=owns[n])
-            two[i].append(
-                RingItem(net, sides[i][1], places[i][1], part, part, n % 2, bufs[:4], finals[i][n])
-            )
-            bufs = bufs[4:]
-
-    def mix(pair):
-        return [item for items in zip(*pair, strict=True) for item in items]
-
-    return mix(one), mix(two)
-
-
-def ffn_items(net, at, far_refs, near_refs, gu_own, down_own, bufs):
-    def parts_of(gu, down):
-        return (
-            (
-                lambda k, way: gu.at[way, pl.ds(0, 2), :, k],
-                lambda k, way: down.at[way, :, down_rows(k), LEFT],
-            ),
-            (
-                lambda k, way: gu.at[k // 2, pl.ds(2, 2), k % 2, pl.ds(2 * way, 2)],
-                lambda k, way: down.at[k // 2, k % 2, pl.ds(144 * way, 144), RIGHT],
-            ),
-        )
-
-    parts, helds = parts_of(*far_refs), parts_of(*near_refs)
-    seconds = (
-        (lambda own, k: own.at[k // 2, :, k % 2], lambda own, k: own.at[k // 2, k % 2]),
-        (
-            lambda own, k: own.at[k // 2, :, k % 2],
-            lambda own, k: own.at[k // 2, pl.ds(pl.multiple_of((k % 2) * 64, 64), 80)],
-        ),
-    )
-    finals = (
-        (gu_own.at[pl.ds(0, 2)], down_own.at[:, LEFT]),
-        (gu_own.at[pl.ds(2, 2)], down_own.at[:, RIGHT]),
-    )
-    return ring_items(net, at, FFN_FIRST, FFN_LAST, parts, helds, seconds, finals, bufs)
-
-
-def small_items(net, at, qkv, out, qkv_own, out_own, bufs):
-    parts = (
-        (lambda k, way: qkv.at[:, k, :, pl.ds(512 * way, 512)],),
-        (lambda k, way: out.at[k // 2, k % 2, pl.ds(2 * way, 2)],),
-    )
-    seconds = ((lambda own, k: own.at[k // 2, k % 2],), (lambda own, k: own.at[k // 2, k % 2],))
-    finals = ((qkv_own,), (out_own,))
-    return ring_items(net, at, SMALL_FIRST, SMALL_LAST, parts, parts, seconds, finals, bufs)
 
 
 def backward_kernel(
@@ -916,13 +936,13 @@
     ow_far,
     qw_far,
     gu_far,
-    down_far,
+    down_own,
     grad_in,
     grad_out,
     grad_qkv,
     small_ref,
     gu_own,
-    down_own,
+    all_down,
     sums_ref,
     sums_in,
     attn_all,
@@ -942,7 +962,6 @@
     ow,
     qw,
     gu,
-    down,
     *rest,
 ):
     bufs, (send_sems, recv_sems, local_sems) = rest[:-3], rest[-3:]
@@ -951,7 +970,7 @@
     held = [
         pltpu.make_async_copy(src, dst, local_sems.at[i])
         for i, (src, dst) in enumerate(
-            ((ow_far, ow), (gu_far, gu), (down_far, down), (qw_far, qw))
+            ((ow_far, ow), (gu_far, gu), (qw_far, qw))
         )
     ]
     for copy in held:
@@ -959,8 +978,22 @@
     at.meet(
         (at.S, at.O, at.OS, at.N1, at.N2, at.N1S, at.N2S, at.YP, at.YM, at.ZP, at.ZM)
     )
-    first, last = ffn_items(net, at, (gu_far, down_far), (gu, down), gu_own, down_own, bufs)
+    first, last = gu_items(net, at, gu_far, gu, gu_own, bufs)
     begin(first)
+
+    def down_slot(k, cols):
+        return all_down.at[cols, pl.ds(pl.multiple_of(k * 80, 16), 80), :]
+
+    down_keys = [
+        net.send(down_own.at[:, pl.ds(aligned(col, FEAT), FEAT)], down_slot(at.dp, at.col), device)
+        for device, col in ((at.S, at.sib), (at.O, at.far), (at.OS, at.sibfar))
+    ]
+    down_mine = pltpu.make_async_copy(
+        down_own.at[:, pl.ds(aligned(at.col, FEAT), FEAT)],
+        down_slot(at.dp, at.col),
+        local_sems.at[3],
+    )
+    down_mine.start()
     peers = ((at.S, at.sib), (at.O, at.far), (at.OS, at.sibfar))
     pair = (at.col, 7 - at.col)
 
@@ -1033,7 +1066,6 @@
         d_attn[pl.ds(j * BLOCK, BLOCK), :] = dot(mid_pair[j], ow[...], 1, 1).astype(BF)
     d_kv[...] = jnp.zeros_like(d_kv)
     held[1].wait()
-    held[2].wait()
     for item in first:
         item.middle()
 
@@ -1077,6 +1109,18 @@
     for item in first:
         item.end()
     begin(last)
+    down_mine.wait()
+    for key, (_, col) in zip(down_keys, peers, strict=True):
+        net.take(key, down_slot(at.dp, col))
+    ring = ring_dp(
+        net,
+        at,
+        (
+            lambda zz, yy: [down_slot(zz * 4 + yy, pl.ds(2 * at.hi, 2))],
+            lambda zz, yy: [down_slot(zz * 4 + yy, pl.ds(2 * (1 - at.hi), 2))],
+        ),
+    )
+    next(ring)
     gather_attn.end()
     for key, (_, row, col) in zip(spread, others, strict=True):
         net.take(key, mid_cols.at[rows_at(block_of(row, col)), :])
@@ -1093,8 +1137,11 @@
         d_qkv_all[rows_at(pair[j]), pl.ds(QCOLS + HEAD, HEAD)] = total[:, HEAD:].astype(BF)
     gather_qkv = GatherCol(d_qkv_all)
     gather_qkv.start()
-
-    held[3].wait()
+    for item in last:
+        item.middle()
+    next(ring)
+
+    held[2].wait()
     part_out[...] = dot(d_qkv_all[rows_at(block_of(1 - at.row, at.col)), :], qw[...], 1, 1).astype(BF)
     part = net.send(part_out, part_in, at.N1)
     d_normed = dot(d_qkv_all[rows_at(at.block), :], qw[...], 1, 1)
@@ -1118,9 +1165,10 @@
         for device, col in peers
     ]
     gi_in[half_rows, :] = gi_out[:, cols_at(at.col)]
-    for item in last:
-        item.middle()
+    next(ring)
+    next(ring)
     gather_qkv.middle()
+    next(ring)
     gather_qkv.end()
     grad_qkv[...] = dot(n1c[...], d_qkv_all[...], 0, 0).astype(BF)
     ones = jnp.ones((8, SEQ), BF)
@@ -1136,6 +1184,7 @@
         net.take(key, gi_in.at[pl.ds(pl.multiple_of(offset * BLOCK, BLOCK), BLOCK), :])
     for item in last:
         item.end()
+    drain(ring)
     grad_in[...] = gi_in[...].astype(F32)
     net.finish()
 
@@ -1150,13 +1199,13 @@
         out((FEAT, QKV), BF),
         out((8, FEAT + QKV), F32),
         out((4, 48, PART), BF),
-        out((80, MODEL), BF),
+        out((4, 1280, FEAT), BF),
     )
     return pl.pallas_call(
         backward_kernel,
         out_shape=outs,
-        in_specs=[vmem()] * (len(args) - 4) + [anywhere()] * 4,
-        out_specs=[vmem()] * len(outs),
+        in_specs=[vmem()] * (len(args) - 4) + [anywhere()] * 3 + [vmem()],
+        out_specs=[vmem()] * (len(outs) - 1) + [anywhere()],
         scratch_shapes=[
             pltpu.VMEM((8, MODEL), F32),
             pltpu.VMEM((8, 8, FEAT), F32),
@@ -1177,10 +1226,9 @@
             pltpu.VMEM((QCOLS, MODEL), BF),
             pltpu.VMEM((MODEL, QKV), BF),
             pltpu.VMEM((2, 4, 2, 4, 48, PART), BF),
-            pltpu.VMEM((2, 2, 288, MODEL), BF),
         ]
-        + ring_scratch(FFN_FIRST, FFN_LAST)
-        + [pltpu.SemaphoreType.DMA((80,)), pltpu.SemaphoreType.DMA((80,))]
+        + ring_scratch(GU_FIRST, GU_LAST)
+        + [pltpu.SemaphoreType.DMA((110,)), pltpu.SemaphoreType.DMA((110,))]
         + [pltpu.SemaphoreType.DMA((4,))],
         compiler_params=pltpu.CompilerParams(
             collective_id=2, has_side_effects=True, vmem_limit_bytes=VMEM_LIMIT
@@ -1194,7 +1242,6 @@
 
 def sums_kernel(
     gu_own,
-    down_own,
     qkv,
     out,
     small_ref,
@@ -1202,7 +1249,6 @@
     hidden_far,
     dw_far,
     all_gu,
-    all_down,
     all_qkv,
     all_out,
     small_out,
@@ -1250,12 +1296,6 @@
     def part_lanes(col):
         return pl.ds(aligned(col, PART), PART)
 
-    def down_slot(col):
-        return all_down.at[col, pl.ds(pl.multiple_of(at.dp * 80, 16), 80), :]
-
-    def feat_lanes(col):
-        return pl.ds(aligned(col, FEAT), FEAT)
-
     def qkv_piece(k):
         rows = pl.ds(pl.multiple_of((k % 8) * 48, 16), 48)
         return all_qkv.at[rows, pl.ds(pl.multiple_of((k // 8) * 512, 512), 512)]
@@ -1267,10 +1307,7 @@
     keys = []
     for device, col in peers:
         keys.append(
-            (
-                net.send(gu_own.at[col], gu_piece(at.dp, part_lanes(at.col)), device),
-                net.send(down_own.at[:, feat_lanes(col)], down_slot(at.col), device),
-            )
+            net.send(gu_own.at[col], gu_piece(at.dp, part_lanes(at.col)), device)
         )
     small_y[y] = small_ref[...]
     small_keys = [net.send(small_ref, small_y.at[y], d) for d in (at.YP, at.YM, at.Y2)]
@@ -1280,16 +1317,12 @@
         pltpu.make_async_copy(
             gu_own.at[at.col], gu_piece(at.dp, part_lanes(at.col)), local_sems.at[0]
         ),
-        pltpu.make_async_copy(
-            down_own.at[:, feat_lanes(at.col)], down_slot(at.col), local_sems.at[1]
-        ),
     ]
     for copy in own_copies:
         copy.start()
 
     def take_from(i):
-        net.take(keys[i][0], gu_piece(at.dp, part_lanes(peers[i][1])))
-        net.take(keys[i][1], down_slot(peers[i][1]))
+        net.take(keys[i], gu_piece(at.dp, part_lanes(peers[i][1])))
 
     def chip_ready():
         for copy in own_copies:
@@ -1303,11 +1336,7 @@
     def half_of(hi):
         def half(zz, yy):
             k = zz * 4 + yy
-            rows = pl.ds(pl.multiple_of(k * 80, 16), 80)
-            return [
-                gu_piece(k, pl.ds(aligned(hi, 2 * PART), 2 * PART)),
-                all_down.at[pl.ds(2 * hi, 2), rows, :],
-            ]
+            return [gu_piece(k, pl.ds(aligned(hi, 2 * PART), 2 * PART))]
 
         return half
 
@@ -1353,13 +1382,12 @@
     net.finish()
 
 
-def run_sums(gu, down, qkv, out, small, mid, hidden, dw):
+def run_sums(gu, qkv, out, small, mid, hidden, dw):
     def shape(dims, dtype):
         return jax.ShapeDtypeStruct(dims, dtype)
 
     outs = (
         shape((2, FEAT, 4 * PART), BF),
-        shape((4, 1280, FEAT), BF),
         shape((FEAT, QKV), BF),
         shape((QCOLS, FEAT), BF),
         shape(small.shape, F32),
@@ -1368,8 +1396,8 @@
     return pl.pallas_call(
         sums_kernel,
         out_shape=outs,
-        in_specs=[vmem()] * 6 + [anywhere()] * 2,
-        out_specs=[anywhere()] * 2 + [vmem()] * 4,
+        in_specs=[vmem()] * 5 + [anywhere()] * 2,
+        out_specs=[anywhere()] + [vmem()] * 4,
         scratch_shapes=[pltpu.VMEM((4,) + small.shape, F32)] * 2
         + [
             pltpu.VMEM((SEQ, PART), BF),
@@ -1387,7 +1415,7 @@
             flops=4 * 10**9, bytes_accessed=60 * 10**6, transcendentals=0
         ),
         name="sums_over_sequences",
-    )(gu, down, qkv, out, small, mid, hidden, dw)
+    )(gu, qkv, out, small, mid, hidden, dw)
 
 
 def widen_kernel(
@@ -1592,11 +1620,10 @@
         out_w,
         qkv_w,
         grad_gu.reshape(2, 4, 2, 4, 48, PART),
-        grad_down.reshape(2, 2, 288, MODEL),
-    )
-    grad_gu, grad_down, grad_qkv, grad_out, small, layer_output = run_sums(
+        grad_down,
+    )
+    grad_gu, grad_qkv, grad_out, small, layer_output = run_sums(
         grad_gu,
-        grad_down,
         grad_qkv.reshape(2, 4, 48, QKV),
         grad_out.reshape(2, 2, 4, 48, FEAT),
         small,

time: 351 us -> 339 us (0.966)
  Pallas kernels: 336 us -> 324 us
    pallas_call x1, Pallas kernels: 89.6 us -> 68.4 us  [run_sums(): pl.pallas_call(sums_kernel, out_shape=outs, in_specs=[vmem()] * 5 + [anyw...]
    pallas_call x1, Pallas kernels: 146 us -> 156 us  [run_forward(): pl.pallas_call(forward_kernel, out_shape=[jax.ShapeDtypeStruct(dims, dtyp...]
where the time goes in v7:
time: 339 us; the launch traced here: 334 us
  Pallas kernels  324 us (96%)
  other arithmetic  5.11 us (2%)
  local copies, waits for them, and re-layouts  4.44 us (1%)
    pallas_call x1, Pallas kernels, run_forward(): pl.pallas_call(forward_kernel, out_shape=[jax.ShapeDtypeStruct(dims, dtyp...  156 us
    pallas_call x1, Pallas kernels, run_backward(): pl.pallas_call(backward_kernel, out_shape=outs, in_specs=[vmem()] * (len(...  84.9 us
    pallas_call x1, Pallas kernels, run_sums(): pl.pallas_call(sums_kernel, out_shape=outs, in_specs=[vmem()] * 5 + [anyw...  68.4 us
    pallas_call x1, Pallas kernels, run_widen(): pl.pallas_call(widen_kernel, out_shape=[jax.ShapeDtypeStruct(dims, F32) f...  15.1 us

profile of v7, /device:TPU:0, one launch (start us, length us, event | category | flops | bytes accessed | tf_op | source)
XLA Modules:
  0.0 334.4 jit_solution(12466915048506635369)
XLA Ops:
  0.6 0.7 reshape.133
  1.3 0.7 reshape.138
  2.0 0.7 concatenate.20
  2.7 1.3 maximum_convert_fusion.bias_ref
  4.0 0.0 copy-start.2
  4.0 0.6 copy-done.2
  4.6 155.6 %forward_and_feed_forward.1 = (bf16[128,1536]{1,0:T(8,128)(2,1)}, bf16[1024,384]{1,0:T(8,128)(2,1)}, bf16[128,1536]{1,0:T(8,128)(2,1)}, bf16[1536,1024]{1,0:T(8,...) custom-call(bf16[512,384]{1,0:T(8,128)(2,1)} %x_ref.1, ...), custom_call_target="tpu_custom_call" | custom-call | flops 36999999488 | bytes 80000000 | tf_op jit(solution)/shard_map/forward_and_feed_forward/pallas_call | solution.py:882
  160.2 84.9 %attention_backward.1 = (f32[512,384]{1,0:T(8,128)}, bf16[768,384]{1,0:T(8,128)(2,1)}, bf16[384,1024]{1,0:T(8,128)(2,1)}, f32[8,1408]{1,0:T(8,128)}, bf16[4,48,1...) custom-call(f32[128,1536]{1,0:T(8,128)} %get-tuple-element.78.dn2_ref, f32[128,1536]{1,0:T(8,128)} %get-tuple-element.79.mid_ref, ...), custom_call_target="tpu_custom_call" | custom-call | flops 10000000000 | bytes 40000000 | tf_op jit(solution)/shard_map/attention_backward/pallas_call | solution.py:1204
  245.0 68.4 %sums_over_sequences.1 = (bf16[2,384,4608]{2,1,0:T(8,128)(2,1)}, bf16[384,1024]{1,0:T(8,128)(2,1)}, bf16[768,384]{1,0:T(8,128)(2,1)}, f32[8,1408]{1,0:T(8,128)}, f32[512,384]{1,0:T(8,128)}) custom-call(bf16[4,48,1152]{2,1,0:T(8,128)(2,1)} %get-tuple-element.93.gu_own, bf16[2,4,48,1024]{3,2,1,0:T(8,128)(2,1)} %bitcast.12, ...), custom_call_target="tpu_custom_call" | custom-call | flops 4000000000 | bytes 60000000 | tf_op jit(solution)/shard_map/sums_over_sequences/pallas_call | solution.py:1396
  313.4 0.0 copy-start.1
  313.4 0.0 copy-start
  313.4 15.1 %widen.1 = (f32[384,4480]{1,0:T(8,128)}, f32[384,4480]{1,0:T(8,128)}, f32[4480,384]{1,0:T(8,128)}, f32[384,768]{1,0:T(8,128)}, f32[384,128]{1,0:T(8,128)}, /*ind...) custom-call(bf16[2,384,4608]{2,1,0:T(8,128)(2,1)} %get-tuple-element, ...), custom_call_target="tpu_custom_call" | custom-call | flops 10000000 | bytes 36000000 | tf_op jit(solution)/shard_map/widen/pallas_call | solution.py:1523
  328.5 1.3 reduce.4
  329.8 1.3 reduce.6
  331.0 1.3 reduce.5
  332.3 0.0 copy-done.1
  332.3 0.9 copy.33
  333.2 0.0 copy-done
  333.2 0.9 copy.34
  (2 shorter events, 0.0 us)
Async XLA Ops:
  4.0 0.6 copy-start.2
  313.4 18.9 %copy-start.1 = (f32[512,384]{1,0:T(8,128)S(1)}, f32[512,384]{1,0:T(8,128)}, u32[]{:S(2)}) copy-start(f32[512,384]{1,0:T(8,128)} %get-tuple-element.132) | copy-start | bytes 2359300
  313.4 19.8 %copy-start = (f32[512,384]{1,0:T(8,128)S(1)}, f32[512,384]{1,0:T(8,128)}, u32[]{:S(2)}) copy-start(f32[512,384]{1,0:T(8,128)} %get-tuple-element.133) | copy-start | bytes 2359300

commit v8 on v7

--- a/solution.py
+++ b/solution.py
@@ -249,6 +249,34 @@
     return pl.BlockSpec(memory_space=pl.ANY)
 
 
+class GatherCol:
+    def __init__(self, net, at, array):
+        self.net, self.at, self.array = net, at, array
+
+    def rows(self, col, j):
+        return self.array.at[pl.ds(aligned(col + j * (7 - 2 * col), BLOCK), BLOCK), :]
+
+    def start(self):
+        net, at = self.net, self.at
+        mine = [self.rows(at.col, j) for j in (0, 1)]
+        self.far = [net.send(ref, ref, at.O) for ref in mine]
+        self.sib = [net.send(ref, ref, at.S) for ref in mine]
+
+    def middle(self):
+        net, at = self.net, self.at
+        self.onward = []
+        for j in (0, 1):
+            ref = self.rows(at.far, j)
+            net.take(self.far[j], ref)
+            self.onward.append(net.send(ref, ref, at.S))
+
+    def end(self):
+        net, at = self.net, self.at
+        for j in (0, 1):
+            net.take(self.sib[j], self.rows(at.sib, j))
+            net.take(self.onward[j], self.rows(at.sibfar, j))
+
+
 class Reduce8:
     def __init__(self, net, at, own, other, sib_in, first_in, last_in, near_in, away_in):
         self.net, self.at, self.own, self.other, self.sib_in = net, at, own, other, sib_in
@@ -479,7 +507,7 @@
     k_ref,
     v_ref,
     lse_ref,
-    attn_ref,
+    attn_all,
     mid_ref,
     gains_all,
     dn2_ref,
@@ -502,6 +530,7 @@
     d_up,
     tile_buf,
     down,
+    attn_ref,
     *rest,
 ):
     red_a, bufs, sems = rest[:7], rest[7:-4], rest[-4:]
@@ -758,6 +787,10 @@
             d_up[rows, lanes] = dot(og_all[rows, :], dw[lanes, :], 1, 1).astype(BF)
         return carry
 
+    gather_attn = GatherCol(net, at, attn_all)
+    for j in (0, 1):
+        gather_attn.rows(at.col, j)[...] = attn_ref[pl.ds(j * BLOCK, BLOCK), :]
+    gather_attn.start()
     lax.fori_loop(0, 4, hidden_back, 0)
     move(dw, dw_out)
     net.take(near[0], gw.at[pl.ds(aligned(at.sib, FEAT), FEAT), :])
@@ -798,6 +831,7 @@
         tile = dot(hidden[...], og_all[:, lanes], 0, 0).astype(BF)
         for q in range(4):
             down[q // 2, q % 2, :, lanes] = tile[288 * q : 288 * (q + 1)]
+    gather_attn.middle()
     sums, last_sums = down_items(net, at, down, down_own, bufs)
     begin(sums)
     for j in range(4):
@@ -834,6 +868,7 @@
             )
             writes[-1].start()
 
+    gather_attn.end()
     for item in sums:
         item.middle()
     outer_sum(n2_all, d_gate, grad_gu.at[0])
@@ -870,7 +905,7 @@
         ((SEQ, HEAD), BF, vmem),
         ((SEQ, HEAD), BF, vmem),
         ((2 * HEADS, BLOCK, 1), F32, vmem),
-        ((2 * BLOCK, QCOLS), BF, vmem),
+        ((SEQ, QCOLS), BF, vmem),
         ((BLOCK, MODEL), F32, vmem),
         ((8, MODEL), F32, vmem),
         ((BLOCK, MODEL), F32, vmem),
@@ -900,6 +935,7 @@
             pltpu.VMEM((SEQ, PART), BF),
             pltpu.VMEM((2, MODEL, 256), BF),
             pltpu.VMEM((2, 2, 288, MODEL), BF),
+            pltpu.VMEM((2 * BLOCK, QCOLS), BF),
         ]
         + reduce8_scratch(BLOCK, MODEL)
         + ring_scratch(DOWN_FIRST, DOWN_LAST)
@@ -924,9 +960,8 @@
     mid_ref,
     og_ref,
     gains_all,
-    xs_ref,
     n1c,
-    attn_ref,
+    attn_all,
     q_ref,
     k_ref,
     v_ref,
@@ -934,33 +969,25 @@
     cos_ref,
     sin_ref,
     ow_far,
-    qw_far,
     gu_far,
     down_own,
-    grad_in,
     grad_out,
     grad_qkv,
-    small_ref,
+    sums_ref,
+    d_mid,
+    d_qkv_own,
+    bias_ref,
     gu_own,
     all_down,
-    sums_ref,
-    sums_in,
-    attn_all,
     mid_cols,
     mid_pair,
-    d_mid,
     d_attn,
     d_q,
     d_kv,
     kv_out,
     kv_in,
     d_qkv_all,
-    part_out,
-    part_in,
-    gi_out,
-    gi_in,
     ow,
-    qw,
     gu,
     *rest,
 ):
@@ -970,7 +997,7 @@
     held = [
         pltpu.make_async_copy(src, dst, local_sems.at[i])
         for i, (src, dst) in enumerate(
-            ((ow_far, ow), (gu_far, gu), (qw_far, qw))
+            ((ow_far, ow), (gu_far, gu))
         )
     ]
     for copy in held:
@@ -1003,33 +1030,7 @@
     def cols_at(col):
         return pl.ds(aligned(col, FEAT), FEAT)
 
-    class GatherCol:
-        def __init__(self, array):
-            self.array = array
-
-        def rows(self, col, j):
-            return self.array.at[rows_at(col + j * (7 - 2 * col)), :]
-
-        def start(self):
-            self.far = [net.send(self.rows(at.col, j), self.rows(at.col, j), at.O) for j in (0, 1)]
-            self.sib = [net.send(self.rows(at.col, j), self.rows(at.col, j), at.S) for j in (0, 1)]
-
-        def middle(self):
-            self.onward = []
-            for j in (0, 1):
-                net.take(self.far[j], self.rows(at.far, j))
-                self.onward.append(net.send(self.rows(at.far, j), self.rows(at.far, j), at.S))
-
-        def end(self):
-            for j in (0, 1):
-                net.take(self.sib[j], self.rows(at.sib, j))
-                net.take(self.onward[j], self.rows(at.sibfar, j))
-
-    gather_attn = GatherCol(attn_all)
-    for j in (0, 1):
-        attn_all[rows_at(pair[j]), :] = attn_ref[pl.ds(j * BLOCK, BLOCK), :]
-
-    gain1, gain2 = gains_all[0:1, :], gains_all[1:2, :]
+    gain2 = gains_all[1:2, :]
     mid = mid_ref[...]
     scale = rms(mid)
     unit = mid * scale
@@ -1059,7 +1060,6 @@
                 mid_pair.at[at.row, :, cols_at(col)], mid_cols.at[rows_at(at.block), :], device
             )
         )
-    gather_attn.start()
     net.take(to_pair, mid_pair.at[1 - at.row])
     held[0].wait()
     for j in (0, 1):
@@ -1088,7 +1088,6 @@
             return carry
 
         lax.fori_loop(0, HEADS, back, 0)
-    gather_attn.middle()
 
     kv_out[...] = d_kv[...].astype(BF)
     kv_keys = [
@@ -1121,7 +1120,6 @@
         ),
     )
     next(ring)
-    gather_attn.end()
     for key, (_, row, col) in zip(spread, others, strict=True):
         net.take(key, mid_cols.at[rows_at(block_of(row, col)), :])
     grad_out[...] = dot(attn_all[...], mid_cols[...], 0, 0).astype(BF)
@@ -1135,36 +1133,14 @@
             key * cosines[j] - turn(key) * sines[j]
         ).astype(BF)
         d_qkv_all[rows_at(pair[j]), pl.ds(QCOLS + HEAD, HEAD)] = total[:, HEAD:].astype(BF)
-    gather_qkv = GatherCol(d_qkv_all)
+    gather_qkv = GatherCol(net, at, d_qkv_all)
     gather_qkv.start()
     for item in last:
         item.middle()
     next(ring)
 
-    held[2].wait()
-    part_out[...] = dot(d_qkv_all[rows_at(block_of(1 - at.row, at.col)), :], qw[...], 1, 1).astype(BF)
-    part = net.send(part_out, part_in, at.N1)
-    d_normed = dot(d_qkv_all[rows_at(at.block), :], qw[...], 1, 1)
-    net.take(part, part_in)
-    d_normed = d_normed + part_in[...].astype(F32)
-    values = xs_ref[...].astype(F32)
-    scale = rms(values)
-    unit = values * scale
-    sums_ref[0:1, :] = jnp.sum(d_normed * unit, axis=0, keepdims=True)
-    bent = d_normed * gain1
-    total = d_mid[...] + scale * (bent - unit * jnp.mean(bent * unit, axis=1, keepdims=True))
-    gi_out[...] = total.astype(BF)
-    sums_in[at.row * 4 + at.col] = sums_ref[:, cols_at(at.col)]
-    sums_keys = [
-        net.send(sums_ref.at[:, cols_at(col)], sums_in.at[at.row * 4 + at.col], device)
-        for device, row, col in others
-    ]
-    half_rows = pl.ds(pl.multiple_of((at.block - 4 * at.row) * BLOCK, BLOCK), BLOCK)
-    gi_keys = [
-        net.send(gi_out.at[:, cols_at(col)], gi_in.at[half_rows, :], device)
-        for device, col in peers
-    ]
-    gi_in[half_rows, :] = gi_out[:, cols_at(at.col)]
+    for j in (0, 1):
+        d_qkv_own[j] = d_qkv_all[rows_at(pair[j]), :]
     next(ring)
     next(ring)
     gather_qkv.middle()
@@ -1172,20 +1148,10 @@
     gather_qkv.end()
     grad_qkv[...] = dot(n1c[...], d_qkv_all[...], 0, 0).astype(BF)
     ones = jnp.ones((8, SEQ), BF)
-    small_ref[:, FEAT:] = dot(ones, d_qkv_all[...])
-    for key, (_, row, col) in zip(sums_keys, others, strict=True):
-        net.take(key, sums_in.at[row * 4 + col])
-    total = sums_in[0]
-    for i in range(1, 8):
-        total = total + sums_in[i]
-    small_ref[:, :FEAT] = total
-    for key, (_, col) in zip(gi_keys, peers, strict=True):
-        offset = block_of(at.row, col) - 4 * at.row
-        net.take(key, gi_in.at[pl.ds(pl.multiple_of(offset * BLOCK, BLOCK), BLOCK), :])
+    bias_ref[...] = dot(ones, d_qkv_all[...])
     for item in last:
         item.end()
     drain(ring)
-    grad_in[...] = gi_in[...].astype(F32)
     net.finish()
 
 
@@ -1194,37 +1160,30 @@
         return jax.ShapeDtypeStruct(shape, dtype)
 
     outs = (
-        out((SEQ // 2, FEAT), F32),
         out((QCOLS, FEAT), BF),
         out((FEAT, QKV), BF),
-        out((8, FEAT + QKV), F32),
+        out((8, MODEL), F32),
+        out((BLOCK, MODEL), F32),
+        out((2, BLOCK, QKV), BF),
+        out((8, QKV), F32),
         out((4, 48, PART), BF),
         out((4, 1280, FEAT), BF),
     )
     return pl.pallas_call(
         backward_kernel,
         out_shape=outs,
-        in_specs=[vmem()] * (len(args) - 4) + [anywhere()] * 3 + [vmem()],
+        in_specs=[vmem()] * (len(args) - 3) + [anywhere()] * 2 + [vmem()],
         out_specs=[vmem()] * (len(outs) - 1) + [anywhere()],
         scratch_shapes=[
-            pltpu.VMEM((8, MODEL), F32),
-            pltpu.VMEM((8, 8, FEAT), F32),
-            pltpu.VMEM((SEQ, QCOLS), BF),
             pltpu.VMEM((SEQ, FEAT), BF),
             pltpu.VMEM((2, BLOCK, MODEL), BF),
-            pltpu.VMEM((BLOCK, MODEL), F32),
             pltpu.VMEM((2 * BLOCK, QCOLS), BF),
             pltpu.VMEM((2 * BLOCK, QCOLS), F32),
             pltpu.VMEM((SEQ, 2 * HEAD), F32),
             pltpu.VMEM((SEQ, 2 * HEAD), BF),
             pltpu.VMEM((3, 2, BLOCK, 2 * HEAD), BF),
             pltpu.VMEM((SEQ, QKV), BF),
-            pltpu.VMEM((BLOCK, MODEL), BF),
-            pltpu.VMEM((BLOCK, MODEL), BF),
-            pltpu.VMEM((BLOCK, MODEL), BF),
-            pltpu.VMEM((SEQ // 2, FEAT), BF),
             pltpu.VMEM((QCOLS, MODEL), BF),
-            pltpu.VMEM((MODEL, QKV), BF),
             pltpu.VMEM((2, 4, 2, 4, 48, PART), BF),
         ]
         + ring_scratch(GU_FIRST, GU_LAST)
@@ -1244,33 +1203,49 @@
     gu_own,
     qkv,
     out,
-    small_ref,
+    sums_ref,
+    d_mid,
+    d_qkv,
+    bias_ref,
+    xs_ref,
+    gains_all,
     mid_ref,
     hidden_far,
     dw_far,
+    qw_far,
     all_gu,
     all_qkv,
     all_out,
     small_out,
     out_ref,
+    grad_in,
     small_y,
     small_z,
     hidden,
     dw,
     ffn,
+    qw,
+    part_out,
+    part_in,
+    gi_out,
+    gi_in,
+    gain_sums,
+    sums_in,
     *rest,
 ):
     red, bufs, (send_sems, recv_sems, local_sems) = rest[:7], rest[7:-3], rest[-3:]
     at = Place()
     net = Net(send_sems, recv_sems, at)
     held = [
+        pltpu.make_async_copy(qw_far, qw, local_sems.at[1]),
         pltpu.make_async_copy(hidden_far, hidden, local_sems.at[2]),
         pltpu.make_async_copy(dw_far, dw, local_sems.at[3]),
     ]
     for copy in held:
         copy.start()
     at.meet(
-        (at.S, at.O, at.OS, at.N1, at.N2, at.YP, at.YM, at.ZP, at.ZM, at.Y2, at.Z2)
+        (at.S, at.O, at.OS, at.N1, at.N2, at.N1S, at.N2S)
+        + (at.YP, at.YM, at.ZP, at.ZM, at.Y2, at.Z2)
     )
     outs = Reduce8(net, at, *red)
 
@@ -1296,6 +1271,9 @@
     def part_lanes(col):
         return pl.ds(aligned(col, PART), PART)
 
+    def feat_lanes(col):
+        return pl.ds(aligned(col, FEAT), FEAT)
+
     def qkv_piece(k):
         rows = pl.ds(pl.multiple_of((k % 8) * 48, 16), 48)
         return all_qkv.at[rows, pl.ds(pl.multiple_of((k // 8) * 512, 512), 512)]
@@ -1309,8 +1287,9 @@
         keys.append(
             net.send(gu_own.at[col], gu_piece(at.dp, part_lanes(at.col)), device)
         )
-    small_y[y] = small_ref[...]
-    small_keys = [net.send(small_ref, small_y.at[y], d) for d in (at.YP, at.YM, at.Y2)]
+    held[0].wait()
+    part_out[...] = dot(d_qkv[1 - at.row], qw[...], 1, 1).astype(BF)
+    part = net.send(part_out, part_in, at.N1)
     first, last = small_items(net, at, qkv, out, qkv_piece(at.dp), out_piece(at.dp), bufs)
     begin(first)
     own_copies = [
@@ -1344,29 +1323,68 @@
         net, at, (half_of(at.hi), half_of(1 - at.hi)), (chip_ready, far_ready)
     )
     next(ring)
-    for copy in held:
-        copy.wait()
+    for item in first:
+        item.middle()
+    d_normed = dot(d_qkv[at.row], qw[...], 1, 1)
+    net.take(part, part_in)
+    d_normed = d_normed + part_in[...].astype(F32)
+    values = xs_ref[...].astype(F32)
+    scale = rms(values)
+    unit = values * scale
+    gain_sums[...] = sums_ref[...]
+    gain_sums[0:1, :] = jnp.sum(d_normed * unit, axis=0, keepdims=True)
+    bent = d_normed * gains_all[0:1, :]
+    total = d_mid[...] + scale * (bent - unit * jnp.mean(bent * unit, axis=1, keepdims=True))
+    gi_out[...] = total.astype(BF)
+
+    def half_block(col):
+        offset = block_of(at.row, col) - 4 * at.row
+        return gi_in.at[pl.ds(pl.multiple_of(offset * BLOCK, BLOCK), BLOCK), :]
+
+    gi_keys = [
+        net.send(gi_out.at[:, feat_lanes(col)], half_block(at.col), device)
+        for device, col in peers
+    ]
+    half_block(at.col)[...] = gi_out[:, feat_lanes(at.col)]
+    others = (
+        (at.S, at.row, at.sib),
+        (at.N1, 1 - at.row, at.col),
+        (at.N1S, 1 - at.row, at.sib),
+        (at.O, at.row, at.far),
+        (at.OS, at.row, at.sibfar),
+        (at.N2, 1 - at.row, at.far),
+        (at.N2S, 1 - at.row, at.sibfar),
+    )
+    sums_in[at.row * 4 + at.col] = gain_sums[:, feat_lanes(at.col)]
+    sums_keys = [
+        net.send(gain_sums.at[:, feat_lanes(col)], sums_in.at[at.row * 4 + at.col], device)
+        for device, row, col in others
+    ]
+    next(ring)
+    held[1].wait()
+    held[2].wait()
     project(0)
     for item in first:
+        item.end()
+    begin(last)
+    next(ring)
+    project(1)
+    for key, (_, row, col) in zip(sums_keys, others, strict=True):
+        net.take(key, sums_in.at[row * 4 + col])
+    total = sums_in[0]
+    for i in range(1, 8):
+        total = total + sums_in[i]
+    small_y[y, :, :FEAT] = total
+    small_y[y, :, FEAT:] = bias_ref[...]
+    small_keys = [net.send(small_y.at[y], small_y.at[y], d) for d in (at.YP, at.YM, at.Y2)]
+    for item in last:
         item.middle()
+    next(ring)
+    project(2)
     for key, k in zip(small_keys, (y - 1, y + 1, y + 2), strict=True):
         net.take(key, small_y.at[lax.rem(k + 4, 4)])
     small_z[z] = (small_y[0] + small_y[1]) + (small_y[2] + small_y[3])
     small_keys = [net.send(small_z.at[z], small_z.at[z], d) for d in (at.ZP, at.ZM, at.Z2)]
-    next(ring)
-    project(1)
-    for item in first:
-        item.end()
-    begin(last)
-    next(ring)
-    project(2)
-    for item in last:
-        item.middle()
-    for key, k in zip(small_keys, (z - 1, z + 1, z + 2), strict=True):
-        net.take(key, small_z.at[lax.rem(k + 4, 4)])
-    small_out[...] = (small_z[0] + small_z[1]) + (small_z[2] + small_z[3])
-    next(ring)
-    project(3)
     for item in last:
         item.end()
     after = ring_dp(
@@ -1375,6 +1393,15 @@
         (lambda zz, yy: [qkv_piece(zz * 4 + yy)], lambda zz, yy: [out_piece(zz * 4 + yy)]),
     )
     next(after)
+    next(ring)
+    project(3)
+    next(after)
+    for key, k in zip(small_keys, (z - 1, z + 1, z + 2), strict=True):
+        net.take(key, small_z.at[lax.rem(k + 4, 4)])
+    small_out[...] = (small_z[0] + small_z[1]) + (small_z[2] + small_z[3])
+    for key, (_, col) in zip(gi_keys, peers, strict=True):
+        net.take(key, half_block(col))
+    grad_in[...] = gi_in[...].astype(F32)
     for _ in ring:
         next(after, None)
     drain(after)
@@ -1382,7 +1409,7 @@
     net.finish()
 
 
-def run_sums(gu, qkv, out, small, mid, hidden, dw):
+def run_sums(gu, qkv, out, *args):
     def shape(dims, dtype):
         return jax.ShapeDtypeStruct(dims, dtype)
 
@@ -1390,19 +1417,27 @@
         shape((2, FEAT, 4 * PART), BF),
         shape((FEAT, QKV), BF),
         shape((QCOLS, FEAT), BF),
-        shape(small.shape, F32),
+        shape((8, FEAT + QKV), F32),
+        shape((SEQ // 2, FEAT), F32),
         shape((SEQ // 2, FEAT), F32),
     )
     return pl.pallas_call(
         sums_kernel,
         out_shape=outs,
-        in_specs=[vmem()] * 5 + [anywhere()] * 2,
-        out_specs=[anywhere()] + [vmem()] * 4,
-        scratch_shapes=[pltpu.VMEM((4,) + small.shape, F32)] * 2
+        in_specs=[vmem()] * len(args) + [anywhere()] * 3,
+        out_specs=[anywhere()] + [vmem()] * 5,
+        scratch_shapes=[pltpu.VMEM((4, 8, FEAT + QKV), F32)] * 2
         + [
             pltpu.VMEM((SEQ, PART), BF),
             pltpu.VMEM((PART, MODEL), BF),
             pltpu.VMEM((SEQ // 2, QCOLS), F32),
+            pltpu.VMEM((MODEL, QKV), BF),
+            pltpu.VMEM((BLOCK, MODEL), BF),
+            pltpu.VMEM((BLOCK, MODEL), BF),
+            pltpu.VMEM((BLOCK, MODEL), BF),
+            pltpu.VMEM((SEQ // 2, FEAT), BF),
+            pltpu.VMEM((8, MODEL), F32),
+            pltpu.VMEM((8, 8, FEAT), F32),
         ]
         + reduce8_scratch(SEQ // 2, FEAT)
         + ring_scratch(SMALL_FIRST, SMALL_LAST)
@@ -1415,7 +1450,7 @@
             flops=4 * 10**9, bytes_accessed=60 * 10**6, transcendentals=0
         ),
         name="sums_over_sequences",
-    )(gu, qkv, out, small, mid, hidden, dw)
+    )(gu, qkv, out, *args)
 
 
 def widen_kernel(
@@ -1490,9 +1525,9 @@
         (bk_out, 0, HEAD),
         (bv_out, 0, HEAD),
     ):
-        ref[...] = small[row : row + 1, first : first + width]
+        ref[...] = small[row, first : first + width]
         first += width
-    gain2_out[...] = small[1:2, :FEAT]
+    gain2_out[...] = small[1, :FEAT]
     leaving = {}
     for n in range(8):
         place = n % 2
@@ -1519,7 +1554,7 @@
 def run_widen(gu, down, qkv, out, small):
     shapes = [(FEAT, UNITS)] * 2 + [(UNITS, FEAT)]
     shapes += [(FEAT, QCOLS), (FEAT, HEAD), (FEAT, HEAD), (QCOLS, FEAT)]
-    shapes += [(1, FEAT), (1, FEAT), (1, QCOLS), (1, HEAD), (1, HEAD)]
+    shapes += [(FEAT,), (FEAT,), (QCOLS,), (HEAD,), (HEAD,)]
     return pl.pallas_call(
         widen_kernel,
         out_shape=[jax.ShapeDtypeStruct(dims, F32) for dims in shapes],
@@ -1603,12 +1638,11 @@
         cosine,
         sine,
     )
-    grad_input, grad_out, grad_qkv, small, grad_gu, grad_down = run_backward(
+    grad_out, grad_qkv, sums, d_mid, d_qkv, bias_sums, grad_gu, grad_down = run_backward(
         dn2,
         mid,
         grads_block,
         gains_all,
-        xs,
         normed1_cols,
         attn,
         queries,
@@ -1618,18 +1652,23 @@
         cosine,
         sine,
         out_w,
-        qkv_w,
         grad_gu.reshape(2, 4, 2, 4, 48, PART),
         grad_down,
     )
-    grad_gu, grad_qkv, grad_out, small, layer_output = run_sums(
+    grad_gu, grad_qkv, grad_out, small, layer_output, grad_input = run_sums(
         grad_gu,
         grad_qkv.reshape(2, 4, 48, QKV),
         grad_out.reshape(2, 2, 4, 48, FEAT),
-        small,
+        sums,
+        d_mid,
+        d_qkv,
+        bias_sums,
+        xs,
+        gains_all,
         mid,
         hidden,
         down_w,
+        qkv_w,
     )
     (
         grad_gate,
@@ -1641,7 +1680,7 @@
         grad_out,
         *vectors,
     ) = run_widen(grad_gu, grad_down, grad_qkv, grad_out, small)
-    gain1, gain2, bias_query, bias_key, bias_value = (vector[0] for vector in vectors)
+    gain1, gain2, bias_query, bias_key, bias_value = vectors
     return (
         layer_output,
         grad_input,

time: 339 us -> 330 us (0.973)
  Pallas kernels: 324 us -> 318 us
  other arithmetic: 5.11 us -> 1.27 us
    pallas_call x1, Pallas kernels: 84.9 us -> 72.2 us  [run_backward(): pl.pallas_call(backward_kernel, out_shape=outs, in_specs=[vmem()] * (len(...]
    pallas_call x3 -> x0, other arithmetic: 3.84 us -> none  [run_widen(): pl.pallas_call(widen_kernel, out_shape=[jax.ShapeDtypeStruct(dims, F32) f...]
    pallas_call x1, Pallas kernels: 68.4 us -> 72.1 us  [run_sums(): pl.pallas_call(sums_kernel, out_shape=outs, in_specs=[vmem()] * len(args)...]
where the time goes in v8:
time: 330 us; the launch traced here: 325 us
  Pallas kernels  318 us (96%)
  local copies, waits for them, and re-layouts  4.44 us (1%)
    pallas_call x1, Pallas kernels, run_forward(): pl.pallas_call(forward_kernel, out_shape=[jax.ShapeDtypeStruct(dims, dtyp...  158 us
    pallas_call x1, Pallas kernels, run_backward(): pl.pallas_call(backward_kernel, out_shape=outs, in_specs=[vmem()] * (len(...  72.2 us
    pallas_call x1, Pallas kernels, run_sums(): pl.pallas_call(sums_kernel, out_shape=outs, in_specs=[vmem()] * len(args)...  72.1 us
    pallas_call x1, Pallas kernels, run_widen(): pl.pallas_call(widen_kernel, out_shape=[jax.ShapeDtypeStruct(dims, F32) f...  15.1 us

profile of v8, /device:TPU:0, one launch (start us, length us, event | category | flops | bytes accessed | tf_op | source)
XLA Modules:
  0.0 324.5 jit_solution(4638970381755204559)
XLA Ops:
  0.6 0.7 reshape.133
  1.3 0.7 reshape.138
  2.0 0.7 concatenate.20
  2.7 1.3 maximum_convert_fusion.bias_ref
  4.0 0.0 copy-start.2
  4.0 0.6 copy-done.2
  4.6 158.5 %forward_and_feed_forward.1 = (bf16[128,1536]{1,0:T(8,128)(2,1)}, bf16[1024,384]{1,0:T(8,128)(2,1)}, bf16[128,1536]{1,0:T(8,128)(2,1)}, bf16[1536,1024]{1,0:T(8,...) custom-call(bf16[512,384]{1,0:T(8,128)(2,1)} %x_ref.1, ...), custom_call_target="tpu_custom_call" | custom-call | flops 36999999488 | bytes 80000000 | tf_op jit(solution)/shard_map/forward_and_feed_forward/pallas_call | solution.py:917
  163.1 72.2 %attention_backward.1 = (bf16[768,384]{1,0:T(8,128)(2,1)}, bf16[384,1024]{1,0:T(8,128)(2,1)}, f32[8,1536]{1,0:T(8,128)}, f32[128,1536]{1,0:T(8,128)}, bf16[2,128...) custom-call(f32[128,1536]{1,0:T(8,128)} %get-tuple-element.81.dn2_ref, ...), custom_call_target="tpu_custom_call" | custom-call | flops 10000000000 | bytes 40000000 | tf_op jit(solution)/shard_map/attention_backward/pallas_call | solution.py:1172
  235.3 72.1 %sums_over_sequences.1 = (bf16[2,384,4608]{2,1,0:T(8,128)(2,1)}, bf16[384,1024]{1,0:T(8,128)(2,1)}, bf16[768,384]{1,0:T(8,128)(2,1)}, f32[8,1408]{1,0:T(8,128)}, f32[512,384]{1,0:T(8,128)}, /*index=5*/f32[512,384]{1,0:T(8,128)}) custom-call(bf16[4,48,1152]{2,1,0:T(8,128)(2,1)} %get-tuple-element.94.gu_own, bf16[2,4,48,1024]{3,2,1,0:T(8,128)(2,1)} %bitcast.8, ...), custom_call_target="tpu_custom_call" | custom-call | flops 4000000000 | bytes 60000000 | tf_op jit(solution)/shard_map/sums_over_sequences/pallas_call | solution.py:1424
  307.4 0.0 copy-start.1
  307.4 0.0 copy-start
  307.4 15.1 %widen.1 = (f32[384,4480]{1,0:T(8,128)}, f32[384,4480]{1,0:T(8,128)}, f32[4480,384]{1,0:T(8,128)}, f32[384,768]{1,0:T(8,128)}, f32[384,128]{1,0:T(8,128)}, /*ind...) custom-call(bf16[2,384,4608]{2,1,0:T(8,128)(2,1)} %get-tuple-element, ...), custom_call_target="tpu_custom_call" | custom-call | flops 10000000 | bytes 36000000 | tf_op jit(solution)/shard_map/widen/pallas_call | solution.py:1558
  322.5 0.0 copy-done.1
  322.5 0.9 copy.33
  323.4 0.0 copy-done
  323.4 0.9 copy.34
  (2 shorter events, 0.0 us)
Async XLA Ops:
  4.0 0.6 copy-start.2
  307.4 15.1 %copy-start.1 = (f32[512,384]{1,0:T(8,128)S(1)}, f32[512,384]{1,0:T(8,128)}, u32[]{:S(2)}) copy-start(f32[512,384]{1,0:T(8,128)} %get-tuple-element.138) | copy-start | bytes 2359300
  307.4 16.0 %copy-start = (f32[512,384]{1,0:T(8,128)S(1)}, f32[512,384]{1,0:T(8,128)}, u32[]{:S(2)}) copy-start(f32[512,384]{1,0:T(8,128)} %get-tuple-element.139) | copy-start | bytes 2359300

commit v9 on v8

--- a/solution.py
+++ b/solution.py
@@ -494,7 +494,6 @@
     wg_ref,
     wu_ref,
     wd_ref,
-    gains_ref,
     bias_ref,
     cos_ref,
     sin_ref,
@@ -531,6 +530,7 @@
     tile_buf,
     down,
     attn_ref,
+    gains_ref,
     *rest,
 ):
     red_a, bufs, sems = rest[:7], rest[7:-4], rest[-4:]
@@ -545,6 +545,9 @@
         local.append(copy)
         return copy
 
+    gains_ref[...] = jnp.zeros_like(gains_ref)
+    for i in (0, 1):
+        gains_ref[i : i + 1, :] = bias_ref[:, QKV + i * FEAT : QKV + (i + 1) * FEAT]
     joined = [
         move(wq_ref, wqkv_ref.at[:, pl.ds(0, QCOLS)]),
         move(wk_ref, wqkv_ref.at[:, pl.ds(QCOLS, HEAD)]),
@@ -640,15 +643,32 @@
         rows = pl.ds(pl.multiple_of(at.core * FEAT + (index % 8) * 48, 16), 48)
         return [ow.at[rows, pl.ds(pl.multiple_of(mine_far + (index // 8) * FEAT, HEAD), FEAT)]]
 
-    def ffn_slices(weights, first, count):
+    def rows_of(weights):
+        def slices(z, y):
+            return [weights.at[pl.ds(pl.multiple_of(mine_far + (z * 4 + y) * 48, 16), 48), :]]
+
+        return slices
+
+    def down_of(first, count):
         def slices(z, y):
             index = z * 4 + y
-            rows = pl.ds(pl.multiple_of(mine_far + index * 48, 16), 48)
-            down_rows = pl.ds(pl.multiple_of((index % 8) * 144 + first, 16), count)
+            rows = pl.ds(pl.multiple_of((index % 8) * 144 + first, 16), count)
             lanes = pl.ds(pl.multiple_of(mine_far + (index // 8) * FEAT, HEAD), FEAT)
-            return [weights.at[rows, :], dw.at[down_rows, lanes]]
+            return [dw.at[rows, lanes]]
 
         return slices
+
+    def ffn_rings():
+        down = ring_dp(net, at, (down_of(0, 80), down_of(80, 64)))
+        both = ring_dp(net, at, (rows_of(gw), rows_of(uw)))
+        for _ in range(3):
+            next(down)
+            yield
+        next(both)
+        yield
+        yield from down
+        yield
+        yield from both
 
     net.take(across[0], qkv_slices(at.z, at.y)[0])
     net.take(across[1], out_slices(at.z, at.y)[0])
@@ -668,10 +688,10 @@
     drain(ring)
     far_qw = net.send(qw.at[far_half, cols_half], qw.at[far_half, cols_half], at.S)
     far_ow = net.send(ow.at[rows_half, far_half], ow.at[rows_half, far_half], at.S)
-    net.take(across[2], ffn_slices(gw, 0, 80)(at.z, at.y)[0])
-    net.take(across[3], ffn_slices(uw, 80, 64)(at.z, at.y)[0])
-    net.take(across[4], ffn_slices(uw, 0, 144)(at.z, at.y)[1])
-    ring = ring_dp(net, at, (ffn_slices(gw, 0, 80), ffn_slices(uw, 80, 64)))
+    net.take(across[2], rows_of(gw)(at.z, at.y)[0])
+    net.take(across[3], rows_of(uw)(at.z, at.y)[0])
+    net.take(across[4], down_of(0, 144)(at.z, at.y)[0])
+    ring = ffn_rings()
     next(ring)
     near = [
         net.send(wg_ref.at[:, pl.ds(quarter_start(at.sib), PART)], gw.at[pl.ds(mine, FEAT), :], at.S),
@@ -710,7 +730,7 @@
 
     def kv_block(i, carry):
         rows = pl.ds(aligned(i, 256), 256)
-        both = dot(n1[rows, :], qw[:, QCOLS:]) + bias_ref[:, QCOLS:]
+        both = dot(n1[rows, :], qw[:, QCOLS:]) + bias_ref[:, QCOLS:QKV]
         key = both[:, :HEAD]
         k_ref[rows, :] = (key * cos_ref[rows, :] + turn(key) * sin_ref[rows, :]).astype(BF)
         v_ref[rows, :] = both[:, HEAD:].astype(BF)
@@ -747,7 +767,9 @@
             attn_ref[rows, lanes] = dot(probs, v_ref[:keys, :]).astype(BF)
             return carry
 
-        lax.fori_loop(0, HEADS, attend, 0)
+        lax.fori_loop(0, HEADS // 2, attend, 0)
+        next(ring)
+        lax.fori_loop(HEADS // 2, HEADS, attend, 0)
         next(ring)
 
     net.take(near_ow, ow.at[:, pl.ds(aligned(at.sib, FEAT), FEAT)])
@@ -756,6 +778,7 @@
     move(ow, ow_out)
     part_out[...] = dot(attn_ref[pl.ds(aligned(1 - at.row, BLOCK), BLOCK), :], ow[...]).astype(BF)
     part = net.send(part_out, part_in, at.N1)
+    next(ring)
     own = dot(attn_ref[pl.ds(aligned(at.row, BLOCK), BLOCK), :], ow[...])
     net.take(part, part_in)
     mid = xs_ref[...].astype(F32) + own + part_in[...].astype(F32)
@@ -773,11 +796,7 @@
     gather_og.end()
     move(og_all.at[my_rows, :], og_out)
     next(ring)
-    gather_n2.middle()
-    next(ring)
-    next(ring)
-    gather_n2.late()
-    drain(ring)
+    next(ring)
     net.take(near[2], dw.at[:, pl.ds(aligned(at.sib, FEAT), FEAT)])
 
     def hidden_back(i, carry):
@@ -787,12 +806,20 @@
             d_up[rows, lanes] = dot(og_all[rows, :], dw[lanes, :], 1, 1).astype(BF)
         return carry
 
+    lax.fori_loop(0, 1, hidden_back, 0)
+    next(ring)
+    lax.fori_loop(1, 2, hidden_back, 0)
+    next(ring)
+    gather_n2.middle()
+    next(ring)
+    lax.fori_loop(2, 3, hidden_back, 0)
+    next(ring)
+    lax.fori_loop(3, 4, hidden_back, 0)
+    move(dw, dw_out)
+    drain(ring)
     gather_attn = GatherCol(net, at, attn_all)
     for j in (0, 1):
         gather_attn.rows(at.col, j)[...] = attn_ref[pl.ds(j * BLOCK, BLOCK), :]
-    gather_attn.start()
-    lax.fori_loop(0, 4, hidden_back, 0)
-    move(dw, dw_out)
     net.take(near[0], gw.at[pl.ds(aligned(at.sib, FEAT), FEAT), :])
     net.take(near[1], uw.at[pl.ds(aligned(at.sib, FEAT), FEAT), :])
 
@@ -809,6 +836,9 @@
 
     for j in (3, 1, 2, 0):
         gather_n2.end(j)
+        if j == 3:
+            gather_n2.late()
+            gather_attn.start()
         rows, _ = tokens(j)
         for first, width in tiles_of(PART, 512):
             lanes = pl.ds(first, width)
@@ -894,7 +924,7 @@
                 copy.wait_send()
 
 
-def run_forward(x, og, wq, wk, wv, wout, wg, wu, wd, gains, bias, cosine, sine):
+def run_forward(x, og, wq, wk, wv, wout, wg, wu, wd, vectors, cosine, sine):
     outs = (
         ((BLOCK, MODEL), BF, vmem),
         ((SEQ, FEAT), BF, vmem),
@@ -917,7 +947,7 @@
     return pl.pallas_call(
         forward_kernel,
         out_shape=[jax.ShapeDtypeStruct(dims, dtype) for dims, dtype, _ in outs],
-        in_specs=[anywhere()] * 9 + [vmem()] * 4,
+        in_specs=[anywhere()] * 9 + [vmem()] * 3,
         out_specs=[place() for _, _, place in outs],
         scratch_shapes=[
             pltpu.VMEM((FEAT, QKV), BF),
@@ -936,6 +966,7 @@
             pltpu.VMEM((2, MODEL, 256), BF),
             pltpu.VMEM((2, 2, 288, MODEL), BF),
             pltpu.VMEM((2 * BLOCK, QCOLS), BF),
+            pltpu.VMEM((8, FEAT), F32),
         ]
         + reduce8_scratch(BLOCK, MODEL)
         + ring_scratch(DOWN_FIRST, DOWN_LAST)
@@ -952,7 +983,7 @@
             flops=37 * 10**9, bytes_accessed=80 * 10**6, transcendentals=4 * 10**6
         ),
         name="forward_and_feed_forward",
-    )(x, og, wq, wk, wv, wout, wg, wu, wd, gains, bias, cosine, sine)
+    )(x, og, wq, wk, wv, wout, wg, wu, wd, vectors, cosine, sine)
 
 
 def backward_kernel(
@@ -1218,7 +1249,7 @@
     all_out,
     small_out,
     out_ref,
-    grad_in,
+    gi_in,
     small_y,
     small_z,
     hidden,
@@ -1228,7 +1259,6 @@
     part_out,
     part_in,
     gi_out,
-    gi_in,
     gain_sums,
     sums_in,
     *rest,
@@ -1401,7 +1431,6 @@
     small_out[...] = (small_z[0] + small_z[1]) + (small_z[2] + small_z[3])
     for key, (_, col) in zip(gi_keys, peers, strict=True):
         net.take(key, half_block(col))
-    grad_in[...] = gi_in[...].astype(F32)
     for _ in ring:
         next(after, None)
     drain(after)
@@ -1419,7 +1448,7 @@
         shape((QCOLS, FEAT), BF),
         shape((8, FEAT + QKV), F32),
         shape((SEQ // 2, FEAT), F32),
-        shape((SEQ // 2, FEAT), F32),
+        shape((SEQ // 2, FEAT), BF),
     )
     return pl.pallas_call(
         sums_kernel,
@@ -1435,7 +1464,6 @@
             pltpu.VMEM((BLOCK, MODEL), BF),
             pltpu.VMEM((BLOCK, MODEL), BF),
             pltpu.VMEM((BLOCK, MODEL), BF),
-            pltpu.VMEM((SEQ // 2, FEAT), BF),
             pltpu.VMEM((8, MODEL), F32),
             pltpu.VMEM((8, 8, FEAT), F32),
         ]
@@ -1459,9 +1487,13 @@
     qkv,
     out,
     small,
+    gi,
+    lo,
     gate_out,
     up_out,
     down_out,
+    lo_out,
+    gi_out,
     query_out,
     key_out,
     value_out,
@@ -1478,15 +1510,15 @@
     down_buf,
     in_sems,
     out_sems,
+    lo_sem,
 ):
     skip = 3 * PART
 
     def loads(n):
-        place = n % 2
         rows = pl.ds(640 * (n % 2), 640)
         return [
-            pltpu.make_async_copy(gu.at[:, pl.ds(n * 48, 48), :], gu_in.at[place], in_sems.at[place, 0]),
-            pltpu.make_async_copy(down.at[n // 2, rows, :], down_in.at[place], in_sems.at[place, 1]),
+            pltpu.make_async_copy(gu.at[:, pl.ds(n * 48, 48), :], gu_in.at[n], in_sems.at[n, 0]),
+            pltpu.make_async_copy(down.at[n // 2, rows, :], down_in.at[n], in_sems.at[n, 1]),
         ]
 
     def stores(n):
@@ -1513,7 +1545,10 @@
         for copy in copies:
             copy.wait()
 
-    arriving = {0: run(loads(0)), 1: run(loads(1))}
+    arriving = [run(loads(n)) for n in range(8)]
+    passed = pltpu.make_async_copy(lo, lo_out, lo_sem.at[0])
+    passed.start()
+    gi_out[...] = gi[...].astype(F32)
     query_out[...] = qkv[:, :QCOLS].astype(F32)
     key_out[...] = qkv[:, QCOLS : QCOLS + HEAD].astype(F32)
     value_out[...] = qkv[:, QCOLS + HEAD :].astype(F32)
@@ -1535,46 +1570,46 @@
         if n > 1:
             wait(leaving[n - 2])
         for i, buf in enumerate((gate_buf, up_buf)):
-            buf[place, :, :skip] = gu_in[place, i, :, :skip].astype(F32)
-            buf[place, :, skip:] = gu_in[place, i, :, skip + HEAD :].astype(F32)
+            buf[place, :, :skip] = gu_in[n, i, :, :skip].astype(F32)
+            buf[place, :, skip:] = gu_in[n, i, :, skip + HEAD :].astype(F32)
         for m in range(4):
             down_buf[place, pl.ds(144 * m, 80), :] = down_in[
-                place, pl.ds(160 * m, 80), :
+                n, pl.ds(160 * m, 80), :
             ].astype(F32)
             down_buf[place, pl.ds(144 * m + 80, 64), :] = down_in[
-                place, pl.ds(160 * m + 96, 64), :
+                n, pl.ds(160 * m + 96, 64), :
             ].astype(F32)
         leaving[n] = run(stores(n))
-        if n + 2 < 8:
-            arriving[n + 2] = run(loads(n + 2))
     wait(leaving[6])
     wait(leaving[7])
-
-
-def run_widen(gu, down, qkv, out, small):
-    shapes = [(FEAT, UNITS)] * 2 + [(UNITS, FEAT)]
+    passed.wait()
+
+
+def run_widen(gu, down, qkv, out, small, grad_input, layer_output):
+    shapes = [(FEAT, UNITS)] * 2 + [(UNITS, FEAT)] + [(SEQ // 2, FEAT)] * 2
     shapes += [(FEAT, QCOLS), (FEAT, HEAD), (FEAT, HEAD), (QCOLS, FEAT)]
     shapes += [(FEAT,), (FEAT,), (QCOLS,), (HEAD,), (HEAD,)]
     return pl.pallas_call(
         widen_kernel,
         out_shape=[jax.ShapeDtypeStruct(dims, F32) for dims in shapes],
-        in_specs=[anywhere()] * 2 + [vmem()] * 3,
-        out_specs=[anywhere()] * 3 + [vmem()] * 9,
+        in_specs=[anywhere()] * 2 + [vmem()] * 4 + [anywhere()],
+        out_specs=[anywhere()] * 4 + [vmem()] * 10,
         scratch_shapes=[
-            pltpu.VMEM((2, 2, 48, 4 * PART), BF),
-            pltpu.VMEM((2, 640, FEAT), BF),
+            pltpu.VMEM((8, 2, 48, 4 * PART), BF),
+            pltpu.VMEM((8, 640, FEAT), BF),
             pltpu.VMEM((2, 48, UNITS), F32),
             pltpu.VMEM((2, 48, UNITS), F32),
             pltpu.VMEM((2, 576, FEAT), F32),
-            pltpu.SemaphoreType.DMA((2, 2)),
+            pltpu.SemaphoreType.DMA((8, 2)),
             pltpu.SemaphoreType.DMA((2, 3)),
+            pltpu.SemaphoreType.DMA((1,)),
         ],
         compiler_params=pltpu.CompilerParams(vmem_limit_bytes=VMEM_LIMIT),
         cost_estimate=pl.CostEstimate(
             flops=10**7, bytes_accessed=36 * 10**6, transcendentals=0
         ),
         name="widen",
-    )(gu, down, qkv, out, small)
+    )(gu, down, qkv, out, small, grad_input, layer_output)
 
 
 def rope_tables(count):
@@ -1603,8 +1638,7 @@
     out_grad,
 ):
     cosine, sine = rope_tables(SEQ)
-    bias = jnp.concatenate([b_query, b_key, b_value]).astype(F32)[None]
-    gains = jnp.zeros((8, FEAT), F32).at[0].set(gain_attn.astype(F32)).at[1].set(gain_ffn.astype(F32))
+    vectors = jnp.concatenate([b_query, b_key, b_value, gain_attn, gain_ffn]).astype(F32)[None]
     (
         xs,
         normed1_cols,
@@ -1633,8 +1667,7 @@
         w_gate,
         w_up,
         w_down,
-        gains,
-        bias,
+        vectors,
         cosine,
         sine,
     )
@@ -1674,12 +1707,16 @@
         grad_gate,
         grad_up,
         grad_down,
+        layer_output,
+        grad_input,
         grad_query,
         grad_key,
         grad_value,
         grad_out,
         *vectors,
-    ) = run_widen(grad_gu, grad_down, grad_qkv, grad_out, small)
+    ) = run_widen(
+        grad_gu, grad_down, grad_qkv, grad_out, small, grad_input, layer_output
+    )
     gain1, gain2, bias_query, bias_key, bias_value = vectors
     return (
         layer_output,

time: 330 us -> 335 us (1.015)
  Pallas kernels: 318 us -> 326 us
    pallas_call x1, Pallas kernels: 15.1 us -> 28.4 us  [run_widen(): pl.pallas_call(widen_kernel, out_shape=[jax.ShapeDtypeStruct(dims, F32) f...]
    pallas_call x1, Pallas kernels: 158 us -> 152 us  [run_forward(): pl.pallas_call(forward_kernel, out_shape=[jax.ShapeDtypeStruct(dims, dtyp...]
where the time goes in v9:
time: 335 us; the launch traced here: 331 us
  Pallas kernels  326 us (97%)
  local copies, waits for them, and re-layouts  3.39 us (1%)
    pallas_call x1, Pallas kernels, run_forward(): pl.pallas_call(forward_kernel, out_shape=[jax.ShapeDtypeStruct(dims, dtyp...  152 us
    pallas_call x1, Pallas kernels, run_backward(): pl.pallas_call(backward_kernel, out_shape=outs, in_specs=[vmem()] * (len(...  72.8 us
    pallas_call x1, Pallas kernels, run_sums(): pl.pallas_call(sums_kernel, out_shape=outs, in_specs=[vmem()] * len(args)...  72.6 us
    pallas_call x1, Pallas kernels, run_widen(): pl.pallas_call(widen_kernel, out_shape=[jax.ShapeDtypeStruct(dims, F32) f...  28.4 us

profile of v9, /device:TPU:0, one launch (start us, length us, event | category | flops | bytes accessed | tf_op | source)
XLA Modules:
  0.0 330.9 jit_solution(15493989680509776999)
XLA Ops:
  0.6 0.7 constant_dynamic-update-slice_fusion.4
  1.3 0.7 constant_dynamic-update-slice_fusion.3
  2.0 0.7 constant_dynamic-update-slice_fusion.2
  2.7 0.7 constant_dynamic-update-slice_fusion.1
  3.3 0.7 constant_dynamic-update-slice_fusion
  4.0 0.6 convert_element_type.10.bias_ref
  4.6 152.2 %forward_and_feed_forward.1 = (bf16[128,1536]{1,0:T(8,128)(2,1)}, bf16[1024,384]{1,0:T(8,128)(2,1)}, bf16[128,1536]{1,0:T(8,128)(2,1)}, bf16[1536,1024]{1,0:T(8,...) custom-call(bf16[512,384]{1,0:T(8,128)(2,1)} %x_ref.1, ...), custom_call_target="tpu_custom_call" | custom-call | flops 36999999488 | bytes 80000000 | tf_op jit(solution)/shard_map/forward_and_feed_forward/pallas_call | solution.py:947
  156.8 72.8 %attention_backward.1 = (bf16[768,384]{1,0:T(8,128)(2,1)}, bf16[384,1024]{1,0:T(8,128)(2,1)}, f32[8,1536]{1,0:T(8,128)}, f32[128,1536]{1,0:T(8,128)}, bf16[2,128...) custom-call(f32[128,1536]{1,0:T(8,128)} %get-tuple-element.59.dn2_ref, ...), custom_call_target="tpu_custom_call" | custom-call | flops 10000000000 | bytes 40000000 | tf_op jit(solution)/shard_map/attention_backward/pallas_call | solution.py:1203
  229.7 72.6 %sums_over_sequences.1 = (bf16[2,384,4608]{2,1,0:T(8,128)(2,1)}, bf16[384,1024]{1,0:T(8,128)(2,1)}, bf16[768,384]{1,0:T(8,128)(2,1)}, f32[8,1408]{1,0:T(8,128)},...) custom-call(bf16[4,48,1152]{2,1,0:T(8,128)(2,1)} %get-tuple-element.72.gu_own, bf16[2,4,48,1024]{3,2,1,0:T(8,128)(2,1)} %bitcast.8, ...), custom_call_target="tpu_custom_call" | custom-call | flops 4000000000 | bytes 60000000 | tf_op jit(solution)/shard_map/sums_over_sequences/pallas_call | solution.py:1453
  302.2 28.4 %widen.1 = (f32[384,4480]{1,0:T(8,128)}, f32[384,4480]{1,0:T(8,128)}, f32[4480,384]{1,0:T(8,128)}, f32[512,384]{1,0:T(8,128)}, f32[512,384]{1,0:T(8,128)}, /*ind...) custom-call(bf16[2,384,4608]{2,1,0:T(8,128)(2,1)} %get-tuple-element, ...), custom_call_target="tpu_custom_call" | custom-call | flops 10000000 | bytes 36000000 | tf_op jit(solution)/shard_map/widen/pallas_call | solution.py:1592

commit v10 on v9

--- a/solution.py
+++ b/solution.py
@@ -1510,7 +1510,6 @@
     down_buf,
     in_sems,
     out_sems,
-    lo_sem,
 ):
     skip = 3 * PART
 
@@ -1546,8 +1545,7 @@
             copy.wait()
 
     arriving = [run(loads(n)) for n in range(8)]
-    passed = pltpu.make_async_copy(lo, lo_out, lo_sem.at[0])
-    passed.start()
+    lo_out[...] = lo[...]
     gi_out[...] = gi[...].astype(F32)
     query_out[...] = qkv[:, :QCOLS].astype(F32)
     key_out[...] = qkv[:, QCOLS : QCOLS + HEAD].astype(F32)
@@ -1582,7 +1580,6 @@
         leaving[n] = run(stores(n))
     wait(leaving[6])
     wait(leaving[7])
-    passed.wait()
 
 
 def run_widen(gu, down, qkv, out, small, grad_input, layer_output):
@@ -1592,8 +1589,8 @@
     return pl.pallas_call(
         widen_kernel,
         out_shape=[jax.ShapeDtypeStruct(dims, F32) for dims in shapes],
-        in_specs=[anywhere()] * 2 + [vmem()] * 4 + [anywhere()],
-        out_specs=[anywhere()] * 4 + [vmem()] * 10,
+        in_specs=[anywhere()] * 2 + [vmem()] * 5,
+        out_specs=[anywhere()] * 3 + [vmem()] * 11,
         scratch_shapes=[
             pltpu.VMEM((8, 2, 48, 4 * PART), BF),
             pltpu.VMEM((8, 640, FEAT), BF),
@@ -1602,7 +1599,6 @@
             pltpu.VMEM((2, 576, FEAT), F32),
             pltpu.SemaphoreType.DMA((8, 2)),
             pltpu.SemaphoreType.DMA((2, 3)),
-            pltpu.SemaphoreType.DMA((1,)),
         ],
         compiler_params=pltpu.CompilerParams(vmem_limit_bytes=VMEM_LIMIT),
         cost_estimate=pl.CostEstimate(

time: 335 us -> 320 us (0.955)
  Pallas kernels: 326 us -> 312 us
    pallas_call x1, Pallas kernels: 28.4 us -> 14 us  [run_widen(): pl.pallas_call(widen_kernel, out_shape=[jax.ShapeDtypeStruct(dims, F32) f...]
where the time goes in v10:
time: 320 us; the launch traced here: 316 us
  Pallas kernels  312 us (98%)
  local copies, waits for them, and re-layouts  3.39 us (1%)
    pallas_call x1, Pallas kernels, run_forward(): pl.pallas_call(forward_kernel, out_shape=[jax.ShapeDtypeStruct(dims, dtyp...  152 us
    pallas_call x1, Pallas kernels, run_backward(): pl.pallas_call(backward_kernel, out_shape=outs, in_specs=[vmem()] * (len(...  72.8 us
    pallas_call x1, Pallas kernels, run_sums(): pl.pallas_call(sums_kernel, out_shape=outs, in_specs=[vmem()] * len(args)...  72.6 us
    pallas_call x1, Pallas kernels, run_widen(): pl.pallas_call(widen_kernel, out_shape=[jax.ShapeDtypeStruct(dims, F32) f...  14 us

profile of v10, /device:TPU:0, one launch (start us, length us, event | category | flops | bytes accessed | tf_op | source)
XLA Modules:
  0.0 316.5 jit_solution(10930070001775396137)
XLA Ops:
  0.6 0.7 constant_dynamic-update-slice_fusion.4
  1.3 0.7 constant_dynamic-update-slice_fusion.3
  2.0 0.7 constant_dynamic-update-slice_fusion.2
  2.7 0.7 constant_dynamic-update-slice_fusion.1
  3.3 0.7 constant_dynamic-update-slice_fusion
  4.0 0.6 convert_element_type.10.bias_ref
  4.6 152.2 %forward_and_feed_forward.1 = (bf16[128,1536]{1,0:T(8,128)(2,1)}, bf16[1024,384]{1,0:T(8,128)(2,1)}, bf16[128,1536]{1,0:T(8,128)(2,1)}, bf16[1536,1024]{1,0:T(8,...) custom-call(bf16[512,384]{1,0:T(8,128)(2,1)} %x_ref.1, ...), custom_call_target="tpu_custom_call" | custom-call | flops 36999999488 | bytes 80000000 | tf_op jit(solution)/shard_map/forward_and_feed_forward/pallas_call | solution.py:947
  156.8 72.8 %attention_backward.1 = (bf16[768,384]{1,0:T(8,128)(2,1)}, bf16[384,1024]{1,0:T(8,128)(2,1)}, f32[8,1536]{1,0:T(8,128)}, f32[128,1536]{1,0:T(8,128)}, bf16[2,128...) custom-call(f32[128,1536]{1,0:T(8,128)} %get-tuple-element.59.dn2_ref, ...), custom_call_target="tpu_custom_call" | custom-call | flops 10000000000 | bytes 40000000 | tf_op jit(solution)/shard_map/attention_backward/pallas_call | solution.py:1203
  229.7 72.6 %sums_over_sequences.1 = (bf16[2,384,4608]{2,1,0:T(8,128)(2,1)}, bf16[384,1024]{1,0:T(8,128)(2,1)}, bf16[768,384]{1,0:T(8,128)(2,1)}, f32[8,1408]{1,0:T(8,128)},...) custom-call(bf16[4,48,1152]{2,1,0:T(8,128)(2,1)} %get-tuple-element.72.gu_own, bf16[2,4,48,1024]{3,2,1,0:T(8,128)(2,1)} %bitcast.8, ...), custom_call_target="tpu_custom_call" | custom-call | flops 4000000000 | bytes 60000000 | tf_op jit(solution)/shard_map/sums_over_sequences/pallas_call | solution.py:1453
  302.2 14.0 %widen.1 = (f32[384,4480]{1,0:T(8,128)}, f32[384,4480]{1,0:T(8,128)}, f32[4480,384]{1,0:T(8,128)}, f32[512,384]{1,0:T(8,128)}, f32[512,384]{1,0:T(8,128)}, /*ind...) custom-call(bf16[2,384,4608]{2,1,0:T(8,128)(2,1)} %get-tuple-element, ...), custom_call_target="tpu_custom_call" | custom-call | flops 10000000 | bytes 36000000 | tf_op jit(solution)/shard_map/widen/pallas_call | solution.py:1589

commit v11 on v10

--- a/solution.py
+++ b/solution.py
@@ -494,9 +494,13 @@
     wg_ref,
     wu_ref,
     wd_ref,
-    bias_ref,
     cos_ref,
     sin_ref,
+    bq_ref,
+    bk_ref,
+    bv_ref,
+    g1_ref,
+    g2_ref,
     xs_ref,
     n1c_ref,
     og_out,
@@ -531,6 +535,7 @@
     down,
     attn_ref,
     gains_ref,
+    bias_ref,
     *rest,
 ):
     red_a, bufs, sems = rest[:7], rest[7:-4], rest[-4:]
@@ -546,8 +551,11 @@
         return copy
 
     gains_ref[...] = jnp.zeros_like(gains_ref)
-    for i in (0, 1):
-        gains_ref[i : i + 1, :] = bias_ref[:, QKV + i * FEAT : QKV + (i + 1) * FEAT]
+    gains_ref[0:1, :] = g1_ref[...].astype(F32)[None]
+    gains_ref[1:2, :] = g2_ref[...].astype(F32)[None]
+    bias_ref[:, :QCOLS] = bq_ref[...].astype(F32)[None]
+    bias_ref[:, QCOLS : QCOLS + HEAD] = bk_ref[...].astype(F32)[None]
+    bias_ref[:, QCOLS + HEAD :] = bv_ref[...].astype(F32)[None]
     joined = [
         move(wq_ref, wqkv_ref.at[:, pl.ds(0, QCOLS)]),
         move(wk_ref, wqkv_ref.at[:, pl.ds(QCOLS, HEAD)]),
@@ -924,7 +932,7 @@
                 copy.wait_send()
 
 
-def run_forward(x, og, wq, wk, wv, wout, wg, wu, wd, vectors, cosine, sine):
+def run_forward(x, og, wq, wk, wv, wout, wg, wu, wd, *small):
     outs = (
         ((BLOCK, MODEL), BF, vmem),
         ((SEQ, FEAT), BF, vmem),
@@ -947,7 +955,7 @@
     return pl.pallas_call(
         forward_kernel,
         out_shape=[jax.ShapeDtypeStruct(dims, dtype) for dims, dtype, _ in outs],
-        in_specs=[anywhere()] * 9 + [vmem()] * 3,
+        in_specs=[anywhere()] * 9 + [vmem()] * 7,
         out_specs=[place() for _, _, place in outs],
         scratch_shapes=[
             pltpu.VMEM((FEAT, QKV), BF),
@@ -967,6 +975,7 @@
             pltpu.VMEM((2, 2, 288, MODEL), BF),
             pltpu.VMEM((2 * BLOCK, QCOLS), BF),
             pltpu.VMEM((8, FEAT), F32),
+            pltpu.VMEM((1, QKV), F32),
         ]
         + reduce8_scratch(BLOCK, MODEL)
         + ring_scratch(DOWN_FIRST, DOWN_LAST)
@@ -983,7 +992,7 @@
             flops=37 * 10**9, bytes_accessed=80 * 10**6, transcendentals=4 * 10**6
         ),
         name="forward_and_feed_forward",
-    )(x, og, wq, wk, wv, wout, wg, wu, wd, vectors, cosine, sine)
+    )(x, og, wq, wk, wv, wout, wg, wu, wd, *small)
 
 
 def backward_kernel(
@@ -1634,7 +1643,6 @@
     out_grad,
 ):
     cosine, sine = rope_tables(SEQ)
-    vectors = jnp.concatenate([b_query, b_key, b_value, gain_attn, gain_ffn]).astype(F32)[None]
     (
         xs,
         normed1_cols,
@@ -1663,9 +1671,13 @@
         w_gate,
         w_up,
         w_down,
-        vectors,
         cosine,
         sine,
+        b_query,
+        b_key,
+        b_value,
+        gain_attn,
+        gain_ffn,
     )
     grad_out, grad_qkv, sums, d_mid, d_qkv, bias_sums, grad_gu, grad_down = run_backward(
         dn2,

time: 320 us -> 316 us (0.988)
  local copies, waits for them, and re-layouts: 3.39 us -> 0 us
where the time goes in v11:
time: 316 us; the launch traced here: 313 us
  Pallas kernels  312 us (99%)
    pallas_call x1, Pallas kernels, run_forward(): pl.pallas_call(forward_kernel, out_shape=[jax.ShapeDtypeStruct(dims, dtyp...  152 us
    pallas_call x1, Pallas kernels, run_backward(): pl.pallas_call(backward_kernel, out_shape=outs, in_specs=[vmem()] * (len(...  72.9 us
    pallas_call x1, Pallas kernels, run_sums(): pl.pallas_call(sums_kernel, out_shape=outs, in_specs=[vmem()] * len(args)...  72.5 us
    pallas_call x1, Pallas kernels, run_widen(): pl.pallas_call(widen_kernel, out_shape=[jax.ShapeDtypeStruct(dims, F32) f...  14 us

profile of v11, /device:TPU:0, one launch (start us, length us, event | category | flops | bytes accessed | tf_op | source)
XLA Modules:
  0.0 312.7 jit_solution(3150101196519593529)
XLA Ops:
  0.7 152.4 %forward_and_feed_forward.1 = (bf16[128,1536]{1,0:T(8,128)(2,1)}, bf16[1024,384]{1,0:T(8,128)(2,1)}, bf16[128,1536]{1,0:T(8,128)(2,1)}, bf16[1536,1024]{1,0:T(8,...) custom-call(bf16[512,384]{1,0:T(8,128)(2,1)} %x_ref.1, ...), custom_call_target="tpu_custom_call" | custom-call | flops 36999999488 | bytes 80000000 | tf_op jit(solution)/shard_map/forward_and_feed_forward/pallas_call | solution.py:955
  153.0 72.9 %attention_backward.1 = (bf16[768,384]{1,0:T(8,128)(2,1)}, bf16[384,1024]{1,0:T(8,128)(2,1)}, f32[8,1536]{1,0:T(8,128)}, f32[128,1536]{1,0:T(8,128)}, bf16[2,128...) custom-call(f32[128,1536]{1,0:T(8,128)} %get-tuple-element.59.dn2_ref, ...), custom_call_target="tpu_custom_call" | custom-call | flops 10000000000 | bytes 40000000 | tf_op jit(solution)/shard_map/attention_backward/pallas_call | solution.py:1212
  225.9 72.5 %sums_over_sequences.1 = (bf16[2,384,4608]{2,1,0:T(8,128)(2,1)}, bf16[384,1024]{1,0:T(8,128)(2,1)}, bf16[768,384]{1,0:T(8,128)(2,1)}, f32[8,1408]{1,0:T(8,128)},...) custom-call(bf16[4,48,1152]{2,1,0:T(8,128)(2,1)} %get-tuple-element.72.gu_own, bf16[2,4,48,1024]{3,2,1,0:T(8,128)(2,1)} %bitcast.4, ...), custom_call_target="tpu_custom_call" | custom-call | flops 4000000000 | bytes 60000000 | tf_op jit(solution)/shard_map/sums_over_sequences/pallas_call | solution.py:1462
  298.4 14.0 %widen.1 = (f32[384,4480]{1,0:T(8,128)}, f32[384,4480]{1,0:T(8,128)}, f32[4480,384]{1,0:T(8,128)}, f32[512,384]{1,0:T(8,128)}, f32[512,384]{1,0:T(8,128)}, /*ind...) custom-call(bf16[2,384,4608]{2,1,0:T(8,128)(2,1)} %get-tuple-element, ...), custom_call_target="tpu_custom_call" | custom-call | flops 10000000 | bytes 36000000 | tf_op jit(solution)/shard_map/widen/pallas_call | solution.py:1598
